TPU v7x, 512 devices: a whole 4x8x8 slice. The times are simulated.
512 devices in a mesh: dp: 16 (over z_hi, x), mp: 32 (over z_lo, y, core).
Axes of the slice: x: 4, y: 8, z: 8 (z_hi: 4, z_lo: 2; z = z_hi * 2 + z_lo), core: 2. Of those that a mesh axis runs over, the one named last changes fastest.
Arguments:
- partials: bfloat16 [16, 2048, 16384], P('dp', 'mp'), may hold values from -0.375 to 0.375
- owner: int32 [32], replicated, may hold values from 0 to 31, each once
- left_prev: float32 [32, 1024, 1024], P('mp', 'dp'), may hold values from -6 to 6
- right_prev: float32 [32, 1024, 1024], P('mp', 'dp'), may hold values from -6 to 6
- left_root: bfloat16 [32, 1024, 1024], P('mp', 'dp'), may hold values from -0.2 to 2.2
- right_root: bfloat16 [32, 1024, 1024], P('mp', 'dp'), may hold values from -0.2 to 2.2
Outputs:
- left_new: float32 [32, 1024, 1024], P('mp', 'dp')
- right_new: float32 [32, 1024, 1024], P('mp', 'dp')
- update: bfloat16 [32, 1024, 1024], P('mp', 'dp')
Inputs may be any that keep to these rules, and one draw needn't show every extreme that they name: `owner`: each mp index owns exactly one block.
All inputs are finite; a program needn't handle non-finite values.
Results may differ from a plain program's by a relative error of at most 0.025.
Values may be sent and summed in bfloat16 or wider, within the bound.
No kernel may reach another device: no remote copies, remote signals or barrier semaphores. Data moves between devices by JAX's collectives and lax.ppermute only.
A program may use at most 64 MiB of HBM per device.

v0:
```python
import jax
import jax.numpy as jnp
from jax import lax
from jax.sharding import PartitionSpec as P

decay_rate = 0.95


def on_device(partials, owner, left_prev, right_prev, left_root, right_root):
    partial_rows = partials[0]
    row_count, col_count = partial_rows.shape
    block_order = left_prev.shape[2]
    share_rows = left_prev.shape[1]
    mp_count = lax.axis_size("mp")
    block_count = owner.shape[0]
    col_blocks = col_count // block_order
    owner_index = lax.axis_index("mp")
    replica = lax.axis_index("dp")
    blocks = jnp.arange(block_count, dtype=jnp.int32)
    holder = jnp.sum(jnp.where(owner[None, :] == blocks[:, None], blocks[None, :], 0), axis=1)
    per_row = mp_count // 2
    my_row = owner_index // per_row
    targets = my_row * col_blocks + jnp.arange(col_blocks, dtype=jnp.int32)
    wanted = (holder[:, None] == targets[None, :]).astype(jnp.bfloat16)
    own_row = holder[owner_index] // col_blocks
    summed = lax.psum(partial_rows.astype(jnp.float32).astype(jnp.bfloat16), "dp")
    grad_grid = summed.reshape(row_count, col_blocks, block_order)
    arrived = lax.all_to_all(
        jnp.einsum("pb,rbw->prw", wanted, grad_grid, preferred_element_type=jnp.float32).astype(
            jnp.bfloat16
        ),
        "mp",
        split_axis=0,
        concat_axis=0,
        tiled=True,
    )
    chosen = lax.dynamic_slice_in_dim(arrived, own_row * per_row, per_row, 0)
    owned_block = chosen.reshape(per_row * row_count, arrived.shape[2])
    first_row = replica * share_rows
    rows_part = lax.dynamic_slice_in_dim(owned_block, first_row, share_rows, 0)
    cols_part = lax.dynamic_slice_in_dim(owned_block, first_row, share_rows, 1)
    left_gram = lax.dot_general(
        rows_part, owned_block, (((1,), (1,)), ((), ())), preferred_element_type=jnp.float32
    )
    right_gram = lax.dot_general(
        cols_part, owned_block, (((0,), (0,)), ((), ())), preferred_element_type=jnp.float32
    )
    left_out = decay_rate * left_prev[0] + (1.0 - decay_rate) * left_gram
    right_out = decay_rate * right_prev[0] + (1.0 - decay_rate) * right_gram
    left_half = jnp.dot(left_root[0], owned_block, preferred_element_type=jnp.float32).astype(
        jnp.bfloat16
    )
    precond = jnp.dot(
        left_half,
        lax.all_gather(right_root[0], "dp", axis=0, tiled=True),
        preferred_element_type=jnp.float32,
    )
    return (left_out[None], right_out[None], precond.astype(jnp.bfloat16)[None])


def solution(mesh):
    return jax.shard_map(
        on_device,
        mesh=mesh,
        in_specs=(
            P("dp", "mp", None),
            P(),
            P("mp", "dp", None),
            P("mp", "dp", None),
            P("mp", "dp", None),
            P("mp", "dp", None),
        ),
        out_specs=(P("mp", "dp", None), P("mp", "dp", None), P("mp", "dp", None)),
        check_vma=False,
    )
```

profile of v0, /device:TPU:24, one launch (start us, length us, event | category | flops | bytes accessed | tf_op | source)
XLA Modules:
  0.0 327.0 jit_solution(14970820900362598397)
XLA Ops:
  7.2 0.0 copy-start
  7.2 0.0 all-reduce.2.cloned.1.call-start
  7.2 4.1 %copy.12 = bf16[8,8,16,1024]{3,2,1,0:T(8,128)(2,1)} copy(bf16[8,8,16,1024]{3,1,2,0:T(8,128)(2,1)} %bitcast.37) | data formatting | bytes 4194304
  11.4 0.0 copy-start.3
  11.4 0.0 all-reduce.2.cloned.1.call-update
  11.4 0.6 copy-done.3
  12.0 0.1 select_reduce_fusion
  12.1 189.1 %all-reduce.2.cloned.1.call-done = bf16[64,16,1024]{2,1,0:T(8,128)(2,1)} async-done(((bf16[64,16,1024]{2,1,0:T(8,128)(2,1)}), bf16[64,16,1024]{2,1,0:T(8,128)(2,1)}) %all-reduce.2.cloned.1.call-update) | async-done | bytes 2097168 | tf_op jit(solution)/shard_map/psum | solution.py:26
  201.2 2.9 convolution_convert_fusion
  204.2 4.3 %copy.11 = bf16[32,64,1024]{2,1,0:T(8,128)(2,1)} copy(bf16[32,64,1024]{2,0,1:T(8,128)(2,1)S(1)} %convolution_convert_fusion) | data formatting | bytes 8388608 | tf_op jit(solution)/shard_map/convert_element_type | solution.py:29
  208.5 7.5 %all-to-all-start = ((bf16[32,64,1024]{2,1,0:T(8,128)(2,1)}), bf16[32,64,1024]{2,1,0:T(8,128)(2,1)}, u32[]{:S(2)}, u32[]{:S(2)}) async-start(bf16[32,64,1024]{2,1,0:T(8,128)(2,1)} %copy.11), calls=%async_computation | async-start | bytes 8388608 | tf_op jit(solution)/shard_map/all_to_all | solution.py:28
  216.0 0.0 all-gather.3.cloned.1.call-start
  216.0 0.7 all-gather.3.cloned.1.call-update
  216.7 0.6 dynamic_slice.12
  219.9 0.0 copy-start.1
  220.0 92.4 %all-to-all-done = bf16[32,64,1024]{2,1,0:T(8,128)(2,1)} async-done(((bf16[32,64,1024]{2,1,0:T(8,128)(2,1)}), bf16[32,64,1024]{2,1,0:T(8,128)(2,1)}, u32[]{:S(2)}, u32[]{:S(2)}) %all-to-all-start) | async-done | bytes 4194336 | tf_op jit(solution)/shard_map/all_to_all | solution.py:28
  312.3 1.8 constant_dynamic-slice_fusion
  314.2 0.0 copy-start.2
  314.2 0.0 copy-done.1
  314.2 1.3 fusion.3
  315.6 0.0 copy-done.2
  315.6 1.5 fusion.5
  317.0 0.0 all-gather.3.cloned.1.call-done
  317.0 0.0 copy-done
  317.0 3.1 fusion.9
  (1 shorter events, 0.0 us)
Async XLA Ops:
  7.2 309.9 %copy-start = (bf16[1,64,1024]{2,1,0:T(8,128)(2,1)S(1)}, bf16[1,64,1024]{2,1,0:T(8,128)(2,1)}, u32[]{:S(2)}) copy-start(bf16[1,64,1024]{2,1,0:T(8,128)(2,1)} %param.10) | copy-start | bytes 393220
  7.2 194.1 %all-reduce.2.cloned.1.call-start = ((), (), s32[]{:S(2)}) async-start(), calls=%async_computation.1 | async-start | bytes 4194304 | tf_op jit(solution)/shard_map/psum | solution.py:26
  11.4 0.7 copy-start.3
  208.5 103.9 %all-to-all-start = ((bf16[32,64,1024]{2,1,0:T(8,128)(2,1)}), bf16[32,64,1024]{2,1,0:T(8,128)(2,1)}, u32[]{:S(2)}, u32[]{:S(2)}) async-start(bf16[32,64,1024]{2,1,0:T(8,128)(2,1)} %copy.11), calls=%async_computation | async-start | bytes 8388608 | tf_op jit(solution)/shard_map/all_to_all | solution.py:28
  216.0 101.0 %all-gather.3.cloned.1.call-start = ((), (), s32[]{:S(2)}) async-start(), calls=%async_computation.2 | async-start | bytes 2228224 | tf_op jit(solution)/shard_map/all_gather | solution.py:55
  219.9 94.3 %copy-start.1 = (f32[1,64,1024]{2,1,0:T(8,128)S(1)}, f32[1,64,1024]{2,1,0:T(8,128)}, u32[]{:S(2)}) copy-start(f32[1,64,1024]{2,1,0:T(8,128)} %param.9) | copy-start | bytes 786436
  314.2 1.4 copy-start.2
Sparse Core Ops, SparseCore 0:
  11.5 189.6 all-reduce.1
  219.8 82.9 all-gather.2
where the time goes:
time: 327 us
  waiting for transfers between devices  282 us (86%)
  between operations  16.7 us (5%)
  local copies, waits for them, and re-layouts  11.5 us (4%)
  matrix products  8.84 us (3%)
  starting transfers between devices  7.58 us (2%)
    psum x1, waiting for transfers between devices, on_device(): lax.psum(partial_rows.astype(jnp.float32).astype(jnp.bfloat16), 'dp')  189 us
    all_to_all x1, waiting for transfers between devices, on_device(): lax.all_to_all(jnp.einsum('pb,rbw->prw', wanted, grad_grid, preferred_ele...  92.4 us
    all_to_all x1, starting transfers between devices, on_device(): lax.all_to_all(jnp.einsum('pb,rbw->prw', wanted, grad_grid, preferred_ele...  7.5 us
  transfers between devices with their start and end apart: 3, of which 2 were waited for; matrix products, arithmetic and copies ran while one was open for 2% of the time, Pallas kernels for 0%

commit v1 on v0

v1 whole, which is shorter than its diff:
```python
import jax
import jax.numpy as jnp
from jax import lax
from jax.experimental import pallas as pl
from jax.experimental.pallas import tpu as pltpu
from jax.sharding import Mesh
from jax.sharding import PartitionSpec as P

decay_rate = 0.95
DP = ("zh", "x")
MP = ("zl", "y", "c")
NX = 4
NZ = 4
VMEM_LIMIT = 32 * 1024 * 1024


def call(kernel, out_shape, **kw):
    return pl.pallas_call(
        kernel,
        out_shape=out_shape,
        compiler_params=pltpu.CompilerParams(vmem_limit_bytes=VMEM_LIMIT),
        **kw,
    )


def sum_x_kernel(got_ref, out_ref):
    _, n_blocks, _, width = out_ref.shape
    for c in range(n_blocks):
        for z in range(NZ):
            cols = slice((c * NZ + z) * width, (c * NZ + z + 1) * width)
            total = got_ref[0, :, cols].astype(jnp.float32)
            for src in range(1, NX):
                total += got_ref[src, :, cols].astype(jnp.float32)
            out_ref[z, c] = total.astype(out_ref.dtype)


def route_kernel(owner_ref, got_ref, out_ref):
    n_blocks = got_ref.shape[1]
    first = lax.axis_index("zl") * n_blocks
    out_ref[...] = jnp.zeros_like(out_ref)
    for c in range(n_blocks):
        total = got_ref[0, c].astype(jnp.float32)
        for src in range(1, NZ):
            total += got_ref[src, c].astype(jnp.float32)
        out_ref[owner_ref[first + c]] = total.astype(out_ref.dtype)


def select_kernel(owner_ref, got_ref, mine_ref):
    n = mine_ref.shape[0]
    me = lax.axis_index(MP)
    row = jnp.int32(0)
    for b in range(n, 2 * n):
        row += (owner_ref[b] == me).astype(jnp.int32)
    mine_ref[...] = got_ref[pl.ds(row * n, n)]


def copies_kernel(one_ref, out_ref):
    out_ref[0] = one_ref[...]


def root_kernel(got_ref, out_ref):
    depth = got_ref.shape[2]
    for z in range(NZ):
        for x in range(NX):
            out_ref[pl.ds((z * NX + x) * depth, depth), :] = got_ref[x, z]


def product_kernel(pieces_ref, right_root_ref, left_root_hbm, left_prev_hbm, right_prev_hbm,
                   left_hbm, right_hbm, update_hbm,
                   g_ref, left_root, left_prev, right_prev, gram_ref, left_new, right_new, update, sems):
    d = lax.axis_index("zh") * NX + lax.axis_index("x")
    loads = [
        pltpu.make_async_copy(a, b, sems.at[i])
        for i, (a, b) in enumerate(
            ((left_root_hbm, left_root), (left_prev_hbm, left_prev), (right_prev_hbm, right_prev))
        )
    ]
    stores = [
        pltpu.make_async_copy(a, b, sems.at[3 + i])
        for i, (a, b) in enumerate(((left_new, left_hbm), (right_new, right_hbm), (update, update_hbm)))
    ]
    for c in loads:
        c.start()
    n_src, high, width = pieces_ref.shape[2:]
    share = left_prev.shape[0]
    for z in range(NZ):
        for x in range(NX):
            for s in range(n_src):
                g_ref[pl.ds((s * NX + x) * high, high), pl.ds(z * width, width)] = pieces_ref[x, z, s]
    rows = g_ref[pl.ds(pl.multiple_of(d * share, share), share), :]
    g = g_ref[...]
    left_gram = lax.dot_general(rows, g, (((1,), (1,)), ((), ())), preferred_element_type=jnp.float32)
    for c in loads:
        c.wait()
    left_new[...] = decay_rate * left_prev[...] + (1.0 - decay_rate) * left_gram
    stores[0].start()
    pair = g_ref[:, pl.ds(pl.multiple_of((d // 2) * 2 * share, 2 * share), 2 * share)]
    gram_ref[...] = lax.dot_general(pair, g, (((0,), (0,)), ((), ())), preferred_element_type=jnp.float32)
    right_gram = gram_ref[pl.ds(pl.multiple_of(lax.rem(d, 2) * share, share), share), :]
    right_new[...] = decay_rate * right_prev[...] + (1.0 - decay_rate) * right_gram
    stores[1].start()
    half = jnp.dot(left_root[...], g, preferred_element_type=jnp.float32).astype(jnp.bfloat16)
    update[...] = jnp.dot(half, right_root_ref[...], preferred_element_type=jnp.float32).astype(update.dtype)
    stores[2].start()
    for c in stores:
        c.wait()


def on_device(partials, owner, left_prev, right_prev, left_root, right_root):
    bf16, f32 = jnp.bfloat16, jnp.float32
    part = partials[0]
    rows, cols = part.shape
    order = left_prev.shape[2]
    share = left_prev.shape[1]
    n_blocks = cols // order
    n_mp = lax.axis_size(MP)
    high = rows // NX
    width = order // NZ
    piece = (n_blocks, high, width)
    vmem = pl.BlockSpec(memory_space=pltpu.VMEM)
    smem = pl.BlockSpec(memory_space=pltpu.SMEM)
    anywhere = pl.BlockSpec(memory_space=pl.ANY)
    shape = jax.ShapeDtypeStruct

    root_z = lax.all_gather(right_root[0], "zh")
    got = lax.all_to_all(part.reshape(NX, high, cols), "x", 0, 0, tiled=True)
    got, root_z = lax.optimization_barrier((got, root_z))
    root_xz = lax.all_gather(root_z, "x")
    cut = 4
    sums = call(
        sum_x_kernel,
        shape((NZ,) + piece, bf16),
        grid=(cut,),
        in_specs=[pl.BlockSpec((NX, high, cols // cut), lambda i: (0, 0, i))],
        out_specs=pl.BlockSpec((NZ, n_blocks // cut, high, width), lambda i: (0, i, 0, 0)),
    )(got)
    got = lax.all_to_all(sums, "zh", 0, 0, tiled=True)
    routed = call(
        route_kernel, shape((n_mp, high, width), bf16), in_specs=[smem, vmem], out_specs=vmem
    )(owner, got)
    got = lax.all_to_all(routed, MP, 0, 0, tiled=True)
    mine = call(select_kernel, shape(piece, bf16), in_specs=[smem, vmem], out_specs=vmem)(owner, got)
    column = lax.all_gather(mine, "zh")
    copies = call(
        copies_kernel,
        shape((NX, NZ) + piece, bf16),
        grid=(NX,),
        in_specs=[pl.BlockSpec((NZ,) + piece, lambda i: (0, 0, 0, 0))],
        out_specs=pl.BlockSpec((1, NZ) + piece, lambda i: (i, 0, 0, 0, 0)),
    )(column)
    pieces = lax.all_to_all(copies, "x", 0, 0, tiled=True)
    root = call(root_kernel, shape((order, order), bf16), in_specs=[vmem], out_specs=vmem)(root_xz)
    left_new, right_new, update = call(
        product_kernel,
        (shape((share, order), f32), shape((share, order), f32), shape((share, order), bf16)),
        in_specs=[vmem, vmem, anywhere, anywhere, anywhere],
        out_specs=(anywhere, anywhere, anywhere),
        scratch_shapes=[
            pltpu.VMEM((order, order), bf16),
            pltpu.VMEM((share, order), bf16),
            pltpu.VMEM((share, order), f32),
            pltpu.VMEM((share, order), f32),
            pltpu.VMEM((2 * share, order), f32),
            pltpu.VMEM((share, order), f32),
            pltpu.VMEM((share, order), f32),
            pltpu.VMEM((share, order), bf16),
            pltpu.SemaphoreType.DMA((6,)),
        ],
    )(pieces, root, left_root[0], left_prev[0], right_prev[0])
    return left_new[None], right_new[None], update[None]


def solution(mesh):
    cut = Mesh(mesh.devices.reshape(NZ, NX, 2, 8, 2), DP + MP)
    spread = P(MP, DP, None)
    return jax.shard_map(
        on_device,
        mesh=cut,
        in_specs=(P(DP, MP, None), P(), spread, spread, spread, spread),
        out_specs=(spread, spread, spread),
        check_vma=False,
    )
```

time: 327 us -> 142 us (0.43)
  the two profiles are of different devices: /device:TPU:24 before, /device:TPU:8 now
where the time goes in v1:
time: 142 us
  blocking collectives  84.4 us (59%)
  waiting for transfers between devices  24 us (17%)
  between operations  14.1 us (10%)
  starting transfers between devices  8.04 us (6%)
  local copies, waits for them, and re-layouts  5.83 us (4%)
  Pallas kernels  5.2 us (4%)
    all_to_all x1, blocking collectives, on_device(): got = lax.all_to_all(sums, 'zh', 0, 0, tiled=True)  26 us
    all_gather x1, blocking collectives, on_device(): root_z = lax.all_gather(right_root[0], 'zh')  21.9 us
    all_to_all x1, blocking collectives, on_device(): got = lax.all_to_all(routed, MP, 0, 0, tiled=True)  19.9 us
    all_to_all x1, waiting for transfers between devices, on_device(): pieces = lax.all_to_all(copies, 'x', 0, 0, tiled=True)  19.6 us
    all_gather x1, blocking collectives, on_device(): column = lax.all_gather(mine, 'zh')  16.6 us
    unnamed x18, local copies, waits for them, and re-layouts  5.83 us
    all_to_all x1, starting transfers between devices, on_device(): got = lax.all_to_all(part.reshape(NX, high, cols), 'x', 0, 0, tiled=True)  4.44 us
    all_to_all x1, waiting for transfers between devices, on_device(): got = lax.all_to_all(part.reshape(NX, high, cols), 'x', 0, 0, tiled=True)  4.43 us
  transfers between devices with their start and end apart: 3, of which 2 were waited for; matrix products, arithmetic and copies ran while one was open for 0% of the time, Pallas kernels for 1%

profile of v1, /device:TPU:8, one launch (start us, length us, event | category | flops | bytes accessed | tf_op | source)
XLA Modules:
  0.0 141.7 jit_solution(10388332298267984202)
XLA Ops:
  7.2 0.0 copy-start.8
  7.2 4.4 %all-to-all-start = ((bf16[4,16,16384]{2,1,0:T(8,128)(2,1)}), bf16[4,16,16384]{2,1,0:T(8,128)(2,1)S(1)}, u32[]{:S(2)}, u32[]{:S(2)}) async-start(bf16[4,16,16384]{2,1,0:T(8,128)(2,1)} %bitcast.14), calls=%async_computation | async-start | bytes 4194304 | tf_op jit(solution)/shard_map/all_to_all | solution.py:126
  11.6 0.0 all-gather.4.cloned.1.call-start
  11.6 0.0 copy-done.8
  11.6 21.9 %all_gather.15 = bf16[4,64,1024]{2,1,0:T(8,128)(2,1)} all-gather(bf16[1,64,1024]{2,1,0:T(8,128)(2,1)S(1)} %copy-done.8), channel_id=1, replica_groups=mesh['zh'=4,'x'=4,'zl'=2,'y'=8,'c'=2] {'zh'}, dimensions={0}, use_global_device_ids=true | all-gather | bytes 655360 | tf_op jit(solution)/shard_map/all_gather | solution.py:125
  33.5 0.0 copy-start.7
  33.5 4.4 %all-to-all-done.got_ref = bf16[4,16,16384]{2,1,0:T(8,128)(2,1)S(1)} async-done(((bf16[4,16,16384]{2,1,0:T(8,128)(2,1)}), bf16[4,16,16384]{2,1,0:T(8,128)(2,1)S(1)}, u32[]{:S(2)}, u32[]{:S(2)}) %all-to-all-start) | async-done | bytes 2097184 | tf_op jit(solution)/shard_map/all_to_all | solution.py:126
  37.9 0.0 all-gather.4.cloned.1.call-update
  38.0 0.5 shard_map.85
  38.5 26.0 %all_to_all.20.got_ref = bf16[4,16,16,256]{3,2,1,0:T(8,128)(2,1)S(1)} all-to-all(bf16[4,16,16,256]{3,2,1,0:T(8,128)(2,1)S(1)} %shard_map.85), channel_id=1, replica_groups=mesh['zh'=4,'x'=4,'zl'=2,'y'=8,'c'=2] {'zh'}, dimensions={0} | all-to-all | bytes 1048576 | tf_op jit(solution)/shard_map/all_to_all | solution.py:137
  64.5 0.0 copy-done.7
  64.5 0.6 shard_map.86
  65.1 19.9 %all_to_all.21.got_ref = bf16[32,16,256]{2,1,0:T(8,128)(2,1)S(1)} all-to-all(bf16[32,16,256]{2,1,0:T(8,128)(2,1)S(1)} %shard_map.86), channel_id=1, replica_groups=mesh['zh'=4,'x'=4,'zl'=2,'y'=8,'c'=2] {'zl','y','c'}, dimensions={0} | all-to-all | bytes 524288 | tf_op jit(solution)/shard_map/all_to_all | solution.py:141
  85.0 0.6 shard_map.87
  85.6 16.6 %all-gather = bf16[64,16,256]{2,1,0:T(8,128)(2,1)S(1)} all-gather(bf16[16,16,256]{2,1,0:T(8,128)(2,1)S(1)} %shard_map.87), channel_id=2, replica_groups=mesh['zh'=4,'x'=4,'zl'=2,'y'=8,'c'=2] {'zh'}, dimensions={0}, use_global_device_ids=true | all-gather | bytes 655360 | tf_op jit(solution)/shard_map/all_gather | solution.py:143
  102.2 0.2 shard_map.88
  102.4 0.0 copy-start
  102.4 1.3 copy-done
  103.8 3.6 %all-to-all-start.3 = ((bf16[4,4,16,16,256]{4,3,2,1,0:T(8,128)(2,1)}), bf16[4,4,16,16,256]{4,3,2,1,0:T(8,128)(2,1)S(1)}, u32[]{:S(2)}, u32[]{:S(2)}) async-start(bf16[4,4,16,16,256]{4,3,2,1,0:T(8,128)(2,1)} %copy-done), calls=%async_computation.3 | async-start | bytes 4194304 | tf_op jit(solution)/shard_map/all_to_all | solution.py:151
  107.4 0.0 all-gather.4.cloned.1.call-done
  107.4 0.0 copy-start.3
  107.4 1.6 %copy-done.3 = bf16[16,64,1024]{2,1,0:T(8,128)(2,1)S(1)} copy-done((bf16[16,64,1024]{2,1,0:T(8,128)(2,1)S(1)}, bf16[16,64,1024]{2,1,0:T(8,128)(2,1)}, u32[]{:S(2)}) %copy-start.3) | copy-done | bytes 2097176
  109.0 0.1 shard_map.89.right_root_ref
  109.1 0.0 copy-start.1
  109.2 1.3 copy-done.1
  110.5 19.6 %all-to-all-done.3.pieces_ref = bf16[4,4,16,16,256]{4,3,2,1,0:T(8,128)(2,1)S(1)} async-done(((bf16[4,4,16,16,256]{4,3,2,1,0:T(8,128)(2,1)}), bf16[4,4,16,16,256]{4,3,2,1,0:T(8,128)(2,1)S(1)}, u32[]{:S(2)}, u32[]{:S(2)}) %all-to-all-start.3) | async-done | bytes 2097184 | tf_op jit(solution)/shard_map/all_to_all | solution.py:151
  130.0 0.0 copy-done.4
  130.0 0.0 copy-done.5
  130.0 0.0 copy-done.6
  130.0 0.0 copy-start.2
  130.1 1.6 %copy-done.2 = bf16[1024,1024]{1,0:T(8,128)(2,1)S(1)} copy-done((bf16[1024,1024]{1,0:T(8,128)(2,1)S(1)}, bf16[1024,1024]{1,0:T(8,128)(2,1)}, u32[]{:S(2)}) %copy-start.2) | copy-done | bytes 2097176
  131.6 3.2 %shard_map.90 = (f32[64,1024]{1,0:T(8,128)}, f32[64,1024]{1,0:T(8,128)}, bf16[64,1024]{1,0:T(8,128)(2,1)}) custom-call(bf16[4,4,16,16,256]{4,3,2,1,0:T(8,128)(2,1)S(1)} %all-to-all-done.3.pieces_ref, bf16[1024,1024]{1,0:T(8,128)(2,1)S(1)} %copy-done.2, bf16[64,1024]{1,0:T(8,128)(2,1)S(1)} %bitcast.13, f32[64,1024]{1,0:T(8,128)S(1)} %bitcast.11, ...), custom_call_target="tpu_custom_call" | custom-call | tf_op jit(solution)/shard_map/pallas_call | solution.py:153
  (3 shorter events, 0.0 us)
Async XLA Ops:
  7.2 4.5 %copy-start.8 = (bf16[1,64,1024]{2,1,0:T(8,128)(2,1)S(1)}, bf16[1,64,1024]{2,1,0:T(8,128)(2,1)}, u32[]{:S(2)}) copy-start(bf16[1,64,1024]{2,1,0:T(8,128)(2,1)} %param.11) | copy-start | bytes 393220
  7.2 30.8 %all-to-all-start = ((bf16[4,16,16384]{2,1,0:T(8,128)(2,1)}), bf16[4,16,16384]{2,1,0:T(8,128)(2,1)S(1)}, u32[]{:S(2)}, u32[]{:S(2)}) async-start(bf16[4,16,16384]{2,1,0:T(8,128)(2,1)} %bitcast.14), calls=%async_computation | async-start | bytes 4194304 | tf_op jit(solution)/shard_map/all_to_all | solution.py:126
  11.6 95.8 %all-gather.4.cloned.1.call-start = ((), (), s32[]{:S(2)}) async-start(), calls=%async_computation.4 | async-start | bytes 2621440 | tf_op jit(solution)/shard_map/all_gather | solution.py:128
  33.5 31.0 %copy-start.7 = (s32[32]{0:T(128)S(1)}, s32[32]{0:T(128)}, u32[]{:S(2)}) copy-start(s32[32]{0:T(128)} %owner_ref.3) | copy-start | bytes 388
  102.4 1.3 copy-start
  103.8 26.3 %all-to-all-start.3 = ((bf16[4,4,16,16,256]{4,3,2,1,0:T(8,128)(2,1)}), bf16[4,4,16,16,256]{4,3,2,1,0:T(8,128)(2,1)S(1)}, u32[]{:S(2)}, u32[]{:S(2)}) async-start(bf16[4,4,16,16,256]{4,3,2,1,0:T(8,128)(2,1)} %copy-done), calls=%async_computation.3 | async-start | bytes 4194304 | tf_op jit(solution)/shard_map/all_to_all | solution.py:151
  107.4 1.6 %copy-start.3 = (bf16[16,64,1024]{2,1,0:T(8,128)(2,1)S(1)}, bf16[16,64,1024]{2,1,0:T(8,128)(2,1)}, u32[]{:S(2)}) copy-start(bf16[16,64,1024]{2,1,0:T(8,128)(2,1)} %all-gather.4.cloned.1.call-done) | copy-start | bytes 6291460
  109.0 21.0 %copy-start.4 = (f32[1,64,1024]{2,1,0:T(8,128)S(1)}, f32[1,64,1024]{2,1,0:T(8,128)}, u32[]{:S(2)}) copy-start(f32[1,64,1024]{2,1,0:T(8,128)} %param.8) | copy-start | bytes 786436
  109.0 21.0 %copy-start.5 = (f32[1,64,1024]{2,1,0:T(8,128)S(1)}, f32[1,64,1024]{2,1,0:T(8,128)}, u32[]{:S(2)}) copy-start(f32[1,64,1024]{2,1,0:T(8,128)} %param.9) | copy-start | bytes 786436
  109.0 21.0 %copy-start.6 = (bf16[1,64,1024]{2,1,0:T(8,128)(2,1)S(1)}, bf16[1,64,1024]{2,1,0:T(8,128)(2,1)}, u32[]{:S(2)}) copy-start(bf16[1,64,1024]{2,1,0:T(8,128)(2,1)} %param.10) | copy-start | bytes 393220
  109.1 1.3 copy-start.1
  130.0 1.6 %copy-start.2 = (bf16[1024,1024]{1,0:T(8,128)(2,1)S(1)}, bf16[1024,1024]{1,0:T(8,128)(2,1)}, u32[]{:S(2)}) copy-start(bf16[1024,1024]{1,0:T(8,128)(2,1)} %copy-done.1) | copy-start | bytes 6291460
Sparse Core Ops, SparseCore 0:
  38.1 38.8 all-gather.3

commit v2 on v1

v2 whole, which is shorter than its diff:
```python
import jax
import jax.numpy as jnp
from jax import lax
from jax.experimental import pallas as pl
from jax.experimental.pallas import tpu as pltpu
from jax.sharding import Mesh
from jax.sharding import PartitionSpec as P

decay_rate = 0.95
DP = ("zh", "x")
MP = ("zl", "y", "c")
NX = 4
NZ = 4
NL = 2
VMEM_LIMIT = 32 * 1024 * 1024


def call(kernel, out_shape, **kw):
    return pl.pallas_call(
        kernel,
        out_shape=out_shape,
        compiler_params=pltpu.CompilerParams(vmem_limit_bytes=VMEM_LIMIT),
        **kw,
    )


def sum_x_kernel(got_ref, out_ref):
    n_z, n_blocks, _, width = out_ref.shape
    for c in range(n_blocks):
        for z in range(n_z):
            cols = slice((c * n_z + z) * width, (c * n_z + z + 1) * width)
            total = got_ref[0, :, cols].astype(jnp.float32)
            for src in range(1, NX):
                total += got_ref[src, :, cols].astype(jnp.float32)
            out_ref[z, c] = total.astype(out_ref.dtype)


def route_kernel(owner_ref, got_ref, out_ref):
    n_blocks = got_ref.shape[1]
    for r in range(NL):
        for c in range(n_blocks):
            total = got_ref[r, c].astype(jnp.float32)
            for src in range(1, NZ):
                total += got_ref[src * NL + r, c].astype(jnp.float32)
            out_ref[owner_ref[r * n_blocks + c]] = total.astype(out_ref.dtype)


def copies_kernel(one_ref, out_ref):
    out_ref[0] = one_ref[...]


def pair_kernel(one_ref, two_ref, out_ref):
    out_ref[0] = one_ref[...]
    out_ref[1] = two_ref[...]


def product_kernel(*refs):
    pieces_ref = refs[0]
    (pair_ref, swap_ref, left_root_hbm, left_prev_hbm, right_prev_hbm, left_hbm, right_hbm, update_hbm,
     g_ref, root_ref, left_root, left_prev, right_prev, gram_ref, left_new, right_new, update, sems) = refs[1:]
    zh = lax.axis_index("zh")
    x_me = lax.axis_index("x")
    d = zh * NX + x_me
    share = left_prev.shape[0]
    loads = [
        pltpu.make_async_copy(a, b, sems.at[i])
        for i, (a, b) in enumerate(
            ((left_root_hbm, left_root), (left_prev_hbm, left_prev), (right_prev_hbm, right_prev))
        )
    ]
    stores = [
        pltpu.make_async_copy(a, b, sems.at[3 + i])
        for i, (a, b) in enumerate(((left_new, left_hbm), (right_new, right_hbm), (update, update_hbm)))
    ]
    for c in loads:
        c.start()
    n_piece, high, width = pieces_ref.shape[2:]
    n_src = n_piece // NL
    for j in range(NX):
        for z in range(NZ):
            for p in range(n_piece):
                at = (p % n_src * NX + j) * high
                to = (z * NL + p // n_src) * width
                g_ref[at : at + high, to : to + width] = pieces_ref[j, z, p]
    rows = g_ref[pl.ds(pl.multiple_of(d * share, share), share), :]
    g = g_ref[...]
    left_gram = lax.dot_general(rows, g, (((1,), (1,)), ((), ())), preferred_element_type=jnp.float32)
    for c in loads:
        c.wait()
    left_new[...] = decay_rate * left_prev[...] + (1.0 - decay_rate) * left_gram
    stores[0].start()
    pair = g_ref[:, pl.ds(pl.multiple_of((d // 2) * 2 * share, 2 * share), 2 * share)]
    gram_ref[...] = lax.dot_general(pair, g, (((0,), (0,)), ((), ())), preferred_element_type=jnp.float32)
    right_gram = gram_ref[pl.ds(pl.multiple_of(lax.rem(d, 2) * share, share), share), :]
    right_new[...] = decay_rate * right_prev[...] + (1.0 - decay_rate) * right_gram
    stores[1].start()
    half = jnp.dot(left_root[...], g, preferred_element_type=jnp.float32).astype(jnp.bfloat16)
    for j, (ref, part) in enumerate(((pair_ref, 0), (pair_ref, 1), (swap_ref, 1), (swap_ref, 0))):
        for z in range(NZ):
            at = pl.multiple_of((z * NX + lax.bitwise_xor(x_me, j)) * share, share)
            root_ref[pl.ds(at, share), :] = ref[part, z * share : (z + 1) * share, :]
    update[...] = jnp.dot(half, root_ref[...], preferred_element_type=jnp.float32).astype(update.dtype)
    stores[2].start()
    for c in stores:
        c.wait()


def on_device(partials, owner, left_prev, right_prev, left_root, right_root):
    bf16, f32 = jnp.bfloat16, jnp.float32
    part = partials[0]
    rows, cols = part.shape
    order = left_prev.shape[2]
    share = left_prev.shape[1]
    n_blocks = cols // order
    n_mp = lax.axis_size(MP)
    high = rows // NX
    width = order // (NZ * NL)
    piece = (n_blocks, high, width)
    vmem = pl.BlockSpec(memory_space=pltpu.VMEM)
    smem = pl.BlockSpec(memory_space=pltpu.SMEM)
    anywhere = pl.BlockSpec(memory_space=pl.ANY)
    shape = jax.ShapeDtypeStruct

    swaps = {k: [(i, i ^ k) for i in range(NX)] for k in range(1, NX)}

    root_z = lax.all_gather(right_root[0], "zh", tiled=True)
    got = lax.all_to_all(part.reshape(NX, high, cols), "x", 0, 0, tiled=True)
    got, root_z = lax.optimization_barrier((got, root_z))
    cut = 4
    sums = call(
        sum_x_kernel,
        shape((NZ * NL,) + piece, bf16),
        grid=(cut,),
        in_specs=[pl.BlockSpec((NX, high, cols // cut), lambda i: (0, 0, i))],
        out_specs=pl.BlockSpec((NZ * NL, n_blocks // cut, high, width), lambda i: (0, i, 0, 0)),
    )(got)
    root_next = lax.ppermute(root_z, "x", swaps[1])
    got = lax.all_to_all(sums, ("zh", "zl"), 0, 0, tiled=True)
    got, root_z, root_next = lax.optimization_barrier((got, root_z, root_next))
    routed = call(
        route_kernel, shape((n_mp, high, width), bf16), in_specs=[smem, vmem], out_specs=vmem
    )(owner, got)
    root_pair = call(
        pair_kernel, shape((2,) + root_z.shape, bf16), in_specs=[vmem, vmem], out_specs=vmem
    )(root_z, root_next)
    routed, root_pair = lax.optimization_barrier((routed, root_pair))
    root_swap = lax.ppermute(root_pair, "x", swaps[3])
    mine = lax.all_to_all(routed, MP, 0, 0, tiled=True)
    column = lax.all_gather(mine, "zh")
    column, root_swap = lax.optimization_barrier((column, root_swap))
    copies = call(
        copies_kernel,
        shape((NX,) + column.shape, bf16),
        grid=(NX,),
        in_specs=[pl.BlockSpec(column.shape, lambda i: (0, 0, 0, 0))],
        out_specs=pl.BlockSpec((1,) + column.shape, lambda i: (i, 0, 0, 0, 0)),
    )(column)
    pieces = lax.all_to_all(copies, "x", 0, 0, tiled=True)
    left_new, right_new, update = call(
        product_kernel,
        (shape((share, order), f32), shape((share, order), f32), shape((share, order), bf16)),
        in_specs=[vmem] * 3 + [anywhere] * 3,
        out_specs=(anywhere, anywhere, anywhere),
        scratch_shapes=[
            pltpu.VMEM((order, order), bf16),
            pltpu.VMEM((order, order), bf16),
            pltpu.VMEM((share, order), bf16),
            pltpu.VMEM((share, order), f32),
            pltpu.VMEM((share, order), f32),
            pltpu.VMEM((2 * share, order), f32),
            pltpu.VMEM((share, order), f32),
            pltpu.VMEM((share, order), f32),
            pltpu.VMEM((share, order), bf16),
            pltpu.SemaphoreType.DMA((6,)),
        ],
    )(pieces, root_pair, root_swap, left_root[0], left_prev[0], right_prev[0])
    return left_new[None], right_new[None], update[None]


def solution(mesh):
    cut = Mesh(mesh.devices.reshape(NZ, NX, 2, 8, 2), DP + MP)
    spread = P(MP, DP, None)
    return jax.shard_map(
        on_device,
        mesh=cut,
        in_specs=(P(DP, MP, None), P(), spread, spread, spread, spread),
        out_specs=(spread, spread, spread),
        check_vma=False,
    )
```

time: 142 us -> 128 us (0.901)
  the two profiles are of different devices: /device:TPU:8 before, /device:TPU:16 now
where the time goes in v2:
time: 128 us
  blocking collectives  82.3 us (64%)
  starting transfers between devices  20.3 us (16%)
  waiting for transfers between devices  18.2 us (14%)
  Pallas kernels  6.08 us (5%)
    all_to_all x1, blocking collectives, on_device(): pieces = lax.all_to_all(copies, 'x', 0, 0, tiled=True)  28.9 us
    all_gather x1, blocking collectives, on_device(): root_z = lax.all_gather(right_root[0], 'zh', tiled=True)  22 us
    all_gather x1, blocking collectives, on_device(): column = lax.all_gather(mine, 'zh')  16.2 us
    all_to_all x1, blocking collectives, on_device(): mine = lax.all_to_all(routed, MP, 0, 0, tiled=True)  15.3 us
    ppermute x1, waiting for transfers between devices, on_device(): root_next = lax.ppermute(root_z, 'x', swaps[1])  11.6 us
    all_to_all x1, starting transfers between devices, on_device(): got = lax.all_to_all(sums, ('zh', 'zl'), 0, 0, tiled=True)  10.3 us
    all_to_all x1, starting transfers between devices, on_device(): got = lax.all_to_all(part.reshape(NX, high, cols), 'x', 0, 0, tiled=True)  4.44 us
    all_to_all x1, waiting for transfers between devices, on_device(): got = lax.all_to_all(part.reshape(NX, high, cols), 'x', 0, 0, tiled=True)  4.36 us
  transfers between devices with their start and end apart: 4, of which 3 were waited for; matrix products, arithmetic and copies ran while one was open for 0% of the time, Pallas kernels for 0%

profile of v2, /device:TPU:16, one launch (start us, length us, event | category | flops | bytes accessed | tf_op | source)
XLA Modules:
  0.0 127.6 jit_solution(17483212418513838411)
XLA Ops:
  0.6 0.0 copy-start.4
  0.6 4.4 %all-to-all-start = ((bf16[4,16,16384]{2,1,0:T(8,128)(2,1)}), bf16[4,16,16384]{2,1,0:T(8,128)(2,1)S(1)}, u32[]{:S(2)}, u32[]{:S(2)}) async-start(bf16[4,16,16384]{2,1,0:T(8,128)(2,1)} %bitcast.15), calls=%async_computation | async-start | bytes 4194304 | tf_op jit(solution)/shard_map/all_to_all | solution.py:127
  5.1 0.0 copy-done.4
  5.1 0.0 copy-start.3
  5.1 22.0 %all-gather = bf16[1,256,1024]{2,1,0:T(8,128)(2,1)S(1)} all-gather(bf16[1,64,1024]{2,1,0:T(8,128)(2,1)S(1)} %copy-done.4), channel_id=2, replica_groups=mesh['zh'=4,'x'=4,'zl'=2,'y'=8,'c'=2] {'zh'}, dimensions={1}, use_global_device_ids=true | all-gather | bytes 655360 | tf_op jit(solution)/shard_map/all_gather | solution.py:126
  27.0 4.4 %all-to-all-done.got_ref = bf16[4,16,16384]{2,1,0:T(8,128)(2,1)S(1)} async-done(((bf16[4,16,16384]{2,1,0:T(8,128)(2,1)}), bf16[4,16,16384]{2,1,0:T(8,128)(2,1)S(1)}, u32[]{:S(2)}, u32[]{:S(2)}) %all-to-all-start) | async-done | bytes 2097184 | tf_op jit(solution)/shard_map/all_to_all | solution.py:127
  31.4 1.7 %shard_map.85 = bf16[8,16,16,128]{3,2,1,0:T(8,128)(2,1)} custom-call(bf16[4,16,16384]{2,1,0:T(8,128)(2,1)S(1)} %all-to-all-done.got_ref), custom_call_target="tpu_custom_call" | custom-call | tf_op jit(solution)/shard_map/pallas_call | solution.py:130
  33.1 10.3 %all-to-all-start.1 = ((bf16[8,16,16,128]{3,2,1,0:T(8,128)(2,1)}), bf16[8,16,16,128]{3,2,1,0:T(8,128)(2,1)S(1)}, u32[]{:S(2)}, u32[]{:S(2)}) async-start(bf16[8,16,16,128]{3,2,1,0:T(8,128)(2,1)} %shard_map.85), calls=%async_computation.1 | async-start | bytes 1048576 | tf_op jit(solution)/shard_map/all_to_all | solution.py:138
  43.4 2.5 %collective-permute-start = (bf16[256,1024]{1,0:T(8,128)(2,1)S(1)}, bf16[256,1024]{1,0:T(8,128)(2,1)S(1)}, u32[]{:S(2)}, u32[]{:S(2)}) collective-permute-start(bf16[256,1024]{1,0:T(8,128)(2,1)S(1)} %bitcast.10), channel_id=1, source_target_pairs={{0,32},{32,0},{64,96},{96,64},{1,33},{33,1},{65,97},{97,65},{2,34}... | collective-permute-start | bytes 1572872 | tf_op jit(solution)/shard_map/ppermute | solution.py:137
  45.9 11.6 %collective-permute-done.two_ref = bf16[256,1024]{1,0:T(8,128)(2,1)S(1)} collective-permute-done((bf16[256,1024]{1,0:T(8,128)(2,1)S(1)}, bf16[256,1024]{1,0:T(8,128)(2,1)S(1)}, u32[]{:S(2)}, u32[]{:S(2)}) %collective-permute-start) | collective-permute-done | bytes 524320 | tf_op jit(solution)/shard_map/ppermute | solution.py:137
  57.5 2.2 %all-to-all-done.1.got_ref = bf16[8,16,16,128]{3,2,1,0:T(8,128)(2,1)S(1)} async-done(((bf16[8,16,16,128]{3,2,1,0:T(8,128)(2,1)}), bf16[8,16,16,128]{3,2,1,0:T(8,128)(2,1)S(1)}, u32[]{:S(2)}, u32[]{:S(2)}) %all-to-all-start.1) | async-done | bytes 524320 | tf_op jit(solution)/shard_map/all_to_all | solution.py:138
  59.7 0.0 copy-done.3
  59.7 0.6 shard_map.86
  60.3 0.1 shard_map.87.refs_1_
  60.4 3.1 %collective-permute-start.1 = (bf16[2,256,1024]{2,1,0:T(8,128)(2,1)S(1)}, bf16[2,256,1024]{2,1,0:T(8,128)(2,1)S(1)}, u32[]{:S(2)}, u32[]{:S(2)}) collective-permute-start(bf16[2,256,1024]{2,1,0:T(8,128)(2,1)S(1)} %shard_map.87.refs_1_), channel_id=1, source_target_pairs={{0,96},{32,64},{64,32},{96,0},{1,97},{33,65},{65,33},{97,1},{2,98}... | collective-permute-start | bytes 3145736 | tf_op jit(solution)/shard_map/ppermute | solution.py:147
  63.5 15.3 %all_to_all.20 = bf16[32,16,128]{2,1,0:T(8,128)(2,1)S(1)} all-to-all(bf16[32,16,128]{2,1,0:T(8,128)(2,1)S(1)} %shard_map.86), channel_id=1, replica_groups=mesh['zh'=4,'x'=4,'zl'=2,'y'=8,'c'=2] {'zl','y','c'}, dimensions={0} | all-to-all | bytes 262144 | tf_op jit(solution)/shard_map/all_to_all | solution.py:148
  78.7 16.2 %all-gather.1 = bf16[128,16,128]{2,1,0:T(8,128)(2,1)S(1)} all-gather(bf16[32,16,128]{2,1,0:T(8,128)(2,1)S(1)} %all_to_all.20), channel_id=3, replica_groups=mesh['zh'=4,'x'=4,'zl'=2,'y'=8,'c'=2] {'zh'}, dimensions={0}, use_global_device_ids=true | all-gather | bytes 655360 | tf_op jit(solution)/shard_map/all_gather | solution.py:149
  94.9 0.0 collective-permute-done.1.refs_2_
  94.9 0.2 shard_map.88
  95.1 0.0 copy-start
  95.1 0.0 copy-start.1
  95.1 0.0 copy-start.2
  95.2 28.9 %all_to_all.21.refs_0_ = bf16[4,4,32,16,128]{4,3,2,1,0:T(8,128)(2,1)S(1)} all-to-all(bf16[4,4,32,16,128]{4,3,2,1,0:T(8,128)(2,1)S(1)} %shard_map.88), channel_id=1, replica_groups=mesh['zh'=4,'x'=4,'zl'=2,'y'=8,'c'=2] {'x'}, dimensions={0} | all-to-all | bytes 4194304 | tf_op jit(solution)/shard_map/all_to_all | solution.py:158
  124.0 0.0 copy-done
  124.0 0.0 copy-done.1
  124.0 0.0 copy-done.2
  124.0 3.5 %shard_map.89 = (f32[64,1024]{1,0:T(8,128)}, f32[64,1024]{1,0:T(8,128)}, bf16[64,1024]{1,0:T(8,128)(2,1)}) custom-call(bf16[4,4,32,16,128]{4,3,2,1,0:T(8,128)(2,1)S(1)} %all_to_all.21.refs_0_, bf16[2,256,1024]{2,1,0:T(8,128)(2,1)S(1)} %shard_map.87.refs_1_, bf16[2,256,1024]{2,1,0:T(8,128)(2,1)S(1)} %collective-permute-done.1.refs_2_, ...), custom_call_target="tpu_custom_call" | custom-call | tf_op jit(solution)/shard_map/pallas_call | solution.py:159
Async XLA Ops:
  0.6 4.4 %copy-start.4 = (bf16[1,64,1024]{2,1,0:T(8,128)(2,1)S(1)}, bf16[1,64,1024]{2,1,0:T(8,128)(2,1)}, u32[]{:S(2)}) copy-start(bf16[1,64,1024]{2,1,0:T(8,128)(2,1)} %param.11) | copy-start | bytes 393220
  0.6 30.8 %all-to-all-start = ((bf16[4,16,16384]{2,1,0:T(8,128)(2,1)}), bf16[4,16,16384]{2,1,0:T(8,128)(2,1)S(1)}, u32[]{:S(2)}, u32[]{:S(2)}) async-start(bf16[4,16,16384]{2,1,0:T(8,128)(2,1)} %bitcast.15), calls=%async_computation | async-start | bytes 4194304 | tf_op jit(solution)/shard_map/all_to_all | solution.py:127
  5.1 54.6 %copy-start.3 = (s32[32]{0:T(128)S(1)}, s32[32]{0:T(128)}, u32[]{:S(2)}) copy-start(s32[32]{0:T(128)} %owner_ref.1) | copy-start | bytes 388
  33.1 26.6 %all-to-all-start.1 = ((bf16[8,16,16,128]{3,2,1,0:T(8,128)(2,1)}), bf16[8,16,16,128]{3,2,1,0:T(8,128)(2,1)S(1)}, u32[]{:S(2)}, u32[]{:S(2)}) async-start(bf16[8,16,16,128]{3,2,1,0:T(8,128)(2,1)} %shard_map.85), calls=%async_computation.1 | async-start | bytes 1048576 | tf_op jit(solution)/shard_map/all_to_all | solution.py:138
  43.4 14.1 %collective-permute-start = (bf16[256,1024]{1,0:T(8,128)(2,1)S(1)}, bf16[256,1024]{1,0:T(8,128)(2,1)S(1)}, u32[]{:S(2)}, u32[]{:S(2)}) collective-permute-start(bf16[256,1024]{1,0:T(8,128)(2,1)S(1)} %bitcast.10), channel_id=1, source_target_pairs={{0,32},{32,0},{64,96},{96,64},{1,33},{33,1},{65,97},{97,65},{2,34}... | collective-permute-start | bytes 1572872 | tf_op jit(solution)/shard_map/ppermute | solution.py:137
  60.4 34.5 %collective-permute-start.1 = (bf16[2,256,1024]{2,1,0:T(8,128)(2,1)S(1)}, bf16[2,256,1024]{2,1,0:T(8,128)(2,1)S(1)}, u32[]{:S(2)}, u32[]{:S(2)}) collective-permute-start(bf16[2,256,1024]{2,1,0:T(8,128)(2,1)S(1)} %shard_map.87.refs_1_), channel_id=1, source_target_pairs={{0,96},{32,64},{64,32},{96,0},{1,97},{33,65},{65,33},{97,1},{2,98}... | collective-permute-start | bytes 3145736 | tf_op jit(solution)/shard_map/ppermute | solution.py:147
  95.1 28.9 %copy-start = (f32[1,64,1024]{2,1,0:T(8,128)S(1)}, f32[1,64,1024]{2,1,0:T(8,128)}, u32[]{:S(2)}) copy-start(f32[1,64,1024]{2,1,0:T(8,128)} %param.8) | copy-start | bytes 786436
  95.1 28.9 %copy-start.1 = (f32[1,64,1024]{2,1,0:T(8,128)S(1)}, f32[1,64,1024]{2,1,0:T(8,128)}, u32[]{:S(2)}) copy-start(f32[1,64,1024]{2,1,0:T(8,128)} %param.9) | copy-start | bytes 786436
  95.1 28.9 %copy-start.2 = (bf16[1,64,1024]{2,1,0:T(8,128)(2,1)S(1)}, bf16[1,64,1024]{2,1,0:T(8,128)(2,1)}, u32[]{:S(2)}) copy-start(bf16[1,64,1024]{2,1,0:T(8,128)(2,1)} %param.10) | copy-start | bytes 393220

commit v3 on v2

--- a/solution.py
+++ b/solution.py
@@ -25,10 +25,11 @@
 
 
 def sum_x_kernel(got_ref, out_ref):
-    n_z, n_blocks, _, width = out_ref.shape
+    n_here, n_blocks, _, width = out_ref.shape
+    first = pl.program_id(0) * n_here
     for c in range(n_blocks):
-        for z in range(n_z):
-            cols = slice((c * n_z + z) * width, (c * n_z + z + 1) * width)
+        for z in range(n_here):
+            cols = pl.ds(pl.multiple_of((c * NZ * NL + first + z) * width, width), width)
             total = got_ref[0, :, cols].astype(jnp.float32)
             for src in range(1, NX):
                 total += got_ref[src, :, cols].astype(jnp.float32)
@@ -45,8 +46,10 @@
             out_ref[owner_ref[r * n_blocks + c]] = total.astype(out_ref.dtype)
 
 
-def copies_kernel(one_ref, out_ref):
-    out_ref[0] = one_ref[...]
+def halves_kernel(column_ref, low_ref, top_ref):
+    n = low_ref.shape[0]
+    low_ref[...] = column_ref[:n]
+    top_ref[...] = column_ref[n:]
 
 
 def pair_kernel(one_ref, two_ref, out_ref):
@@ -54,10 +57,19 @@
     out_ref[1] = two_ref[...]
 
 
+def root_kernel(pair_ref, swap_ref, root_ref):
+    x_me = lax.axis_index("x")
+    share = pair_ref.shape[1] // NZ
+    for j, (ref, part) in enumerate(((pair_ref, 0), (pair_ref, 1), (swap_ref, 1), (swap_ref, 0))):
+        for z in range(NZ):
+            at = pl.multiple_of((z * NX + lax.bitwise_xor(x_me, j)) * share, share)
+            root_ref[pl.ds(at, share), :] = ref[part, z * share : (z + 1) * share, :]
+
+
 def product_kernel(*refs):
-    pieces_ref = refs[0]
-    (pair_ref, swap_ref, left_root_hbm, left_prev_hbm, right_prev_hbm, left_hbm, right_hbm, update_hbm,
-     g_ref, root_ref, left_root, left_prev, right_prev, gram_ref, left_new, right_new, update, sems) = refs[1:]
+    piece_refs = refs[: 2 * NX]
+    (root_ref, left_root_hbm, left_prev_hbm, right_prev_hbm, left_hbm, right_hbm, update_hbm,
+     g_ref, stack_ref, left_prev, right_prev, pair_ref, both_ref, left_new, right_new, update, sems) = refs[2 * NX :]
     zh = lax.axis_index("zh")
     x_me = lax.axis_index("x")
     d = zh * NX + x_me
@@ -65,7 +77,7 @@
     loads = [
         pltpu.make_async_copy(a, b, sems.at[i])
         for i, (a, b) in enumerate(
-            ((left_root_hbm, left_root), (left_prev_hbm, left_prev), (right_prev_hbm, right_prev))
+            ((left_root_hbm, stack_ref.at[:share]), (left_prev_hbm, left_prev), (right_prev_hbm, right_prev))
         )
     ]
     stores = [
@@ -74,14 +86,16 @@
     ]
     for c in loads:
         c.start()
-    n_piece, high, width = pieces_ref.shape[2:]
+    n_half, n_piece, high, width = piece_refs[0].shape
     n_src = n_piece // NL
     for j in range(NX):
+        x = lax.bitwise_xor(x_me, j)
         for z in range(NZ):
+            ref = piece_refs[2 * j + z // n_half]
             for p in range(n_piece):
-                at = (p % n_src * NX + j) * high
+                at = pl.multiple_of((p % n_src * NX + x) * high, high)
                 to = (z * NL + p // n_src) * width
-                g_ref[at : at + high, to : to + width] = pieces_ref[j, z, p]
+                g_ref[pl.ds(at, high), to : to + width] = ref[z % n_half, p]
     rows = g_ref[pl.ds(pl.multiple_of(d * share, share), share), :]
     g = g_ref[...]
     left_gram = lax.dot_general(rows, g, (((1,), (1,)), ((), ())), preferred_element_type=jnp.float32)
@@ -90,15 +104,12 @@
     left_new[...] = decay_rate * left_prev[...] + (1.0 - decay_rate) * left_gram
     stores[0].start()
     pair = g_ref[:, pl.ds(pl.multiple_of((d // 2) * 2 * share, 2 * share), 2 * share)]
-    gram_ref[...] = lax.dot_general(pair, g, (((0,), (0,)), ((), ())), preferred_element_type=jnp.float32)
-    right_gram = gram_ref[pl.ds(pl.multiple_of(lax.rem(d, 2) * share, share), share), :]
-    right_new[...] = decay_rate * right_prev[...] + (1.0 - decay_rate) * right_gram
+    pair_ref[...] = pair.T
+    stack_ref[share:, :] = pair_ref[pl.ds(pl.multiple_of(lax.rem(d, 2) * share, share), share), :]
+    both_ref[...] = jnp.dot(stack_ref[...], g, preferred_element_type=jnp.float32)
+    right_new[...] = decay_rate * right_prev[...] + (1.0 - decay_rate) * both_ref[share:, :]
     stores[1].start()
-    half = jnp.dot(left_root[...], g, preferred_element_type=jnp.float32).astype(jnp.bfloat16)
-    for j, (ref, part) in enumerate(((pair_ref, 0), (pair_ref, 1), (swap_ref, 1), (swap_ref, 0))):
-        for z in range(NZ):
-            at = pl.multiple_of((z * NX + lax.bitwise_xor(x_me, j)) * share, share)
-            root_ref[pl.ds(at, share), :] = ref[part, z * share : (z + 1) * share, :]
+    half = both_ref[:share, :].astype(jnp.bfloat16)
     update[...] = jnp.dot(half, root_ref[...], preferred_element_type=jnp.float32).astype(update.dtype)
     stores[2].start()
     for c in stores:
@@ -131,8 +142,8 @@
         sum_x_kernel,
         shape((NZ * NL,) + piece, bf16),
         grid=(cut,),
-        in_specs=[pl.BlockSpec((NX, high, cols // cut), lambda i: (0, 0, i))],
-        out_specs=pl.BlockSpec((NZ * NL, n_blocks // cut, high, width), lambda i: (0, i, 0, 0)),
+        in_specs=[pl.BlockSpec((NX, high, cols), lambda i: (0, 0, 0))],
+        out_specs=pl.BlockSpec((NZ * NL // cut,) + piece, lambda i: (i, 0, 0, 0)),
     )(got)
     root_next = lax.ppermute(root_z, "x", swaps[1])
     got = lax.all_to_all(sums, ("zh", "zl"), 0, 0, tiled=True)
@@ -148,32 +159,35 @@
     mine = lax.all_to_all(routed, MP, 0, 0, tiled=True)
     column = lax.all_gather(mine, "zh")
     column, root_swap = lax.optimization_barrier((column, root_swap))
-    copies = call(
-        copies_kernel,
-        shape((NX,) + column.shape, bf16),
-        grid=(NX,),
-        in_specs=[pl.BlockSpec(column.shape, lambda i: (0, 0, 0, 0))],
-        out_specs=pl.BlockSpec((1,) + column.shape, lambda i: (i, 0, 0, 0, 0)),
-    )(column)
-    pieces = lax.all_to_all(copies, "x", 0, 0, tiled=True)
+    low, top = call(
+        halves_kernel, (shape((NZ // 2,) + column.shape[1:], bf16),) * 2, in_specs=[vmem], out_specs=(vmem, vmem)
+    )(column.reshape((NZ, n_mp) + piece[1:]))
+    low_1 = lax.ppermute(low, "x", swaps[1])
+    top_3 = lax.ppermute(top, "x", swaps[3])
+    top_1 = lax.ppermute(top, "x", swaps[1])
+    low_3 = lax.ppermute(low, "x", swaps[3])
+    low_2 = lax.ppermute(low_1, "x", swaps[3])
+    top_2 = lax.ppermute(top_3, "x", swaps[1])
+    pieces = [low, top, low_1, top_1, low_2, top_2, low_3, top_3]
+    root = call(root_kernel, shape((order, order), bf16), in_specs=[vmem, vmem], out_specs=vmem)(root_pair, root_swap)
     left_new, right_new, update = call(
         product_kernel,
         (shape((share, order), f32), shape((share, order), f32), shape((share, order), bf16)),
-        in_specs=[vmem] * 3 + [anywhere] * 3,
+        in_specs=[vmem] * (2 * NX + 1) + [anywhere] * 3,
         out_specs=(anywhere, anywhere, anywhere),
         scratch_shapes=[
             pltpu.VMEM((order, order), bf16),
-            pltpu.VMEM((order, order), bf16),
-            pltpu.VMEM((share, order), bf16),
-            pltpu.VMEM((share, order), f32),
-            pltpu.VMEM((share, order), f32),
+            pltpu.VMEM((2 * share, order), bf16),
+            pltpu.VMEM((share, order), f32),
+            pltpu.VMEM((share, order), f32),
+            pltpu.VMEM((2 * share, order), bf16),
             pltpu.VMEM((2 * share, order), f32),
             pltpu.VMEM((share, order), f32),
             pltpu.VMEM((share, order), f32),
             pltpu.VMEM((share, order), bf16),
             pltpu.SemaphoreType.DMA((6,)),
         ],
-    )(pieces, root_pair, root_swap, left_root[0], left_prev[0], right_prev[0])
+    )(*pieces, root, left_root[0], left_prev[0], right_prev[0])
     return left_new[None], right_new[None], update[None]
 
 

time: 128 us -> 126 us (0.984)
  the two profiles are of different devices: /device:TPU:16 before, /device:TPU:8 now
where the time goes in v3:
time: 126 us; the launch traced here: 125 us
  blocking collectives  55.5 us (44%)
  starting transfers between devices  38.7 us (31%)
  waiting for transfers between devices  24.5 us (19%)
  Pallas kernels  5.76 us (5%)
    all_gather x1, blocking collectives, on_device(): root_z = lax.all_gather(right_root[0], 'zh', tiled=True)  21.8 us
    all_gather x1, blocking collectives, on_device(): column = lax.all_gather(mine, 'zh')  16.8 us
    all_to_all x1, blocking collectives, on_device(): mine = lax.all_to_all(routed, MP, 0, 0, tiled=True)  16.8 us
    ppermute x1, waiting for transfers between devices, on_device(): root_next = lax.ppermute(root_z, 'x', swaps[1])  11.6 us
    all_to_all x1, starting transfers between devices, on_device(): got = lax.all_to_all(sums, ('zh', 'zl'), 0, 0, tiled=True)  10.4 us
    all_to_all x1, waiting for transfers between devices, on_device(): got = lax.all_to_all(part.reshape(NX, high, cols), 'x', 0, 0, tiled=True)  4.49 us
    all_to_all x1, starting transfers between devices, on_device(): got = lax.all_to_all(part.reshape(NX, high, cols), 'x', 0, 0, tiled=True)  4.44 us
    ppermute x1, starting transfers between devices, on_device(): top_3 = lax.ppermute(top, 'x', swaps[3])  4.11 us
  transfers between devices with their start and end apart: 10, of which 6 were waited for; matrix products, arithmetic and copies ran while one was open for 0% of the time, Pallas kernels for 0%

profile of v3, /device:TPU:8, one launch (start us, length us, event | category | flops | bytes accessed | tf_op | source)
XLA Modules:
  0.0 125.3 jit_solution(5283398662689270174)
XLA Ops:
  0.6 4.4 %all-to-all-start = ((bf16[4,16,16384]{2,1,0:T(8,128)(2,1)}), bf16[4,16,16384]{2,1,0:T(8,128)(2,1)S(1)}, u32[]{:S(2)}, u32[]{:S(2)}) async-start(bf16[4,16,16384]{2,1,0:T(8,128)(2,1)} %bitcast.15), calls=%async_computation | async-start | bytes 4194304 | tf_op jit(solution)/shard_map/all_to_all | solution.py:138
  5.1 21.8 %all-gather = bf16[1,256,1024]{2,1,0:T(8,128)(2,1)S(1)} all-gather(bf16[1,64,1024]{2,1,0:T(8,128)(2,1)S(1)} %copy-done.4), channel_id=2, replica_groups=mesh['zh'=4,'x'=4,'zl'=2,'y'=8,'c'=2] {'zh'}, dimensions={1}, use_global_device_ids=true | all-gather | bytes 655360 | tf_op jit(solution)/shard_map/all_gather | solution.py:137
  26.9 4.5 %all-to-all-done.got_ref = bf16[4,16,16384]{2,1,0:T(8,128)(2,1)S(1)} async-done(((bf16[4,16,16384]{2,1,0:T(8,128)(2,1)}), bf16[4,16,16384]{2,1,0:T(8,128)(2,1)S(1)}, u32[]{:S(2)}, u32[]{:S(2)}) %all-to-all-start) | async-done | bytes 2097184 | tf_op jit(solution)/shard_map/all_to_all | solution.py:138
  31.4 1.7 %shard_map.85 = bf16[8,16,16,128]{3,2,1,0:T(8,128)(2,1)} custom-call(bf16[4,16,16384]{2,1,0:T(8,128)(2,1)S(1)} %all-to-all-done.got_ref), custom_call_target="tpu_custom_call" | custom-call | tf_op jit(solution)/shard_map/pallas_call | solution.py:141
  33.1 10.4 %all-to-all-start.1 = ((bf16[8,16,16,128]{3,2,1,0:T(8,128)(2,1)}), bf16[8,16,16,128]{3,2,1,0:T(8,128)(2,1)S(1)}, u32[]{:S(2)}, u32[]{:S(2)}) async-start(bf16[8,16,16,128]{3,2,1,0:T(8,128)(2,1)} %shard_map.85), calls=%async_computation.1 | async-start | bytes 1048576 | tf_op jit(solution)/shard_map/all_to_all | solution.py:149
  43.6 2.5 %collective-permute-start = (bf16[256,1024]{1,0:T(8,128)(2,1)S(1)}, bf16[256,1024]{1,0:T(8,128)(2,1)S(1)}, u32[]{:S(2)}, u32[]{:S(2)}) collective-permute-start(bf16[256,1024]{1,0:T(8,128)(2,1)S(1)} %bitcast.10), channel_id=1, source_target_pairs={{0,32},{32,0},{64,96},{96,64},{1,33},{33,1},{65,97},{97,65},{2,34}... | collective-permute-start | bytes 1572872 | tf_op jit(solution)/shard_map/ppermute | solution.py:148
  46.1 11.6 %collective-permute-done.two_ref = bf16[256,1024]{1,0:T(8,128)(2,1)S(1)} collective-permute-done((bf16[256,1024]{1,0:T(8,128)(2,1)S(1)}, bf16[256,1024]{1,0:T(8,128)(2,1)S(1)}, u32[]{:S(2)}, u32[]{:S(2)}) %collective-permute-start) | collective-permute-done | bytes 524320 | tf_op jit(solution)/shard_map/ppermute | solution.py:148
  57.7 2.2 %all-to-all-done.1.got_ref = bf16[8,16,16,128]{3,2,1,0:T(8,128)(2,1)S(1)} async-done(((bf16[8,16,16,128]{3,2,1,0:T(8,128)(2,1)}), bf16[8,16,16,128]{3,2,1,0:T(8,128)(2,1)S(1)}, u32[]{:S(2)}, u32[]{:S(2)}) %all-to-all-start.1) | async-done | bytes 524320 | tf_op jit(solution)/shard_map/all_to_all | solution.py:149
  59.9 0.1 shard_map.87.pair_ref
  60.0 0.6 shard_map.86
  60.6 3.1 %collective-permute-start.1 = (bf16[2,256,1024]{2,1,0:T(8,128)(2,1)S(1)}, bf16[2,256,1024]{2,1,0:T(8,128)(2,1)S(1)}, u32[]{:S(2)}, u32[]{:S(2)}) collective-permute-start(bf16[2,256,1024]{2,1,0:T(8,128)(2,1)S(1)} %shard_map.87.pair_ref), channel_id=1, source_target_pairs={{0,96},{32,64},{64,32},{96,0},{1,97},{33,65},{65,33},{97,1},{2,98}... | collective-permute-start | bytes 3145736 | tf_op jit(solution)/shard_map/ppermute | solution.py:158
  63.7 16.8 %all_to_all.15 = bf16[32,16,128]{2,1,0:T(8,128)(2,1)S(1)} all-to-all(bf16[32,16,128]{2,1,0:T(8,128)(2,1)S(1)} %shard_map.86), channel_id=1, replica_groups=mesh['zh'=4,'x'=4,'zl'=2,'y'=8,'c'=2] {'zl','y','c'}, dimensions={0} | all-to-all | bytes 262144 | tf_op jit(solution)/shard_map/all_to_all | solution.py:159
  80.5 16.8 %all-gather.1 = bf16[128,16,128]{2,1,0:T(8,128)(2,1)S(1)} all-gather(bf16[32,16,128]{2,1,0:T(8,128)(2,1)S(1)} %all_to_all.15), channel_id=3, replica_groups=mesh['zh'=4,'x'=4,'zl'=2,'y'=8,'c'=2] {'zh'}, dimensions={0}, use_global_device_ids=true | all-gather | bytes 655360 | tf_op jit(solution)/shard_map/all_gather | solution.py:160
  97.4 0.0 collective-permute-done.1.swap_ref
  97.4 1.9 %collective-permute-start.2 = (bf16[2,32,16,128]{3,2,1,0:T(8,128)(2,1)S(1)}, bf16[2,32,16,128]{3,2,1,0:T(8,128)(2,1)S(1)}, u32[]{:S(2)}, u32[]{:S(2)}) collective-permute-start(bf16[2,32,16,128]{3,2,1,0:T(8,128)(2,1)S(1)} %get-tuple-element.25.refs_0_), channel_id=1, source_target_pairs={{0,32},{32,0},{64,96},{96,64},{1,33},{33,1},{65,97},{97,65},{2,34}... | collective-permute-start | bytes 786440 | tf_op jit(solution)/shard_map/ppermute | solution.py:165
  99.3 0.0 copy-start
  99.3 0.0 copy-start.1
  99.3 0.0 copy-start.2
  99.4 4.1 %collective-permute-start.5 = (bf16[2,32,16,128]{3,2,1,0:T(8,128)(2,1)S(1)}, bf16[2,32,16,128]{3,2,1,0:T(8,128)(2,1)S(1)}, u32[]{:S(2)}, u32[]{:S(2)}) collective-permute-start(bf16[2,32,16,128]{3,2,1,0:T(8,128)(2,1)S(1)} %get-tuple-element.26.refs_1_), channel_id=1, source_target_pairs={{0,96},{32,64},{64,32},{96,0},{1,97},{33,65},{65,33},{97,1},{2,98}... | collective-permute-start | bytes 786440 | tf_op jit(solution)/shard_map/ppermute | solution.py:166
  103.5 3.3 %collective-permute-start.3 = (bf16[2,32,16,128]{3,2,1,0:T(8,128)(2,1)S(1)}, bf16[2,32,16,128]{3,2,1,0:T(8,128)(2,1)S(1)}, u32[]{:S(2)}, u32[]{:S(2)}) collective-permute-start(bf16[2,32,16,128]{3,2,1,0:T(8,128)(2,1)S(1)} %get-tuple-element.26.refs_1_), channel_id=1, source_target_pairs={{0,32},{32,0},{64,96},{96,64},{1,33},{33,1},{65,97},{97,65},{2,34}... | collective-permute-start | bytes 786440 | tf_op jit(solution)/shard_map/ppermute | solution.py:167
  106.8 3.1 %collective-permute-start.7 = (bf16[2,32,16,128]{3,2,1,0:T(8,128)(2,1)S(1)}, bf16[2,32,16,128]{3,2,1,0:T(8,128)(2,1)S(1)}, u32[]{:S(2)}, u32[]{:S(2)}) collective-permute-start(bf16[2,32,16,128]{3,2,1,0:T(8,128)(2,1)S(1)} %get-tuple-element.25.refs_0_), channel_id=1, source_target_pairs={{0,96},{32,64},{64,32},{96,0},{1,97},{33,65},{65,33},{97,1},{2,98}... | collective-permute-start | bytes 786440 | tf_op jit(solution)/shard_map/ppermute | solution.py:168
  109.9 0.0 collective-permute-done.2.refs_2_
  109.9 4.0 %collective-permute-start.4 = (bf16[2,32,16,128]{3,2,1,0:T(8,128)(2,1)S(1)}, bf16[2,32,16,128]{3,2,1,0:T(8,128)(2,1)S(1)}, u32[]{:S(2)}, u32[]{:S(2)}) collective-permute-start(bf16[2,32,16,128]{3,2,1,0:T(8,128)(2,1)S(1)} %collective-permute-done.2.refs_2_), channel_id=1, source_target_pairs={{0,96},{32,64},{64,32},{96,0},{1,97},{33,65},{65,33},{97,1},{2,98}... | collective-permute-start | bytes 786440 | tf_op jit(solution)/shard_map/ppermute | solution.py:169
  113.9 0.0 collective-permute-done.5.refs_7_
  113.9 1.9 %collective-permute-start.6 = (bf16[2,32,16,128]{3,2,1,0:T(8,128)(2,1)S(1)}, bf16[2,32,16,128]{3,2,1,0:T(8,128)(2,1)S(1)}, u32[]{:S(2)}, u32[]{:S(2)}) collective-permute-start(bf16[2,32,16,128]{3,2,1,0:T(8,128)(2,1)S(1)} %collective-permute-done.5.refs_7_), channel_id=1, source_target_pairs={{0,32},{32,0},{64,96},{96,64},{1,33},{33,1},{65,97},{97,65},{2,34}... | collective-permute-start | bytes 786440 | tf_op jit(solution)/shard_map/ppermute | solution.py:170
  115.8 0.2 shard_map.89.refs_8_
  116.0 0.0 collective-permute-done.3.refs_3_
  116.0 1.4 %collective-permute-done.7.refs_6_ = bf16[2,32,16,128]{3,2,1,0:T(8,128)(2,1)S(1)} collective-permute-done((bf16[2,32,16,128]{3,2,1,0:T(8,128)(2,1)S(1)}, bf16[2,32,16,128]{3,2,1,0:T(8,128)(2,1)S(1)}, u32[]{:S(2)}, u32[]{:S(2)}) %collective-permute-start.7) | collective-permute-done | bytes 262176 | tf_op jit(solution)/shard_map/ppermute | solution.py:168
  117.4 2.8 %collective-permute-done.4.refs_4_ = bf16[2,32,16,128]{3,2,1,0:T(8,128)(2,1)S(1)} collective-permute-done((bf16[2,32,16,128]{3,2,1,0:T(8,128)(2,1)S(1)}, bf16[2,32,16,128]{3,2,1,0:T(8,128)(2,1)S(1)}, u32[]{:S(2)}, u32[]{:S(2)}) %collective-permute-start.4) | collective-permute-done | bytes 262176 | tf_op jit(solution)/shard_map/ppermute | solution.py:169
  120.2 2.0 %collective-permute-done.6.refs_5_ = bf16[2,32,16,128]{3,2,1,0:T(8,128)(2,1)S(1)} collective-permute-done((bf16[2,32,16,128]{3,2,1,0:T(8,128)(2,1)S(1)}, bf16[2,32,16,128]{3,2,1,0:T(8,128)(2,1)S(1)}, u32[]{:S(2)}, u32[]{:S(2)}) %collective-permute-start.6) | collective-permute-done | bytes 262176 | tf_op jit(solution)/shard_map/ppermute | solution.py:170
  122.2 0.0 copy-done
  122.2 3.2 %shard_map.90 = (f32[64,1024]{1,0:T(8,128)}, f32[64,1024]{1,0:T(8,128)}, bf16[64,1024]{1,0:T(8,128)(2,1)}) custom-call(bf16[2,32,16,128]{3,2,1,0:T(8,128)(2,1)S(1)} %get-tuple-element.25.refs_0_, bf16[2,32,16,128]{3,2,1,0:T(8,128)(2,1)S(1)} %get-tuple-element.26.refs_1_, bf16[2,32,16,128]{3,2,1,0:T(8,128)(2,1)S(1)} %collective-permute-done.2.refs_2_, ...), custom_call_target="tpu_custom_call" | custom-call | tf_op jit(solution)/shard_map/pallas_call | solution.py:173
  (7 shorter events, 0.0 us)
Async XLA Ops:
  0.6 4.4 %copy-start.4 = (bf16[1,64,1024]{2,1,0:T(8,128)(2,1)S(1)}, bf16[1,64,1024]{2,1,0:T(8,128)(2,1)}, u32[]{:S(2)}) copy-start(bf16[1,64,1024]{2,1,0:T(8,128)(2,1)} %param.11) | copy-start | bytes 393220
  0.6 30.8 %all-to-all-start = ((bf16[4,16,16384]{2,1,0:T(8,128)(2,1)}), bf16[4,16,16384]{2,1,0:T(8,128)(2,1)S(1)}, u32[]{:S(2)}, u32[]{:S(2)}) async-start(bf16[4,16,16384]{2,1,0:T(8,128)(2,1)} %bitcast.15), calls=%async_computation | async-start | bytes 4194304 | tf_op jit(solution)/shard_map/all_to_all | solution.py:138
  33.1 26.8 %copy-start.3 = (s32[32]{0:T(128)S(1)}, s32[32]{0:T(128)}, u32[]{:S(2)}) copy-start(s32[32]{0:T(128)} %owner_ref.1) | copy-start | bytes 388
  33.1 26.8 %all-to-all-start.1 = ((bf16[8,16,16,128]{3,2,1,0:T(8,128)(2,1)}), bf16[8,16,16,128]{3,2,1,0:T(8,128)(2,1)S(1)}, u32[]{:S(2)}, u32[]{:S(2)}) async-start(bf16[8,16,16,128]{3,2,1,0:T(8,128)(2,1)} %shard_map.85), calls=%async_computation.1 | async-start | bytes 1048576 | tf_op jit(solution)/shard_map/all_to_all | solution.py:149
  43.6 14.1 %collective-permute-start = (bf16[256,1024]{1,0:T(8,128)(2,1)S(1)}, bf16[256,1024]{1,0:T(8,128)(2,1)S(1)}, u32[]{:S(2)}, u32[]{:S(2)}) collective-permute-start(bf16[256,1024]{1,0:T(8,128)(2,1)S(1)} %bitcast.10), channel_id=1, source_target_pairs={{0,32},{32,0},{64,96},{96,64},{1,33},{33,1},{65,97},{97,65},{2,34}... | collective-permute-start | bytes 1572872 | tf_op jit(solution)/shard_map/ppermute | solution.py:148
  60.6 36.8 %collective-permute-start.1 = (bf16[2,256,1024]{2,1,0:T(8,128)(2,1)S(1)}, bf16[2,256,1024]{2,1,0:T(8,128)(2,1)S(1)}, u32[]{:S(2)}, u32[]{:S(2)}) collective-permute-start(bf16[2,256,1024]{2,1,0:T(8,128)(2,1)S(1)} %shard_map.87.pair_ref), channel_id=1, source_target_pairs={{0,96},{32,64},{64,32},{96,0},{1,97},{33,65},{65,33},{97,1},{2,98}... | collective-permute-start | bytes 3145736 | tf_op jit(solution)/shard_map/ppermute | solution.py:158
  97.4 12.5 %collective-permute-start.2 = (bf16[2,32,16,128]{3,2,1,0:T(8,128)(2,1)S(1)}, bf16[2,32,16,128]{3,2,1,0:T(8,128)(2,1)S(1)}, u32[]{:S(2)}, u32[]{:S(2)}) collective-permute-start(bf16[2,32,16,128]{3,2,1,0:T(8,128)(2,1)S(1)} %get-tuple-element.25.refs_0_), channel_id=1, source_target_pairs={{0,32},{32,0},{64,96},{96,64},{1,33},{33,1},{65,97},{97,65},{2,34}... | collective-permute-start | bytes 786440 | tf_op jit(solution)/shard_map/ppermute | solution.py:165
  99.3 22.8 %copy-start = (f32[1,64,1024]{2,1,0:T(8,128)S(1)}, f32[1,64,1024]{2,1,0:T(8,128)}, u32[]{:S(2)}) copy-start(f32[1,64,1024]{2,1,0:T(8,128)} %param.8) | copy-start | bytes 786436
  99.3 22.8 %copy-start.1 = (f32[1,64,1024]{2,1,0:T(8,128)S(1)}, f32[1,64,1024]{2,1,0:T(8,128)}, u32[]{:S(2)}) copy-start(f32[1,64,1024]{2,1,0:T(8,128)} %param.9) | copy-start | bytes 786436
  99.3 22.8 %copy-start.2 = (bf16[1,64,1024]{2,1,0:T(8,128)(2,1)S(1)}, bf16[1,64,1024]{2,1,0:T(8,128)(2,1)}, u32[]{:S(2)}) copy-start(bf16[1,64,1024]{2,1,0:T(8,128)(2,1)} %param.10) | copy-start | bytes 393220
  99.4 14.5 %collective-permute-start.5 = (bf16[2,32,16,128]{3,2,1,0:T(8,128)(2,1)S(1)}, bf16[2,32,16,128]{3,2,1,0:T(8,128)(2,1)S(1)}, u32[]{:S(2)}, u32[]{:S(2)}) collective-permute-start(bf16[2,32,16,128]{3,2,1,0:T(8,128)(2,1)S(1)} %get-tuple-element.26.refs_1_), channel_id=1, source_target_pairs={{0,96},{32,64},{64,32},{96,0},{1,97},{33,65},{65,33},{97,1},{2,98}... | collective-permute-start | bytes 786440 | tf_op jit(solution)/shard_map/ppermute | solution.py:166
  103.5 12.5 %collective-permute-start.3 = (bf16[2,32,16,128]{3,2,1,0:T(8,128)(2,1)S(1)}, bf16[2,32,16,128]{3,2,1,0:T(8,128)(2,1)S(1)}, u32[]{:S(2)}, u32[]{:S(2)}) collective-permute-start(bf16[2,32,16,128]{3,2,1,0:T(8,128)(2,1)S(1)} %get-tuple-element.26.refs_1_), channel_id=1, source_target_pairs={{0,32},{32,0},{64,96},{96,64},{1,33},{33,1},{65,97},{97,65},{2,34}... | collective-permute-start | bytes 786440 | tf_op jit(solution)/shard_map/ppermute | solution.py:167
  106.8 10.6 %collective-permute-start.7 = (bf16[2,32,16,128]{3,2,1,0:T(8,128)(2,1)S(1)}, bf16[2,32,16,128]{3,2,1,0:T(8,128)(2,1)S(1)}, u32[]{:S(2)}, u32[]{:S(2)}) collective-permute-start(bf16[2,32,16,128]{3,2,1,0:T(8,128)(2,1)S(1)} %get-tuple-element.25.refs_0_), channel_id=1, source_target_pairs={{0,96},{32,64},{64,32},{96,0},{1,97},{33,65},{65,33},{97,1},{2,98}... | collective-permute-start | bytes 786440 | tf_op jit(solution)/shard_map/ppermute | solution.py:168
  109.9 10.3 %collective-permute-start.4 = (bf16[2,32,16,128]{3,2,1,0:T(8,128)(2,1)S(1)}, bf16[2,32,16,128]{3,2,1,0:T(8,128)(2,1)S(1)}, u32[]{:S(2)}, u32[]{:S(2)}) collective-permute-start(bf16[2,32,16,128]{3,2,1,0:T(8,128)(2,1)S(1)} %collective-permute-done.2.refs_2_), channel_id=1, source_target_pairs={{0,96},{32,64},{64,32},{96,0},{1,97},{33,65},{65,33},{97,1},{2,98}... | collective-permute-start | bytes 786440 | tf_op jit(solution)/shard_map/ppermute | solution.py:169
  113.9 8.3 %collective-permute-start.6 = (bf16[2,32,16,128]{3,2,1,0:T(8,128)(2,1)S(1)}, bf16[2,32,16,128]{3,2,1,0:T(8,128)(2,1)S(1)}, u32[]{:S(2)}, u32[]{:S(2)}) collective-permute-start(bf16[2,32,16,128]{3,2,1,0:T(8,128)(2,1)S(1)} %collective-permute-done.5.refs_7_), channel_id=1, source_target_pairs={{0,32},{32,0},{64,96},{96,64},{1,33},{33,1},{65,97},{97,65},{2,34}... | collective-permute-start | bytes 786440 | tf_op jit(solution)/shard_map/ppermute | solution.py:170

commit v4 on v3

--- a/solution.py
+++ b/solution.py
@@ -43,7 +43,9 @@
             total = got_ref[r, c].astype(jnp.float32)
             for src in range(1, NZ):
                 total += got_ref[src * NL + r, c].astype(jnp.float32)
-            out_ref[owner_ref[r * n_blocks + c]] = total.astype(out_ref.dtype)
+            owner = owner_ref[r * n_blocks + c]
+            for z in range(NZ):
+                out_ref[z, owner] = total.astype(out_ref.dtype)
 
 
 def halves_kernel(column_ref, low_ref, top_ref):
@@ -137,7 +139,7 @@
     root_z = lax.all_gather(right_root[0], "zh", tiled=True)
     got = lax.all_to_all(part.reshape(NX, high, cols), "x", 0, 0, tiled=True)
     got, root_z = lax.optimization_barrier((got, root_z))
-    cut = 4
+    cut = 1
     sums = call(
         sum_x_kernel,
         shape((NZ * NL,) + piece, bf16),
@@ -149,19 +151,19 @@
     got = lax.all_to_all(sums, ("zh", "zl"), 0, 0, tiled=True)
     got, root_z, root_next = lax.optimization_barrier((got, root_z, root_next))
     routed = call(
-        route_kernel, shape((n_mp, high, width), bf16), in_specs=[smem, vmem], out_specs=vmem
+        route_kernel, shape((NZ, n_mp, high, width), bf16), in_specs=[smem, vmem], out_specs=vmem
     )(owner, got)
     root_pair = call(
         pair_kernel, shape((2,) + root_z.shape, bf16), in_specs=[vmem, vmem], out_specs=vmem
     )(root_z, root_next)
     routed, root_pair = lax.optimization_barrier((routed, root_pair))
     root_swap = lax.ppermute(root_pair, "x", swaps[3])
-    mine = lax.all_to_all(routed, MP, 0, 0, tiled=True)
-    column = lax.all_gather(mine, "zh")
+    column = lax.all_to_all(routed.reshape((NZ * n_mp,) + piece[1:]), ("zh",) + MP, 0, 0, tiled=True)
+    column = column.reshape((NZ, n_mp) + piece[1:])
     column, root_swap = lax.optimization_barrier((column, root_swap))
     low, top = call(
         halves_kernel, (shape((NZ // 2,) + column.shape[1:], bf16),) * 2, in_specs=[vmem], out_specs=(vmem, vmem)
-    )(column.reshape((NZ, n_mp) + piece[1:]))
+    )(column)
     low_1 = lax.ppermute(low, "x", swaps[1])
     top_3 = lax.ppermute(top, "x", swaps[3])
     top_1 = lax.ppermute(top, "x", swaps[1])

time: 126 us -> 125 us (level)
  the two profiles are of different devices: /device:TPU:8 before, /device:TPU:1 now
where the time goes in v4:
time: 125 us; the launch traced here: 124 us
  blocking collectives  55.6 us (44%)
  starting transfers between devices  41.7 us (33%)
  waiting for transfers between devices  20.9 us (17%)
  Pallas kernels  5.09 us (4%)
    all_to_all x1, blocking collectives, on_device(): lax.all_to_all(routed.reshape((NZ * n_mp,) + piece[1:]), ('zh',) + MP, 0,...  34.8 us
    all_gather x1, blocking collectives, on_device(): root_z = lax.all_gather(right_root[0], 'zh', tiled=True)  20.8 us
    all_to_all x1, starting transfers between devices, on_device(): got = lax.all_to_all(sums, ('zh', 'zl'), 0, 0, tiled=True)  14.8 us
    ppermute x1, waiting for transfers between devices, on_device(): root_next = lax.ppermute(root_z, 'x', swaps[1])  11 us
    ppermute x1, waiting for transfers between devices, on_device(): low_2 = lax.ppermute(low_1, 'x', swaps[3])  5.62 us
    all_to_all x1, starting transfers between devices, on_device(): got = lax.all_to_all(part.reshape(NX, high, cols), 'x', 0, 0, tiled=True)  4.99 us
    ppermute x1, starting transfers between devices, on_device(): top_3 = lax.ppermute(top, 'x', swaps[3])  3.83 us
    ppermute x1, starting transfers between devices, on_device(): low_2 = lax.ppermute(low_1, 'x', swaps[3])  3.7 us
  transfers between devices with their start and end apart: 10, of which 4 were waited for; matrix products, arithmetic and copies ran while one was open for 0% of the time, Pallas kernels for 0%

profile of v4, /device:TPU:1, one launch (start us, length us, event | category | flops | bytes accessed | tf_op | source)
XLA Modules:
  0.0 124.1 jit_solution(14154134590778852887)
XLA Ops:
  0.6 0.0 copy-start.4
  0.6 5.0 %all-to-all-start = ((bf16[4,16,16384]{2,1,0:T(8,128)(2,1)}), bf16[4,16,16384]{2,1,0:T(8,128)(2,1)S(1)}, u32[]{:S(2)}, u32[]{:S(2)}) async-start(bf16[4,16,16384]{2,1,0:T(8,128)(2,1)} %bitcast.17), calls=%async_computation | async-start | bytes 4194304 | tf_op jit(solution)/shard_map/all_to_all | solution.py:140
  5.6 0.0 copy-done.4
  5.6 20.8 %all-gather = bf16[1,256,1024]{2,1,0:T(8,128)(2,1)S(1)} all-gather(bf16[1,64,1024]{2,1,0:T(8,128)(2,1)S(1)} %copy-done.4), channel_id=2, replica_groups=mesh['zh'=4,'x'=4,'zl'=2,'y'=8,'c'=2] {'zh'}, dimensions={1}, use_global_device_ids=true | all-gather | bytes 655360 | tf_op jit(solution)/shard_map/all_gather | solution.py:139
  26.4 0.0 all-to-all-done.got_ref
  26.4 1.1 shard_map.85
  27.4 14.8 %all-to-all-start.1 = ((bf16[8,16,16,128]{3,2,1,0:T(8,128)(2,1)}), bf16[8,16,16,128]{3,2,1,0:T(8,128)(2,1)S(1)}, u32[]{:S(2)}, u32[]{:S(2)}) async-start(bf16[8,16,16,128]{3,2,1,0:T(8,128)(2,1)} %shard_map.85), calls=%async_computation.1 | async-start | bytes 1048576 | tf_op jit(solution)/shard_map/all_to_all | solution.py:151
  42.3 2.2 %collective-permute-start = (bf16[256,1024]{1,0:T(8,128)(2,1)S(1)}, bf16[256,1024]{1,0:T(8,128)(2,1)S(1)}, u32[]{:S(2)}, u32[]{:S(2)}) collective-permute-start(bf16[256,1024]{1,0:T(8,128)(2,1)S(1)} %bitcast.10), channel_id=1, source_target_pairs={{0,32},{32,0},{64,96},{96,64},{1,33},{33,1},{65,97},{97,65},{2,34}... | collective-permute-start | bytes 1572872 | tf_op jit(solution)/shard_map/ppermute | solution.py:150
  44.5 11.0 %collective-permute-done.two_ref = bf16[256,1024]{1,0:T(8,128)(2,1)S(1)} collective-permute-done((bf16[256,1024]{1,0:T(8,128)(2,1)S(1)}, bf16[256,1024]{1,0:T(8,128)(2,1)S(1)}, u32[]{:S(2)}, u32[]{:S(2)}) %collective-permute-start) | collective-permute-done | bytes 524320 | tf_op jit(solution)/shard_map/ppermute | solution.py:150
  55.4 2.4 %all-to-all-done.1.got_ref = bf16[8,16,16,128]{3,2,1,0:T(8,128)(2,1)S(1)} async-done(((bf16[8,16,16,128]{3,2,1,0:T(8,128)(2,1)}), bf16[8,16,16,128]{3,2,1,0:T(8,128)(2,1)S(1)}, u32[]{:S(2)}, u32[]{:S(2)}) %all-to-all-start.1) | async-done | bytes 524320 | tf_op jit(solution)/shard_map/all_to_all | solution.py:151
  57.9 0.1 shard_map.87.pair_ref
  58.0 0.6 shard_map.86
  58.6 2.8 %collective-permute-start.1 = (bf16[2,256,1024]{2,1,0:T(8,128)(2,1)S(1)}, bf16[2,256,1024]{2,1,0:T(8,128)(2,1)S(1)}, u32[]{:S(2)}, u32[]{:S(2)}) collective-permute-start(bf16[2,256,1024]{2,1,0:T(8,128)(2,1)S(1)} %shard_map.87.pair_ref), channel_id=1, source_target_pairs={{0,96},{32,64},{64,32},{96,0},{1,97},{33,65},{65,33},{97,1},{2,98}... | collective-permute-start | bytes 3145736 | tf_op jit(solution)/shard_map/ppermute | solution.py:160
  61.4 34.8 %all_to_all.15 = bf16[128,16,128]{2,1,0:T(8,128)(2,1)S(1)} all-to-all(bf16[128,16,128]{2,1,0:T(8,128)(2,1)S(1)} %bitcast.13), channel_id=1, replica_groups=mesh['zh'=4,'x'=4,'zl'=2,'y'=8,'c'=2] {'zh','zl','y','c'}, dimensions={0} | all-to-all | bytes 1048576 | tf_op jit(solution)/shard_map/all_to_all | solution.py:161
  96.2 0.0 collective-permute-done.1.swap_ref
  96.2 1.9 %collective-permute-start.2 = (bf16[2,32,16,128]{3,2,1,0:T(8,128)(2,1)S(1)}, bf16[2,32,16,128]{3,2,1,0:T(8,128)(2,1)S(1)}, u32[]{:S(2)}, u32[]{:S(2)}) collective-permute-start(bf16[2,32,16,128]{3,2,1,0:T(8,128)(2,1)S(1)} %get-tuple-element.25.refs_0_), channel_id=1, source_target_pairs={{0,32},{32,0},{64,96},{96,64},{1,33},{33,1},{65,97},{97,65},{2,34}... | collective-permute-start | bytes 786440 | tf_op jit(solution)/shard_map/ppermute | solution.py:167
  98.2 0.0 copy-start
  98.2 0.0 copy-start.1
  98.2 0.0 copy-start.2
  98.2 3.8 %collective-permute-start.5 = (bf16[2,32,16,128]{3,2,1,0:T(8,128)(2,1)S(1)}, bf16[2,32,16,128]{3,2,1,0:T(8,128)(2,1)S(1)}, u32[]{:S(2)}, u32[]{:S(2)}) collective-permute-start(bf16[2,32,16,128]{3,2,1,0:T(8,128)(2,1)S(1)} %get-tuple-element.26.refs_1_), channel_id=1, source_target_pairs={{0,96},{32,64},{64,32},{96,0},{1,97},{33,65},{65,33},{97,1},{2,98}... | collective-permute-start | bytes 786440 | tf_op jit(solution)/shard_map/ppermute | solution.py:168
  102.0 2.8 %collective-permute-start.3 = (bf16[2,32,16,128]{3,2,1,0:T(8,128)(2,1)S(1)}, bf16[2,32,16,128]{3,2,1,0:T(8,128)(2,1)S(1)}, u32[]{:S(2)}, u32[]{:S(2)}) collective-permute-start(bf16[2,32,16,128]{3,2,1,0:T(8,128)(2,1)S(1)} %get-tuple-element.26.refs_1_), channel_id=1, source_target_pairs={{0,32},{32,0},{64,96},{96,64},{1,33},{33,1},{65,97},{97,65},{2,34}... | collective-permute-start | bytes 786440 | tf_op jit(solution)/shard_map/ppermute | solution.py:169
  104.8 2.8 %collective-permute-start.7 = (bf16[2,32,16,128]{3,2,1,0:T(8,128)(2,1)S(1)}, bf16[2,32,16,128]{3,2,1,0:T(8,128)(2,1)S(1)}, u32[]{:S(2)}, u32[]{:S(2)}) collective-permute-start(bf16[2,32,16,128]{3,2,1,0:T(8,128)(2,1)S(1)} %get-tuple-element.25.refs_0_), channel_id=1, source_target_pairs={{0,96},{32,64},{64,32},{96,0},{1,97},{33,65},{65,33},{97,1},{2,98}... | collective-permute-start | bytes 786440 | tf_op jit(solution)/shard_map/ppermute | solution.py:170
  107.6 0.0 collective-permute-done.2.refs_2_
  107.6 3.7 %collective-permute-start.4 = (bf16[2,32,16,128]{3,2,1,0:T(8,128)(2,1)S(1)}, bf16[2,32,16,128]{3,2,1,0:T(8,128)(2,1)S(1)}, u32[]{:S(2)}, u32[]{:S(2)}) collective-permute-start(bf16[2,32,16,128]{3,2,1,0:T(8,128)(2,1)S(1)} %collective-permute-done.2.refs_2_), channel_id=1, source_target_pairs={{0,96},{32,64},{64,32},{96,0},{1,97},{33,65},{65,33},{97,1},{2,98}... | collective-permute-start | bytes 786440 | tf_op jit(solution)/shard_map/ppermute | solution.py:171
  111.3 0.0 collective-permute-done.5.refs_7_
  111.3 1.9 %collective-permute-start.6 = (bf16[2,32,16,128]{3,2,1,0:T(8,128)(2,1)S(1)}, bf16[2,32,16,128]{3,2,1,0:T(8,128)(2,1)S(1)}, u32[]{:S(2)}, u32[]{:S(2)}) collective-permute-start(bf16[2,32,16,128]{3,2,1,0:T(8,128)(2,1)S(1)} %collective-permute-done.5.refs_7_), channel_id=1, source_target_pairs={{0,32},{32,0},{64,96},{96,64},{1,33},{33,1},{65,97},{97,65},{2,34}... | collective-permute-start | bytes 786440 | tf_op jit(solution)/shard_map/ppermute | solution.py:172
  113.3 0.2 shard_map.89.refs_8_
  113.4 0.0 collective-permute-done.3.refs_3_
  113.4 1.9 %collective-permute-done.7.refs_6_ = bf16[2,32,16,128]{3,2,1,0:T(8,128)(2,1)S(1)} collective-permute-done((bf16[2,32,16,128]{3,2,1,0:T(8,128)(2,1)S(1)}, bf16[2,32,16,128]{3,2,1,0:T(8,128)(2,1)S(1)}, u32[]{:S(2)}, u32[]{:S(2)}) %collective-permute-start.7) | collective-permute-done | bytes 262176 | tf_op jit(solution)/shard_map/ppermute | solution.py:170
  115.3 5.6 %collective-permute-done.4.refs_4_ = bf16[2,32,16,128]{3,2,1,0:T(8,128)(2,1)S(1)} collective-permute-done((bf16[2,32,16,128]{3,2,1,0:T(8,128)(2,1)S(1)}, bf16[2,32,16,128]{3,2,1,0:T(8,128)(2,1)S(1)}, u32[]{:S(2)}, u32[]{:S(2)}) %collective-permute-start.4) | collective-permute-done | bytes 262176 | tf_op jit(solution)/shard_map/ppermute | solution.py:171
  121.0 0.0 collective-permute-done.6.refs_5_
  121.0 3.2 %shard_map.90 = (f32[64,1024]{1,0:T(8,128)}, f32[64,1024]{1,0:T(8,128)}, bf16[64,1024]{1,0:T(8,128)(2,1)}) custom-call(bf16[2,32,16,128]{3,2,1,0:T(8,128)(2,1)S(1)} %get-tuple-element.25.refs_0_, bf16[2,32,16,128]{3,2,1,0:T(8,128)(2,1)S(1)} %get-tuple-element.26.refs_1_, bf16[2,32,16,128]{3,2,1,0:T(8,128)(2,1)S(1)} %collective-permute-done.2.refs_2_, ...), custom_call_target="tpu_custom_call" | custom-call | tf_op jit(solution)/shard_map/pallas_call | solution.py:175
  (6 shorter events, 0.0 us)
Async XLA Ops:
  0.6 5.0 %copy-start.4 = (bf16[1,64,1024]{2,1,0:T(8,128)(2,1)S(1)}, bf16[1,64,1024]{2,1,0:T(8,128)(2,1)}, u32[]{:S(2)}) copy-start(bf16[1,64,1024]{2,1,0:T(8,128)(2,1)} %param.11) | copy-start | bytes 393220
  0.6 25.7 %all-to-all-start = ((bf16[4,16,16384]{2,1,0:T(8,128)(2,1)}), bf16[4,16,16384]{2,1,0:T(8,128)(2,1)S(1)}, u32[]{:S(2)}, u32[]{:S(2)}) async-start(bf16[4,16,16384]{2,1,0:T(8,128)(2,1)} %bitcast.17), calls=%async_computation | async-start | bytes 4194304 | tf_op jit(solution)/shard_map/all_to_all | solution.py:140
  27.4 30.5 %copy-start.3 = (s32[32]{0:T(128)S(1)}, s32[32]{0:T(128)}, u32[]{:S(2)}) copy-start(s32[32]{0:T(128)} %owner_ref.1) | copy-start | bytes 388
  27.4 30.4 %all-to-all-start.1 = ((bf16[8,16,16,128]{3,2,1,0:T(8,128)(2,1)}), bf16[8,16,16,128]{3,2,1,0:T(8,128)(2,1)S(1)}, u32[]{:S(2)}, u32[]{:S(2)}) async-start(bf16[8,16,16,128]{3,2,1,0:T(8,128)(2,1)} %shard_map.85), calls=%async_computation.1 | async-start | bytes 1048576 | tf_op jit(solution)/shard_map/all_to_all | solution.py:151
  42.3 13.2 %collective-permute-start = (bf16[256,1024]{1,0:T(8,128)(2,1)S(1)}, bf16[256,1024]{1,0:T(8,128)(2,1)S(1)}, u32[]{:S(2)}, u32[]{:S(2)}) collective-permute-start(bf16[256,1024]{1,0:T(8,128)(2,1)S(1)} %bitcast.10), channel_id=1, source_target_pairs={{0,32},{32,0},{64,96},{96,64},{1,33},{33,1},{65,97},{97,65},{2,34}... | collective-permute-start | bytes 1572872 | tf_op jit(solution)/shard_map/ppermute | solution.py:150
  58.6 37.6 %collective-permute-start.1 = (bf16[2,256,1024]{2,1,0:T(8,128)(2,1)S(1)}, bf16[2,256,1024]{2,1,0:T(8,128)(2,1)S(1)}, u32[]{:S(2)}, u32[]{:S(2)}) collective-permute-start(bf16[2,256,1024]{2,1,0:T(8,128)(2,1)S(1)} %shard_map.87.pair_ref), channel_id=1, source_target_pairs={{0,96},{32,64},{64,32},{96,0},{1,97},{33,65},{65,33},{97,1},{2,98}... | collective-permute-start | bytes 3145736 | tf_op jit(solution)/shard_map/ppermute | solution.py:160
  96.2 11.4 %collective-permute-start.2 = (bf16[2,32,16,128]{3,2,1,0:T(8,128)(2,1)S(1)}, bf16[2,32,16,128]{3,2,1,0:T(8,128)(2,1)S(1)}, u32[]{:S(2)}, u32[]{:S(2)}) collective-permute-start(bf16[2,32,16,128]{3,2,1,0:T(8,128)(2,1)S(1)} %get-tuple-element.25.refs_0_), channel_id=1, source_target_pairs={{0,32},{32,0},{64,96},{96,64},{1,33},{33,1},{65,97},{97,65},{2,34}... | collective-permute-start | bytes 786440 | tf_op jit(solution)/shard_map/ppermute | solution.py:167
  98.2 22.8 %copy-start = (f32[1,64,1024]{2,1,0:T(8,128)S(1)}, f32[1,64,1024]{2,1,0:T(8,128)}, u32[]{:S(2)}) copy-start(f32[1,64,1024]{2,1,0:T(8,128)} %param.8) | copy-start | bytes 786436
  98.2 22.8 %copy-start.1 = (f32[1,64,1024]{2,1,0:T(8,128)S(1)}, f32[1,64,1024]{2,1,0:T(8,128)}, u32[]{:S(2)}) copy-start(f32[1,64,1024]{2,1,0:T(8,128)} %param.9) | copy-start | bytes 786436
  98.2 22.8 %copy-start.2 = (bf16[1,64,1024]{2,1,0:T(8,128)(2,1)S(1)}, bf16[1,64,1024]{2,1,0:T(8,128)(2,1)}, u32[]{:S(2)}) copy-start(bf16[1,64,1024]{2,1,0:T(8,128)(2,1)} %param.10) | copy-start | bytes 393220
  98.2 13.1 %collective-permute-start.5 = (bf16[2,32,16,128]{3,2,1,0:T(8,128)(2,1)S(1)}, bf16[2,32,16,128]{3,2,1,0:T(8,128)(2,1)S(1)}, u32[]{:S(2)}, u32[]{:S(2)}) collective-permute-start(bf16[2,32,16,128]{3,2,1,0:T(8,128)(2,1)S(1)} %get-tuple-element.26.refs_1_), channel_id=1, source_target_pairs={{0,96},{32,64},{64,32},{96,0},{1,97},{33,65},{65,33},{97,1},{2,98}... | collective-permute-start | bytes 786440 | tf_op jit(solution)/shard_map/ppermute | solution.py:168
  102.0 11.4 %collective-permute-start.3 = (bf16[2,32,16,128]{3,2,1,0:T(8,128)(2,1)S(1)}, bf16[2,32,16,128]{3,2,1,0:T(8,128)(2,1)S(1)}, u32[]{:S(2)}, u32[]{:S(2)}) collective-permute-start(bf16[2,32,16,128]{3,2,1,0:T(8,128)(2,1)S(1)} %get-tuple-element.26.refs_1_), channel_id=1, source_target_pairs={{0,32},{32,0},{64,96},{96,64},{1,33},{33,1},{65,97},{97,65},{2,34}... | collective-permute-start | bytes 786440 | tf_op jit(solution)/shard_map/ppermute | solution.py:169
  104.8 10.5 %collective-permute-start.7 = (bf16[2,32,16,128]{3,2,1,0:T(8,128)(2,1)S(1)}, bf16[2,32,16,128]{3,2,1,0:T(8,128)(2,1)S(1)}, u32[]{:S(2)}, u32[]{:S(2)}) collective-permute-start(bf16[2,32,16,128]{3,2,1,0:T(8,128)(2,1)S(1)} %get-tuple-element.25.refs_0_), channel_id=1, source_target_pairs={{0,96},{32,64},{64,32},{96,0},{1,97},{33,65},{65,33},{97,1},{2,98}... | collective-permute-start | bytes 786440 | tf_op jit(solution)/shard_map/ppermute | solution.py:170
  107.6 13.3 %collective-permute-start.4 = (bf16[2,32,16,128]{3,2,1,0:T(8,128)(2,1)S(1)}, bf16[2,32,16,128]{3,2,1,0:T(8,128)(2,1)S(1)}, u32[]{:S(2)}, u32[]{:S(2)}) collective-permute-start(bf16[2,32,16,128]{3,2,1,0:T(8,128)(2,1)S(1)} %collective-permute-done.2.refs_2_), channel_id=1, source_target_pairs={{0,96},{32,64},{64,32},{96,0},{1,97},{33,65},{65,33},{97,1},{2,98}... | collective-permute-start | bytes 786440 | tf_op jit(solution)/shard_map/ppermute | solution.py:171
  111.3 9.6 %collective-permute-start.6 = (bf16[2,32,16,128]{3,2,1,0:T(8,128)(2,1)S(1)}, bf16[2,32,16,128]{3,2,1,0:T(8,128)(2,1)S(1)}, u32[]{:S(2)}, u32[]{:S(2)}) collective-permute-start(bf16[2,32,16,128]{3,2,1,0:T(8,128)(2,1)S(1)} %collective-permute-done.5.refs_7_), channel_id=1, source_target_pairs={{0,32},{32,0},{64,96},{96,64},{1,33},{33,1},{65,97},{97,65},{2,34}... | collective-permute-start | bytes 786440 | tf_op jit(solution)/shard_map/ppermute | solution.py:172

commit v5 on v4

--- a/solution.py
+++ b/solution.py
@@ -40,12 +40,12 @@
     n_blocks = got_ref.shape[1]
     for r in range(NL):
         for c in range(n_blocks):
-            total = got_ref[r, c].astype(jnp.float32)
+            total = got_ref[r * NZ, c].astype(jnp.float32)
             for src in range(1, NZ):
-                total += got_ref[src * NL + r, c].astype(jnp.float32)
+                total += got_ref[r * NZ + src, c].astype(jnp.float32)
             owner = owner_ref[r * n_blocks + c]
             for z in range(NZ):
-                out_ref[z, owner] = total.astype(out_ref.dtype)
+                out_ref[owner, z] = total.astype(out_ref.dtype)
 
 
 def halves_kernel(column_ref, low_ref, top_ref):
@@ -88,16 +88,15 @@
     ]
     for c in loads:
         c.start()
-    n_half, n_piece, high, width = piece_refs[0].shape
-    n_src = n_piece // NL
+    n_src, _, high, width = piece_refs[0].shape
     for j in range(NX):
         x = lax.bitwise_xor(x_me, j)
-        for z in range(NZ):
-            ref = piece_refs[2 * j + z // n_half]
-            for p in range(n_piece):
-                at = pl.multiple_of((p % n_src * NX + x) * high, high)
-                to = (z * NL + p // n_src) * width
-                g_ref[pl.ds(at, high), to : to + width] = ref[z % n_half, p]
+        for half in range(NL):
+            for s in range(n_src):
+                at = pl.multiple_of((s * NX + x) * high, high)
+                for z in range(NZ):
+                    to = (half * NZ + z) * width
+                    g_ref[pl.ds(at, high), to : to + width] = piece_refs[2 * j + half][s, z]
     rows = g_ref[pl.ds(pl.multiple_of(d * share, share), share), :]
     g = g_ref[...]
     left_gram = lax.dot_general(rows, g, (((1,), (1,)), ((), ())), preferred_element_type=jnp.float32)
@@ -148,21 +147,21 @@
         out_specs=pl.BlockSpec((NZ * NL // cut,) + piece, lambda i: (i, 0, 0, 0)),
     )(got)
     root_next = lax.ppermute(root_z, "x", swaps[1])
-    got = lax.all_to_all(sums, ("zh", "zl"), 0, 0, tiled=True)
+    got = lax.all_to_all(sums, ("zl", "zh"), 0, 0, tiled=True)
     got, root_z, root_next = lax.optimization_barrier((got, root_z, root_next))
     routed = call(
-        route_kernel, shape((NZ, n_mp, high, width), bf16), in_specs=[smem, vmem], out_specs=vmem
+        route_kernel, shape((n_mp, NZ, high, width), bf16), in_specs=[smem, vmem], out_specs=vmem
     )(owner, got)
     root_pair = call(
         pair_kernel, shape((2,) + root_z.shape, bf16), in_specs=[vmem, vmem], out_specs=vmem
     )(root_z, root_next)
     routed, root_pair = lax.optimization_barrier((routed, root_pair))
     root_swap = lax.ppermute(root_pair, "x", swaps[3])
-    column = lax.all_to_all(routed.reshape((NZ * n_mp,) + piece[1:]), ("zh",) + MP, 0, 0, tiled=True)
-    column = column.reshape((NZ, n_mp) + piece[1:])
+    column = lax.all_to_all(routed.reshape((n_mp * NZ,) + piece[1:]), MP + ("zh",), 0, 0, tiled=True)
+    column = column.reshape((n_mp, NZ) + piece[1:])
     column, root_swap = lax.optimization_barrier((column, root_swap))
     low, top = call(
-        halves_kernel, (shape((NZ // 2,) + column.shape[1:], bf16),) * 2, in_specs=[vmem], out_specs=(vmem, vmem)
+        halves_kernel, (shape((n_mp // 2,) + column.shape[1:], bf16),) * 2, in_specs=[vmem], out_specs=(vmem, vmem)
     )(column)
     low_1 = lax.ppermute(low, "x", swaps[1])
     top_3 = lax.ppermute(top, "x", swaps[3])

time: 125 us -> 124 us (level)
  the two profiles are of different devices: /device:TPU:1 before, /device:TPU:8 now
where the time goes in v5:
time: 124 us; the launch traced here: 123 us
  blocking collectives  54.3 us (44%)
  starting transfers between devices  38.8 us (31%)
  waiting for transfers between devices  24.5 us (20%)
  Pallas kernels  4.94 us (4%)
    all_to_all x1, blocking collectives, on_device(): lax.all_to_all(routed.reshape((n_mp * NZ,) + piece[1:]), MP + ('zh',), 0,...  32.4 us
    all_gather x1, blocking collectives, on_device(): root_z = lax.all_gather(right_root[0], 'zh', tiled=True)  21.8 us
    ppermute x1, waiting for transfers between devices, on_device(): root_next = lax.ppermute(root_z, 'x', swaps[1])  11.6 us
    all_to_all x1, starting transfers between devices, on_device(): got = lax.all_to_all(sums, ('zl', 'zh'), 0, 0, tiled=True)  10.4 us
    ppermute x1, waiting for transfers between devices, on_device(): low_2 = lax.ppermute(low_1, 'x', swaps[3])  5.29 us
    all_to_all x1, waiting for transfers between devices, on_device(): got = lax.all_to_all(part.reshape(NX, high, cols), 'x', 0, 0, tiled=True)  4.49 us
    all_to_all x1, starting transfers between devices, on_device(): got = lax.all_to_all(part.reshape(NX, high, cols), 'x', 0, 0, tiled=True)  4.44 us
    ppermute x1, starting transfers between devices, on_device(): top_3 = lax.ppermute(top, 'x', swaps[3])  4.11 us
  transfers between devices with their start and end apart: 10, of which 4 were waited for; matrix products, arithmetic and copies ran while one was open for 0% of the time, Pallas kernels for 0%

profile of v5, /device:TPU:8, one launch (start us, length us, event | category | flops | bytes accessed | tf_op | source)
XLA Modules:
  0.0 123.3 jit_solution(1934578436594745)
XLA Ops:
  0.6 4.4 %all-to-all-start = ((bf16[4,16,16384]{2,1,0:T(8,128)(2,1)}), bf16[4,16,16384]{2,1,0:T(8,128)(2,1)S(1)}, u32[]{:S(2)}, u32[]{:S(2)}) async-start(bf16[4,16,16384]{2,1,0:T(8,128)(2,1)} %bitcast.17), calls=%async_computation | async-start | bytes 4194304 | tf_op jit(solution)/shard_map/all_to_all | solution.py:139
  5.1 21.8 %all-gather = bf16[1,256,1024]{2,1,0:T(8,128)(2,1)S(1)} all-gather(bf16[1,64,1024]{2,1,0:T(8,128)(2,1)S(1)} %copy-done.4), channel_id=2, replica_groups=mesh['zh'=4,'x'=4,'zl'=2,'y'=8,'c'=2] {'zh'}, dimensions={1}, use_global_device_ids=true | all-gather | bytes 655360 | tf_op jit(solution)/shard_map/all_gather | solution.py:138
  26.9 4.5 %all-to-all-done.got_ref = bf16[4,16,16384]{2,1,0:T(8,128)(2,1)S(1)} async-done(((bf16[4,16,16384]{2,1,0:T(8,128)(2,1)}), bf16[4,16,16384]{2,1,0:T(8,128)(2,1)S(1)}, u32[]{:S(2)}, u32[]{:S(2)}) %all-to-all-start) | async-done | bytes 2097184 | tf_op jit(solution)/shard_map/all_to_all | solution.py:139
  31.4 1.1 shard_map.85
  32.5 10.4 %all-to-all-start.1 = ((bf16[8,16,16,128]{3,2,1,0:T(8,128)(2,1)}), bf16[8,16,16,128]{3,2,1,0:T(8,128)(2,1)S(1)}, u32[]{:S(2)}, u32[]{:S(2)}) async-start(bf16[8,16,16,128]{3,2,1,0:T(8,128)(2,1)} %shard_map.85), calls=%async_computation.1 | async-start | bytes 1048576 | tf_op jit(solution)/shard_map/all_to_all | solution.py:150
  42.9 2.5 %collective-permute-start = (bf16[256,1024]{1,0:T(8,128)(2,1)S(1)}, bf16[256,1024]{1,0:T(8,128)(2,1)S(1)}, u32[]{:S(2)}, u32[]{:S(2)}) collective-permute-start(bf16[256,1024]{1,0:T(8,128)(2,1)S(1)} %bitcast.10), channel_id=1, source_target_pairs={{0,32},{32,0},{64,96},{96,64},{1,33},{33,1},{65,97},{97,65},{2,34}... | collective-permute-start | bytes 1572872 | tf_op jit(solution)/shard_map/ppermute | solution.py:149
  45.4 11.6 %collective-permute-done.two_ref = bf16[256,1024]{1,0:T(8,128)(2,1)S(1)} collective-permute-done((bf16[256,1024]{1,0:T(8,128)(2,1)S(1)}, bf16[256,1024]{1,0:T(8,128)(2,1)S(1)}, u32[]{:S(2)}, u32[]{:S(2)}) %collective-permute-start) | collective-permute-done | bytes 524320 | tf_op jit(solution)/shard_map/ppermute | solution.py:149
  57.0 0.0 all-to-all-done.1.got_ref
  57.0 0.1 shard_map.87.pair_ref
  57.1 0.0 copy-done.3
  57.1 0.6 shard_map.86
  57.7 3.1 %collective-permute-start.1 = (bf16[2,256,1024]{2,1,0:T(8,128)(2,1)S(1)}, bf16[2,256,1024]{2,1,0:T(8,128)(2,1)S(1)}, u32[]{:S(2)}, u32[]{:S(2)}) collective-permute-start(bf16[2,256,1024]{2,1,0:T(8,128)(2,1)S(1)} %shard_map.87.pair_ref), channel_id=1, source_target_pairs={{0,96},{32,64},{64,32},{96,0},{1,97},{33,65},{65,33},{97,1},{2,98}... | collective-permute-start | bytes 3145736 | tf_op jit(solution)/shard_map/ppermute | solution.py:159
  60.8 32.4 %all_to_all.15 = bf16[128,16,128]{2,1,0:T(8,128)(2,1)S(1)} all-to-all(bf16[128,16,128]{2,1,0:T(8,128)(2,1)S(1)} %bitcast.13), channel_id=1, replica_groups=mesh['zh'=4,'x'=4,'zl'=2,'y'=8,'c'=2] {'zl','y','c','zh'}, dimensions={0} | all-to-all | bytes 1048576 | tf_op jit(solution)/shard_map/all_to_all | solution.py:160
  93.2 0.0 collective-permute-done.1.swap_ref
  93.2 1.9 %collective-permute-start.2 = (bf16[16,4,16,128]{3,2,1,0:T(8,128)(2,1)S(1)}, bf16[16,4,16,128]{3,2,1,0:T(8,128)(2,1)S(1)}, u32[]{:S(2)}, u32[]{:S(2)}) collective-permute-start(bf16[16,4,16,128]{3,2,1,0:T(8,128)(2,1)S(1)} %get-tuple-element.25.refs_0_), channel_id=1, source_target_pairs={{0,32},{32,0},{64,96},{96,64},{1,33},{33,1},{65,97},{97,65},{2,34}... | collective-permute-start | bytes 786440 | tf_op jit(solution)/shard_map/ppermute | solution.py:166
  95.2 0.0 copy-start
  95.2 0.0 copy-start.1
  95.2 0.0 copy-start.2
  95.2 4.1 %collective-permute-start.5 = (bf16[16,4,16,128]{3,2,1,0:T(8,128)(2,1)S(1)}, bf16[16,4,16,128]{3,2,1,0:T(8,128)(2,1)S(1)}, u32[]{:S(2)}, u32[]{:S(2)}) collective-permute-start(bf16[16,4,16,128]{3,2,1,0:T(8,128)(2,1)S(1)} %get-tuple-element.26.refs_1_), channel_id=1, source_target_pairs={{0,96},{32,64},{64,32},{96,0},{1,97},{33,65},{65,33},{97,1},{2,98}... | collective-permute-start | bytes 786440 | tf_op jit(solution)/shard_map/ppermute | solution.py:167
  99.3 3.3 %collective-permute-start.3 = (bf16[16,4,16,128]{3,2,1,0:T(8,128)(2,1)S(1)}, bf16[16,4,16,128]{3,2,1,0:T(8,128)(2,1)S(1)}, u32[]{:S(2)}, u32[]{:S(2)}) collective-permute-start(bf16[16,4,16,128]{3,2,1,0:T(8,128)(2,1)S(1)} %get-tuple-element.26.refs_1_), channel_id=1, source_target_pairs={{0,32},{32,0},{64,96},{96,64},{1,33},{33,1},{65,97},{97,65},{2,34}... | collective-permute-start | bytes 786440 | tf_op jit(solution)/shard_map/ppermute | solution.py:168
  102.7 3.1 %collective-permute-start.7 = (bf16[16,4,16,128]{3,2,1,0:T(8,128)(2,1)S(1)}, bf16[16,4,16,128]{3,2,1,0:T(8,128)(2,1)S(1)}, u32[]{:S(2)}, u32[]{:S(2)}) collective-permute-start(bf16[16,4,16,128]{3,2,1,0:T(8,128)(2,1)S(1)} %get-tuple-element.25.refs_0_), channel_id=1, source_target_pairs={{0,96},{32,64},{64,32},{96,0},{1,97},{33,65},{65,33},{97,1},{2,98}... | collective-permute-start | bytes 786440 | tf_op jit(solution)/shard_map/ppermute | solution.py:169
  105.7 0.0 collective-permute-done.2.refs_2_
  105.7 4.0 %collective-permute-start.4 = (bf16[16,4,16,128]{3,2,1,0:T(8,128)(2,1)S(1)}, bf16[16,4,16,128]{3,2,1,0:T(8,128)(2,1)S(1)}, u32[]{:S(2)}, u32[]{:S(2)}) collective-permute-start(bf16[16,4,16,128]{3,2,1,0:T(8,128)(2,1)S(1)} %collective-permute-done.2.refs_2_), channel_id=1, source_target_pairs={{0,96},{32,64},{64,32},{96,0},{1,97},{33,65},{65,33},{97,1},{2,98}... | collective-permute-start | bytes 786440 | tf_op jit(solution)/shard_map/ppermute | solution.py:170
  109.7 0.0 collective-permute-done.5.refs_7_
  109.8 1.9 %collective-permute-start.6 = (bf16[16,4,16,128]{3,2,1,0:T(8,128)(2,1)S(1)}, bf16[16,4,16,128]{3,2,1,0:T(8,128)(2,1)S(1)}, u32[]{:S(2)}, u32[]{:S(2)}) collective-permute-start(bf16[16,4,16,128]{3,2,1,0:T(8,128)(2,1)S(1)} %collective-permute-done.5.refs_7_), channel_id=1, source_target_pairs={{0,32},{32,0},{64,96},{96,64},{1,33},{33,1},{65,97},{97,65},{2,34}... | collective-permute-start | bytes 786440 | tf_op jit(solution)/shard_map/ppermute | solution.py:171
  111.7 0.2 shard_map.89.refs_8_
  111.9 0.0 collective-permute-done.3.refs_3_
  111.9 3.1 %collective-permute-done.7.refs_6_ = bf16[16,4,16,128]{3,2,1,0:T(8,128)(2,1)S(1)} collective-permute-done((bf16[16,4,16,128]{3,2,1,0:T(8,128)(2,1)S(1)}, bf16[16,4,16,128]{3,2,1,0:T(8,128)(2,1)S(1)}, u32[]{:S(2)}, u32[]{:S(2)}) %collective-permute-start.7) | collective-permute-done | bytes 262176 | tf_op jit(solution)/shard_map/ppermute | solution.py:169
  114.9 5.3 %collective-permute-done.4.refs_4_ = bf16[16,4,16,128]{3,2,1,0:T(8,128)(2,1)S(1)} collective-permute-done((bf16[16,4,16,128]{3,2,1,0:T(8,128)(2,1)S(1)}, bf16[16,4,16,128]{3,2,1,0:T(8,128)(2,1)S(1)}, u32[]{:S(2)}, u32[]{:S(2)}) %collective-permute-start.4) | collective-permute-done | bytes 262176 | tf_op jit(solution)/shard_map/ppermute | solution.py:170
  120.2 0.0 collective-permute-done.6.refs_5_
  120.2 0.0 copy-done
  120.2 3.0 %shard_map.90 = (f32[64,1024]{1,0:T(8,128)}, f32[64,1024]{1,0:T(8,128)}, bf16[64,1024]{1,0:T(8,128)(2,1)}) custom-call(bf16[16,4,16,128]{3,2,1,0:T(8,128)(2,1)S(1)} %get-tuple-element.25.refs_0_, bf16[16,4,16,128]{3,2,1,0:T(8,128)(2,1)S(1)} %get-tuple-element.26.refs_1_, bf16[16,4,16,128]{3,2,1,0:T(8,128)(2,1)S(1)} %collective-permute-done.2.refs_2_, ...), custom_call_target="tpu_custom_call" | custom-call | tf_op jit(solution)/shard_map/pallas_call | solution.py:174
  (6 shorter events, 0.0 us)
Async XLA Ops:
  0.6 4.4 %copy-start.4 = (bf16[1,64,1024]{2,1,0:T(8,128)(2,1)S(1)}, bf16[1,64,1024]{2,1,0:T(8,128)(2,1)}, u32[]{:S(2)}) copy-start(bf16[1,64,1024]{2,1,0:T(8,128)(2,1)} %param.11) | copy-start | bytes 393220
  0.6 30.8 %all-to-all-start = ((bf16[4,16,16384]{2,1,0:T(8,128)(2,1)}), bf16[4,16,16384]{2,1,0:T(8,128)(2,1)S(1)}, u32[]{:S(2)}, u32[]{:S(2)}) async-start(bf16[4,16,16384]{2,1,0:T(8,128)(2,1)} %bitcast.17), calls=%async_computation | async-start | bytes 4194304 | tf_op jit(solution)/shard_map/all_to_all | solution.py:139
  32.5 24.6 %copy-start.3 = (s32[32]{0:T(128)S(1)}, s32[32]{0:T(128)}, u32[]{:S(2)}) copy-start(s32[32]{0:T(128)} %owner_ref.1) | copy-start | bytes 388
  32.5 24.5 %all-to-all-start.1 = ((bf16[8,16,16,128]{3,2,1,0:T(8,128)(2,1)}), bf16[8,16,16,128]{3,2,1,0:T(8,128)(2,1)S(1)}, u32[]{:S(2)}, u32[]{:S(2)}) async-start(bf16[8,16,16,128]{3,2,1,0:T(8,128)(2,1)} %shard_map.85), calls=%async_computation.1 | async-start | bytes 1048576 | tf_op jit(solution)/shard_map/all_to_all | solution.py:150
  42.9 14.1 %collective-permute-start = (bf16[256,1024]{1,0:T(8,128)(2,1)S(1)}, bf16[256,1024]{1,0:T(8,128)(2,1)S(1)}, u32[]{:S(2)}, u32[]{:S(2)}) collective-permute-start(bf16[256,1024]{1,0:T(8,128)(2,1)S(1)} %bitcast.10), channel_id=1, source_target_pairs={{0,32},{32,0},{64,96},{96,64},{1,33},{33,1},{65,97},{97,65},{2,34}... | collective-permute-start | bytes 1572872 | tf_op jit(solution)/shard_map/ppermute | solution.py:149
  57.7 35.5 %collective-permute-start.1 = (bf16[2,256,1024]{2,1,0:T(8,128)(2,1)S(1)}, bf16[2,256,1024]{2,1,0:T(8,128)(2,1)S(1)}, u32[]{:S(2)}, u32[]{:S(2)}) collective-permute-start(bf16[2,256,1024]{2,1,0:T(8,128)(2,1)S(1)} %shard_map.87.pair_ref), channel_id=1, source_target_pairs={{0,96},{32,64},{64,32},{96,0},{1,97},{33,65},{65,33},{97,1},{2,98}... | collective-permute-start | bytes 3145736 | tf_op jit(solution)/shard_map/ppermute | solution.py:159
  93.2 12.5 %collective-permute-start.2 = (bf16[16,4,16,128]{3,2,1,0:T(8,128)(2,1)S(1)}, bf16[16,4,16,128]{3,2,1,0:T(8,128)(2,1)S(1)}, u32[]{:S(2)}, u32[]{:S(2)}) collective-permute-start(bf16[16,4,16,128]{3,2,1,0:T(8,128)(2,1)S(1)} %get-tuple-element.25.refs_0_), channel_id=1, source_target_pairs={{0,32},{32,0},{64,96},{96,64},{1,33},{33,1},{65,97},{97,65},{2,34}... | collective-permute-start | bytes 786440 | tf_op jit(solution)/shard_map/ppermute | solution.py:166
  95.2 25.1 %copy-start = (f32[1,64,1024]{2,1,0:T(8,128)S(1)}, f32[1,64,1024]{2,1,0:T(8,128)}, u32[]{:S(2)}) copy-start(f32[1,64,1024]{2,1,0:T(8,128)} %param.8) | copy-start | bytes 786436
  95.2 25.0 %copy-start.1 = (f32[1,64,1024]{2,1,0:T(8,128)S(1)}, f32[1,64,1024]{2,1,0:T(8,128)}, u32[]{:S(2)}) copy-start(f32[1,64,1024]{2,1,0:T(8,128)} %param.9) | copy-start | bytes 786436
  95.2 25.0 %copy-start.2 = (bf16[1,64,1024]{2,1,0:T(8,128)(2,1)S(1)}, bf16[1,64,1024]{2,1,0:T(8,128)(2,1)}, u32[]{:S(2)}) copy-start(bf16[1,64,1024]{2,1,0:T(8,128)(2,1)} %param.10) | copy-start | bytes 393220
  95.2 14.5 %collective-permute-start.5 = (bf16[16,4,16,128]{3,2,1,0:T(8,128)(2,1)S(1)}, bf16[16,4,16,128]{3,2,1,0:T(8,128)(2,1)S(1)}, u32[]{:S(2)}, u32[]{:S(2)}) collective-permute-start(bf16[16,4,16,128]{3,2,1,0:T(8,128)(2,1)S(1)} %get-tuple-element.26.refs_1_), channel_id=1, source_target_pairs={{0,96},{32,64},{64,32},{96,0},{1,97},{33,65},{65,33},{97,1},{2,98}... | collective-permute-start | bytes 786440 | tf_op jit(solution)/shard_map/ppermute | solution.py:167
  99.3 12.5 %collective-permute-start.3 = (bf16[16,4,16,128]{3,2,1,0:T(8,128)(2,1)S(1)}, bf16[16,4,16,128]{3,2,1,0:T(8,128)(2,1)S(1)}, u32[]{:S(2)}, u32[]{:S(2)}) collective-permute-start(bf16[16,4,16,128]{3,2,1,0:T(8,128)(2,1)S(1)} %get-tuple-element.26.refs_1_), channel_id=1, source_target_pairs={{0,32},{32,0},{64,96},{96,64},{1,33},{33,1},{65,97},{97,65},{2,34}... | collective-permute-start | bytes 786440 | tf_op jit(solution)/shard_map/ppermute | solution.py:168
  102.7 12.3 %collective-permute-start.7 = (bf16[16,4,16,128]{3,2,1,0:T(8,128)(2,1)S(1)}, bf16[16,4,16,128]{3,2,1,0:T(8,128)(2,1)S(1)}, u32[]{:S(2)}, u32[]{:S(2)}) collective-permute-start(bf16[16,4,16,128]{3,2,1,0:T(8,128)(2,1)S(1)} %get-tuple-element.25.refs_0_), channel_id=1, source_target_pairs={{0,96},{32,64},{64,32},{96,0},{1,97},{33,65},{65,33},{97,1},{2,98}... | collective-permute-start | bytes 786440 | tf_op jit(solution)/shard_map/ppermute | solution.py:169
  105.7 14.5 %collective-permute-start.4 = (bf16[16,4,16,128]{3,2,1,0:T(8,128)(2,1)S(1)}, bf16[16,4,16,128]{3,2,1,0:T(8,128)(2,1)S(1)}, u32[]{:S(2)}, u32[]{:S(2)}) collective-permute-start(bf16[16,4,16,128]{3,2,1,0:T(8,128)(2,1)S(1)} %collective-permute-done.2.refs_2_), channel_id=1, source_target_pairs={{0,96},{32,64},{64,32},{96,0},{1,97},{33,65},{65,33},{97,1},{2,98}... | collective-permute-start | bytes 786440 | tf_op jit(solution)/shard_map/ppermute | solution.py:170
  109.8 10.5 %collective-permute-start.6 = (bf16[16,4,16,128]{3,2,1,0:T(8,128)(2,1)S(1)}, bf16[16,4,16,128]{3,2,1,0:T(8,128)(2,1)S(1)}, u32[]{:S(2)}, u32[]{:S(2)}) collective-permute-start(bf16[16,4,16,128]{3,2,1,0:T(8,128)(2,1)S(1)} %collective-permute-done.5.refs_7_), channel_id=1, source_target_pairs={{0,32},{32,0},{64,96},{96,64},{1,33},{33,1},{65,97},{97,65},{2,34}... | collective-permute-start | bytes 786440 | tf_op jit(solution)/shard_map/ppermute | solution.py:171

commit v6 on v5

--- a/solution.py
+++ b/solution.py
@@ -48,30 +48,28 @@
                 out_ref[owner, z] = total.astype(out_ref.dtype)
 
 
-def halves_kernel(column_ref, low_ref, top_ref):
-    n = low_ref.shape[0]
-    low_ref[...] = column_ref[:n]
-    top_ref[...] = column_ref[n:]
-
-
-def pair_kernel(one_ref, two_ref, out_ref):
-    out_ref[0] = one_ref[...]
-    out_ref[1] = two_ref[...]
-
-
-def root_kernel(pair_ref, swap_ref, root_ref):
-    x_me = lax.axis_index("x")
-    share = pair_ref.shape[1] // NZ
-    for j, (ref, part) in enumerate(((pair_ref, 0), (pair_ref, 1), (swap_ref, 1), (swap_ref, 0))):
+def halves_kernel(column_ref, rest_ref, low_ref, top_ref):
+    n = column_ref.shape[0] // 2
+    high = column_ref.shape[2]
+    deep = rest_ref.shape[0] // 2
+    for i, ref in enumerate((low_ref, top_ref)):
+        ref[:n] = column_ref[i * n : (i + 1) * n]
+        for u in range(deep // high):
+            ref[n + u // NZ, u % NZ] = rest_ref[i * deep + u * high : i * deep + (u + 1) * high, :]
+
+
+def root_kernel(a_ref, b_ref, root_ref):
+    share = a_ref.shape[1] * 2 // NZ
+    for x in range(NX):
         for z in range(NZ):
-            at = pl.multiple_of((z * NX + lax.bitwise_xor(x_me, j)) * share, share)
-            root_ref[pl.ds(at, share), :] = ref[part, z * share : (z + 1) * share, :]
+            ref, at = (a_ref, z) if z < NZ // 2 else (b_ref, z - NZ // 2)
+            root_ref[(z * NX + x) * share : (z * NX + x + 1) * share, :] = ref[x, at * share : (at + 1) * share, :]
 
 
 def product_kernel(*refs):
     piece_refs = refs[: 2 * NX]
     (root_ref, left_root_hbm, left_prev_hbm, right_prev_hbm, left_hbm, right_hbm, update_hbm,
-     g_ref, stack_ref, left_prev, right_prev, pair_ref, both_ref, left_new, right_new, update, sems) = refs[2 * NX :]
+     g_ref, rest_ref, stack_ref, left_prev, right_prev, pair_ref, both_ref, left_new, right_new, update, sems) = refs[2 * NX :]
     zh = lax.axis_index("zh")
     x_me = lax.axis_index("x")
     d = zh * NX + x_me
@@ -88,7 +86,10 @@
     ]
     for c in loads:
         c.start()
-    n_src, _, high, width = piece_refs[0].shape
+    n_src = g_ref.shape[0] // (NX * piece_refs[0].shape[2])
+    high, width = piece_refs[0].shape[2:]
+    per = share // high
+    main = root_ref.shape[1]
     for j in range(NX):
         x = lax.bitwise_xor(x_me, j)
         for half in range(NL):
@@ -97,6 +98,9 @@
                 for z in range(NZ):
                     to = (half * NZ + z) * width
                     g_ref[pl.ds(at, high), to : to + width] = piece_refs[2 * j + half][s, z]
+            for u in range(NZ // 2 * per):
+                at = pl.multiple_of(((half * NZ // 2 + u // per) * NX + x) * share + u % per * high, high)
+                rest_ref[pl.ds(at, high), :] = piece_refs[2 * j + half][n_src + u // NZ, u % NZ]
     rows = g_ref[pl.ds(pl.multiple_of(d * share, share), share), :]
     g = g_ref[...]
     left_gram = lax.dot_general(rows, g, (((1,), (1,)), ((), ())), preferred_element_type=jnp.float32)
@@ -111,7 +115,8 @@
     right_new[...] = decay_rate * right_prev[...] + (1.0 - decay_rate) * both_ref[share:, :]
     stores[1].start()
     half = both_ref[:share, :].astype(jnp.bfloat16)
-    update[...] = jnp.dot(half, root_ref[...], preferred_element_type=jnp.float32).astype(update.dtype)
+    update[:, :main] = jnp.dot(half, root_ref[...], preferred_element_type=jnp.float32).astype(update.dtype)
+    update[:, main:] = jnp.dot(half, rest_ref[...], preferred_element_type=jnp.float32).astype(update.dtype)
     stores[2].start()
     for c in stores:
         c.wait()
@@ -138,6 +143,8 @@
     root_z = lax.all_gather(right_root[0], "zh", tiled=True)
     got = lax.all_to_all(part.reshape(NX, high, cols), "x", 0, 0, tiled=True)
     got, root_z = lax.optimization_barrier((got, root_z))
+    deep, main = NZ * share // 2, order - width
+    root_a, root_b, root_rest = root_z[:deep, :main], root_z[deep:, :main], root_z[:, main:]
     cut = 1
     sums = call(
         sum_x_kernel,
@@ -146,23 +153,22 @@
         in_specs=[pl.BlockSpec((NX, high, cols), lambda i: (0, 0, 0))],
         out_specs=pl.BlockSpec((NZ * NL // cut,) + piece, lambda i: (i, 0, 0, 0)),
     )(got)
-    root_next = lax.ppermute(root_z, "x", swaps[1])
+    sums, root_a, root_b, root_rest = lax.optimization_barrier((sums, root_a, root_b, root_rest))
+    root_a = lax.all_gather(root_a, "x")
     got = lax.all_to_all(sums, ("zl", "zh"), 0, 0, tiled=True)
-    got, root_z, root_next = lax.optimization_barrier((got, root_z, root_next))
+    got, root_a, root_b = lax.optimization_barrier((got, root_a, root_b))
     routed = call(
         route_kernel, shape((n_mp, NZ, high, width), bf16), in_specs=[smem, vmem], out_specs=vmem
     )(owner, got)
-    root_pair = call(
-        pair_kernel, shape((2,) + root_z.shape, bf16), in_specs=[vmem, vmem], out_specs=vmem
-    )(root_z, root_next)
-    routed, root_pair = lax.optimization_barrier((routed, root_pair))
-    root_swap = lax.ppermute(root_pair, "x", swaps[3])
+    routed, root_b = lax.optimization_barrier((routed, root_b))
+    root_b = lax.all_gather(root_b, "x")
     column = lax.all_to_all(routed.reshape((n_mp * NZ,) + piece[1:]), MP + ("zh",), 0, 0, tiled=True)
     column = column.reshape((n_mp, NZ) + piece[1:])
-    column, root_swap = lax.optimization_barrier((column, root_swap))
+    column, root_b = lax.optimization_barrier((column, root_b))
+    n_half = n_mp // 2 + deep // (NZ * high)
     low, top = call(
-        halves_kernel, (shape((n_mp // 2,) + column.shape[1:], bf16),) * 2, in_specs=[vmem], out_specs=(vmem, vmem)
-    )(column)
+        halves_kernel, (shape((n_half,) + column.shape[1:], bf16),) * 2, in_specs=[vmem] * 2, out_specs=(vmem, vmem)
+    )(column, root_rest)
     low_1 = lax.ppermute(low, "x", swaps[1])
     top_3 = lax.ppermute(top, "x", swaps[3])
     top_1 = lax.ppermute(top, "x", swaps[1])
@@ -170,7 +176,7 @@
     low_2 = lax.ppermute(low_1, "x", swaps[3])
     top_2 = lax.ppermute(top_3, "x", swaps[1])
     pieces = [low, top, low_1, top_1, low_2, top_2, low_3, top_3]
-    root = call(root_kernel, shape((order, order), bf16), in_specs=[vmem, vmem], out_specs=vmem)(root_pair, root_swap)
+    root = call(root_kernel, shape((order, main), bf16), in_specs=[vmem] * 2, out_specs=vmem)(root_a, root_b)
     left_new, right_new, update = call(
         product_kernel,
         (shape((share, order), f32), shape((share, order), f32), shape((share, order), bf16)),
@@ -178,6 +184,7 @@
         out_specs=(anywhere, anywhere, anywhere),
         scratch_shapes=[
             pltpu.VMEM((order, order), bf16),
+            pltpu.VMEM((order, width), bf16),
             pltpu.VMEM((2 * share, order), bf16),
             pltpu.VMEM((share, order), f32),
             pltpu.VMEM((share, order), f32),

time: 124 us -> 123 us (level)
  starting transfers between devices: 38.8 us -> 46.8 us
  waiting for transfers between devices: 24.5 us -> 18.9 us
  blocking collectives: 54.3 us -> 50.4 us
    all_to_all x1 -> x0, blocking collectives: 32.4 us -> none  [on_device(): lax.all_to_all(routed.reshape((n_mp * NZ,) + piece[1:]), MP + ('zh',), 0,...]
    all_gather x0 -> x2, blocking collectives: none -> 28.6 us  [the longest x1 14.3 us: on_device(): root_a = lax.all_gather(root_a, 'x')]
    all_to_all x0 -> x1, starting transfers between devices: none -> 14.3 us  [on_device(): lax.all_to_all(routed.reshape((n_mp * NZ,) + piece[1:]), MP + ('zh',), 0,...]
    ppermute x2 -> x0, waiting for transfers between devices: 11.6 us -> none  [the longest x1 11.6 us: on_device(): root_next = lax.ppermute(root_z, 'x', swaps[1])]
    ppermute x2 -> x0, starting transfers between devices: 5.54 us -> none  [the longest x1 3.08 us: on_device(): root_swap = lax.ppermute(root_pair, 'x', swaps[3])]
    all_to_all x0 -> x1, waiting for transfers between devices: none -> 4.4 us  [on_device(): lax.all_to_all(routed.reshape((n_mp * NZ,) + piece[1:]), MP + ('zh',), 0,...]
  transfers between devices with their start and end apart: 10 -> 9, of which waited for: 4 -> 4; matrix products, arithmetic and copies ran while one was open for 0% -> 0% of each run, Pallas kernels for 0% -> 0%
where the time goes in v6:
time: 123 us
  blocking collectives  50.4 us (41%)
  starting transfers between devices  46.8 us (38%)
  waiting for transfers between devices  18.9 us (15%)
  Pallas kernels  5.75 us (5%)
    all_gather x1, blocking collectives, on_device(): root_z = lax.all_gather(right_root[0], 'zh', tiled=True)  21.8 us
    all_gather x1, blocking collectives, on_device(): root_a = lax.all_gather(root_a, 'x')  14.3 us
    all_to_all x1, starting transfers between devices, on_device(): lax.all_to_all(routed.reshape((n_mp * NZ,) + piece[1:]), MP + ('zh',), 0,...  14.3 us
    all_gather x1, blocking collectives, on_device(): root_b = lax.all_gather(root_b, 'x')  14.2 us
    all_to_all x1, starting transfers between devices, on_device(): got = lax.all_to_all(sums, ('zl', 'zh'), 0, 0, tiled=True)  10.3 us
    ppermute x1, waiting for transfers between devices, on_device(): low_2 = lax.ppermute(low_1, 'x', swaps[3])  6.11 us
    all_to_all x1, waiting for transfers between devices, on_device(): got = lax.all_to_all(part.reshape(NX, high, cols), 'x', 0, 0, tiled=True)  4.49 us
    all_to_all x1, starting transfers between devices, on_device(): got = lax.all_to_all(part.reshape(NX, high, cols), 'x', 0, 0, tiled=True)  4.44 us
  transfers between devices with their start and end apart: 9, of which 4 were waited for; matrix products, arithmetic and copies ran while one was open for 0% of the time, Pallas kernels for 0%

profile of v6, /device:TPU:8, one launch (start us, length us, event | category | flops | bytes accessed | tf_op | source)
XLA Modules:
  0.0 122.7 jit_solution(6703113278225900292)
XLA Ops:
  0.6 0.0 copy-start.4
  0.6 4.4 %all-to-all-start = ((bf16[4,16,16384]{2,1,0:T(8,128)(2,1)}), bf16[4,16,16384]{2,1,0:T(8,128)(2,1)S(1)}, u32[]{:S(2)}, u32[]{:S(2)}) async-start(bf16[4,16,16384]{2,1,0:T(8,128)(2,1)} %bitcast.20), calls=%async_computation | async-start | bytes 4194304 | tf_op jit(solution)/shard_map/all_to_all | solution.py:144
  5.1 0.0 copy-done.4
  5.1 21.8 %all-gather = bf16[1,256,1024]{2,1,0:T(8,128)(2,1)S(1)} all-gather(bf16[1,64,1024]{2,1,0:T(8,128)(2,1)S(1)} %copy-done.4), channel_id=2, replica_groups=mesh['zh'=4,'x'=4,'zl'=2,'y'=8,'c'=2] {'zh'}, dimensions={1}, use_global_device_ids=true | all-gather | bytes 655360 | tf_op jit(solution)/shard_map/all_gather | solution.py:143
  26.9 4.5 %all-to-all-done.got_ref = bf16[4,16,16384]{2,1,0:T(8,128)(2,1)S(1)} async-done(((bf16[4,16,16384]{2,1,0:T(8,128)(2,1)}), bf16[4,16,16384]{2,1,0:T(8,128)(2,1)S(1)}, u32[]{:S(2)}, u32[]{:S(2)}) %all-to-all-start) | async-done | bytes 2097184 | tf_op jit(solution)/shard_map/all_to_all | solution.py:144
  31.5 0.0 copy-start.3
  31.5 1.1 shard_map.85
  32.5 10.3 %all-to-all-start.1 = ((bf16[8,16,16,128]{3,2,1,0:T(8,128)(2,1)}), bf16[8,16,16,128]{3,2,1,0:T(8,128)(2,1)S(1)}, u32[]{:S(2)}, u32[]{:S(2)}) async-start(bf16[8,16,16,128]{3,2,1,0:T(8,128)(2,1)} %shard_map.85), calls=%async_computation.1 | async-start | bytes 1048576 | tf_op jit(solution)/shard_map/all_to_all | solution.py:158
  42.9 14.3 %all-gather.1 = bf16[512,896]{1,0:T(8,128)(2,1)S(1)} all-gather(bf16[128,896]{1,0:T(8,128)(2,1)S(1)} %get-tuple-element.24), channel_id=3, replica_groups=mesh['zh'=4,'x'=4,'zl'=2,'y'=8,'c'=2] {'x'}, dimensions={0}, use_global_device_ids=true | all-gather | bytes 1146880 | tf_op jit(solution)/shard_map/all_gather | solution.py:157
  57.2 0.0 all-to-all-done.1.got_ref
  57.2 0.0 copy-done.3
  57.2 1.4 %shard_map.86 = bf16[32,4,16,128]{3,2,1,0:T(8,128)(2,1)} custom-call(s32[32]{0:T(128)S(1)} %copy-done.3, bf16[8,16,16,128]{3,2,1,0:T(8,128)(2,1)S(1)} %all-to-all-done.1.got_ref), custom_call_target="tpu_custom_call" | custom-call | tf_op jit(solution)/shard_map/pallas_call | solution.py:160
  58.6 14.3 %all-to-all-start.2 = ((bf16[128,16,128]{2,1,0:T(8,128)(2,1)}), bf16[128,16,128]{2,1,0:T(8,128)(2,1)S(1)}, u32[]{:S(2)}, u32[]{:S(2)}) async-start(bf16[128,16,128]{2,1,0:T(8,128)(2,1)} %bitcast.3), calls=%async_computation.2 | async-start | bytes 1048576 | tf_op jit(solution)/shard_map/all_to_all | solution.py:165
  72.9 14.2 %all-gather.2 = bf16[512,896]{1,0:T(8,128)(2,1)S(1)} all-gather(bf16[128,896]{1,0:T(8,128)(2,1)S(1)} %get-tuple-element.29), channel_id=4, replica_groups=mesh['zh'=4,'x'=4,'zl'=2,'y'=8,'c'=2] {'x'}, dimensions={0}, use_global_device_ids=true | all-gather | bytes 1146880 | tf_op jit(solution)/shard_map/all_gather | solution.py:164
  87.1 4.4 %all-to-all-done.2 = bf16[128,16,128]{2,1,0:T(8,128)(2,1)S(1)} async-done(((bf16[128,16,128]{2,1,0:T(8,128)(2,1)}), bf16[128,16,128]{2,1,0:T(8,128)(2,1)S(1)}, u32[]{:S(2)}, u32[]{:S(2)}) %all-to-all-start.2) | async-done | bytes 524320 | tf_op jit(solution)/shard_map/all_to_all | solution.py:165
  91.6 2.4 %collective-permute-start = (bf16[18,4,16,128]{3,2,1,0:T(8,128)(2,1)S(1)}, bf16[18,4,16,128]{3,2,1,0:T(8,128)(2,1)S(1)}, u32[]{:S(2)}, u32[]{:S(2)}) collective-permute-start(bf16[18,4,16,128]{3,2,1,0:T(8,128)(2,1)S(1)} %get-tuple-element.32.refs_0_), channel_id=1, source_target_pairs={{0,32},{32,0},{64,96},{96,64},{1,33},{33,1},{65,97},{97,65},{2,34}... | collective-permute-start | bytes 884744 | tf_op jit(solution)/shard_map/ppermute | solution.py:172
  94.0 3.6 %collective-permute-start.3 = (bf16[18,4,16,128]{3,2,1,0:T(8,128)(2,1)S(1)}, bf16[18,4,16,128]{3,2,1,0:T(8,128)(2,1)S(1)}, u32[]{:S(2)}, u32[]{:S(2)}) collective-permute-start(bf16[18,4,16,128]{3,2,1,0:T(8,128)(2,1)S(1)} %get-tuple-element.33.refs_1_), channel_id=1, source_target_pairs={{0,96},{32,64},{64,32},{96,0},{1,97},{33,65},{65,33},{97,1},{2,98}... | collective-permute-start | bytes 884744 | tf_op jit(solution)/shard_map/ppermute | solution.py:173
  97.6 2.8 %collective-permute-start.1 = (bf16[18,4,16,128]{3,2,1,0:T(8,128)(2,1)S(1)}, bf16[18,4,16,128]{3,2,1,0:T(8,128)(2,1)S(1)}, u32[]{:S(2)}, u32[]{:S(2)}) collective-permute-start(bf16[18,4,16,128]{3,2,1,0:T(8,128)(2,1)S(1)} %get-tuple-element.33.refs_1_), channel_id=1, source_target_pairs={{0,32},{32,0},{64,96},{96,64},{1,33},{33,1},{65,97},{97,65},{2,34}... | collective-permute-start | bytes 884744 | tf_op jit(solution)/shard_map/ppermute | solution.py:174
  100.4 3.6 %collective-permute-start.5 = (bf16[18,4,16,128]{3,2,1,0:T(8,128)(2,1)S(1)}, bf16[18,4,16,128]{3,2,1,0:T(8,128)(2,1)S(1)}, u32[]{:S(2)}, u32[]{:S(2)}) collective-permute-start(bf16[18,4,16,128]{3,2,1,0:T(8,128)(2,1)S(1)} %get-tuple-element.32.refs_0_), channel_id=1, source_target_pairs={{0,96},{32,64},{64,32},{96,0},{1,97},{33,65},{65,33},{97,1},{2,98}... | collective-permute-start | bytes 884744 | tf_op jit(solution)/shard_map/ppermute | solution.py:175
  104.0 0.0 collective-permute-done.refs_2_
  104.0 3.5 %collective-permute-start.2 = (bf16[18,4,16,128]{3,2,1,0:T(8,128)(2,1)S(1)}, bf16[18,4,16,128]{3,2,1,0:T(8,128)(2,1)S(1)}, u32[]{:S(2)}, u32[]{:S(2)}) collective-permute-start(bf16[18,4,16,128]{3,2,1,0:T(8,128)(2,1)S(1)} %collective-permute-done.refs_2_), channel_id=1, source_target_pairs={{0,96},{32,64},{64,32},{96,0},{1,97},{33,65},{65,33},{97,1},{2,98}... | collective-permute-start | bytes 884744 | tf_op jit(solution)/shard_map/ppermute | solution.py:176
  107.5 0.0 collective-permute-done.3.refs_7_
  107.5 1.9 %collective-permute-start.4 = (bf16[18,4,16,128]{3,2,1,0:T(8,128)(2,1)S(1)}, bf16[18,4,16,128]{3,2,1,0:T(8,128)(2,1)S(1)}, u32[]{:S(2)}, u32[]{:S(2)}) collective-permute-start(bf16[18,4,16,128]{3,2,1,0:T(8,128)(2,1)S(1)} %collective-permute-done.3.refs_7_), channel_id=1, source_target_pairs={{0,32},{32,0},{64,96},{96,64},{1,33},{33,1},{65,97},{97,65},{2,34}... | collective-permute-start | bytes 884744 | tf_op jit(solution)/shard_map/ppermute | solution.py:177
  109.5 0.1 shard_map.88.refs_8_
  109.6 0.0 collective-permute-done.1.refs_3_
  109.6 3.9 %collective-permute-done.5.refs_6_ = bf16[18,4,16,128]{3,2,1,0:T(8,128)(2,1)S(1)} collective-permute-done((bf16[18,4,16,128]{3,2,1,0:T(8,128)(2,1)S(1)}, bf16[18,4,16,128]{3,2,1,0:T(8,128)(2,1)S(1)}, u32[]{:S(2)}, u32[]{:S(2)}) %collective-permute-start.5) | collective-permute-done | bytes 294944 | tf_op jit(solution)/shard_map/ppermute | solution.py:175
  113.5 6.1 %collective-permute-done.2.refs_4_ = bf16[18,4,16,128]{3,2,1,0:T(8,128)(2,1)S(1)} collective-permute-done((bf16[18,4,16,128]{3,2,1,0:T(8,128)(2,1)S(1)}, bf16[18,4,16,128]{3,2,1,0:T(8,128)(2,1)S(1)}, u32[]{:S(2)}, u32[]{:S(2)}) %collective-permute-start.2) | collective-permute-done | bytes 294944 | tf_op jit(solution)/shard_map/ppermute | solution.py:176
  119.6 0.0 collective-permute-done.4.refs_5_
  119.6 0.0 copy-done
  119.6 0.0 copy-done.1
  119.6 0.0 copy-done.2
  119.6 3.1 %shard_map.89 = (f32[64,1024]{1,0:T(8,128)}, f32[64,1024]{1,0:T(8,128)}, bf16[64,1024]{1,0:T(8,128)(2,1)}) custom-call(bf16[18,4,16,128]{3,2,1,0:T(8,128)(2,1)S(1)} %get-tuple-element.32.refs_0_, bf16[18,4,16,128]{3,2,1,0:T(8,128)(2,1)S(1)} %get-tuple-element.33.refs_1_, bf16[18,4,16,128]{3,2,1,0:T(8,128)(2,1)S(1)} %collective-permute-done.refs_2_, ...), custom_call_target="tpu_custom_call" | custom-call | tf_op jit(solution)/shard_map/pallas_call | solution.py:180
  (6 shorter events, 0.1 us)
Async XLA Ops:
  0.6 4.4 %copy-start.4 = (bf16[1,64,1024]{2,1,0:T(8,128)(2,1)S(1)}, bf16[1,64,1024]{2,1,0:T(8,128)(2,1)}, u32[]{:S(2)}) copy-start(bf16[1,64,1024]{2,1,0:T(8,128)(2,1)} %param.11) | copy-start | bytes 393220
  0.6 30.8 %all-to-all-start = ((bf16[4,16,16384]{2,1,0:T(8,128)(2,1)}), bf16[4,16,16384]{2,1,0:T(8,128)(2,1)S(1)}, u32[]{:S(2)}, u32[]{:S(2)}) async-start(bf16[4,16,16384]{2,1,0:T(8,128)(2,1)} %bitcast.20), calls=%async_computation | async-start | bytes 4194304 | tf_op jit(solution)/shard_map/all_to_all | solution.py:144
  31.5 25.7 %copy-start.3 = (s32[32]{0:T(128)S(1)}, s32[32]{0:T(128)}, u32[]{:S(2)}) copy-start(s32[32]{0:T(128)} %owner_ref.1) | copy-start | bytes 388
  32.5 24.6 %all-to-all-start.1 = ((bf16[8,16,16,128]{3,2,1,0:T(8,128)(2,1)}), bf16[8,16,16,128]{3,2,1,0:T(8,128)(2,1)S(1)}, u32[]{:S(2)}, u32[]{:S(2)}) async-start(bf16[8,16,16,128]{3,2,1,0:T(8,128)(2,1)} %shard_map.85), calls=%async_computation.1 | async-start | bytes 1048576 | tf_op jit(solution)/shard_map/all_to_all | solution.py:158
  58.6 32.9 %all-to-all-start.2 = ((bf16[128,16,128]{2,1,0:T(8,128)(2,1)}), bf16[128,16,128]{2,1,0:T(8,128)(2,1)S(1)}, u32[]{:S(2)}, u32[]{:S(2)}) async-start(bf16[128,16,128]{2,1,0:T(8,128)(2,1)} %bitcast.3), calls=%async_computation.2 | async-start | bytes 1048576 | tf_op jit(solution)/shard_map/all_to_all | solution.py:165
  91.5 28.1 %copy-start = (f32[1,64,1024]{2,1,0:T(8,128)S(1)}, f32[1,64,1024]{2,1,0:T(8,128)}, u32[]{:S(2)}) copy-start(f32[1,64,1024]{2,1,0:T(8,128)} %param.8) | copy-start | bytes 786436
  91.5 28.1 %copy-start.1 = (f32[1,64,1024]{2,1,0:T(8,128)S(1)}, f32[1,64,1024]{2,1,0:T(8,128)}, u32[]{:S(2)}) copy-start(f32[1,64,1024]{2,1,0:T(8,128)} %param.9) | copy-start | bytes 786436
  91.5 28.1 %copy-start.2 = (bf16[1,64,1024]{2,1,0:T(8,128)(2,1)S(1)}, bf16[1,64,1024]{2,1,0:T(8,128)(2,1)}, u32[]{:S(2)}) copy-start(bf16[1,64,1024]{2,1,0:T(8,128)(2,1)} %param.10) | copy-start | bytes 393220
  91.6 12.5 %collective-permute-start = (bf16[18,4,16,128]{3,2,1,0:T(8,128)(2,1)S(1)}, bf16[18,4,16,128]{3,2,1,0:T(8,128)(2,1)S(1)}, u32[]{:S(2)}, u32[]{:S(2)}) collective-permute-start(bf16[18,4,16,128]{3,2,1,0:T(8,128)(2,1)S(1)} %get-tuple-element.32.refs_0_), channel_id=1, source_target_pairs={{0,32},{32,0},{64,96},{96,64},{1,33},{33,1},{65,97},{97,65},{2,34}... | collective-permute-start | bytes 884744 | tf_op jit(solution)/shard_map/ppermute | solution.py:172
  94.0 13.6 %collective-permute-start.3 = (bf16[18,4,16,128]{3,2,1,0:T(8,128)(2,1)S(1)}, bf16[18,4,16,128]{3,2,1,0:T(8,128)(2,1)S(1)}, u32[]{:S(2)}, u32[]{:S(2)}) collective-permute-start(bf16[18,4,16,128]{3,2,1,0:T(8,128)(2,1)S(1)} %get-tuple-element.33.refs_1_), channel_id=1, source_target_pairs={{0,96},{32,64},{64,32},{96,0},{1,97},{33,65},{65,33},{97,1},{2,98}... | collective-permute-start | bytes 884744 | tf_op jit(solution)/shard_map/ppermute | solution.py:173
  97.6 12.0 %collective-permute-start.1 = (bf16[18,4,16,128]{3,2,1,0:T(8,128)(2,1)S(1)}, bf16[18,4,16,128]{3,2,1,0:T(8,128)(2,1)S(1)}, u32[]{:S(2)}, u32[]{:S(2)}) collective-permute-start(bf16[18,4,16,128]{3,2,1,0:T(8,128)(2,1)S(1)} %get-tuple-element.33.refs_1_), channel_id=1, source_target_pairs={{0,32},{32,0},{64,96},{96,64},{1,33},{33,1},{65,97},{97,65},{2,34}... | collective-permute-start | bytes 884744 | tf_op jit(solution)/shard_map/ppermute | solution.py:174
  100.4 13.1 %collective-permute-start.5 = (bf16[18,4,16,128]{3,2,1,0:T(8,128)(2,1)S(1)}, bf16[18,4,16,128]{3,2,1,0:T(8,128)(2,1)S(1)}, u32[]{:S(2)}, u32[]{:S(2)}) collective-permute-start(bf16[18,4,16,128]{3,2,1,0:T(8,128)(2,1)S(1)} %get-tuple-element.32.refs_0_), channel_id=1, source_target_pairs={{0,96},{32,64},{64,32},{96,0},{1,97},{33,65},{65,33},{97,1},{2,98}... | collective-permute-start | bytes 884744 | tf_op jit(solution)/shard_map/ppermute | solution.py:175
  104.0 15.5 %collective-permute-start.2 = (bf16[18,4,16,128]{3,2,1,0:T(8,128)(2,1)S(1)}, bf16[18,4,16,128]{3,2,1,0:T(8,128)(2,1)S(1)}, u32[]{:S(2)}, u32[]{:S(2)}) collective-permute-start(bf16[18,4,16,128]{3,2,1,0:T(8,128)(2,1)S(1)} %collective-permute-done.refs_2_), channel_id=1, source_target_pairs={{0,96},{32,64},{64,32},{96,0},{1,97},{33,65},{65,33},{97,1},{2,98}... | collective-permute-start | bytes 884744 | tf_op jit(solution)/shard_map/ppermute | solution.py:176
  107.5 12.1 %collective-permute-start.4 = (bf16[18,4,16,128]{3,2,1,0:T(8,128)(2,1)S(1)}, bf16[18,4,16,128]{3,2,1,0:T(8,128)(2,1)S(1)}, u32[]{:S(2)}, u32[]{:S(2)}) collective-permute-start(bf16[18,4,16,128]{3,2,1,0:T(8,128)(2,1)S(1)} %collective-permute-done.3.refs_7_), channel_id=1, source_target_pairs={{0,32},{32,0},{64,96},{96,64},{1,33},{33,1},{65,97},{97,65},{2,34}... | collective-permute-start | bytes 884744 | tf_op jit(solution)/shard_map/ppermute | solution.py:177

commit v7 on v6

--- a/solution.py
+++ b/solution.py
@@ -68,24 +68,16 @@
 
 def product_kernel(*refs):
     piece_refs = refs[: 2 * NX]
-    (root_ref, left_root_hbm, left_prev_hbm, right_prev_hbm, left_hbm, right_hbm, update_hbm,
-     g_ref, rest_ref, stack_ref, left_prev, right_prev, pair_ref, both_ref, left_new, right_new, update, sems) = refs[2 * NX :]
+    (root_ref, left_root_ref, left_prev, right_prev, left_hbm, right_hbm, update_hbm,
+     g_ref, rest_ref, stack_ref, pair_ref, both_ref, left_new, right_new, update, sems) = refs[2 * NX :]
     zh = lax.axis_index("zh")
     x_me = lax.axis_index("x")
     d = zh * NX + x_me
     share = left_prev.shape[0]
-    loads = [
+    stores = [
         pltpu.make_async_copy(a, b, sems.at[i])
-        for i, (a, b) in enumerate(
-            ((left_root_hbm, stack_ref.at[:share]), (left_prev_hbm, left_prev), (right_prev_hbm, right_prev))
-        )
-    ]
-    stores = [
-        pltpu.make_async_copy(a, b, sems.at[3 + i])
         for i, (a, b) in enumerate(((left_new, left_hbm), (right_new, right_hbm), (update, update_hbm)))
     ]
-    for c in loads:
-        c.start()
     n_src = g_ref.shape[0] // (NX * piece_refs[0].shape[2])
     high, width = piece_refs[0].shape[2:]
     per = share // high
@@ -104,12 +96,11 @@
     rows = g_ref[pl.ds(pl.multiple_of(d * share, share), share), :]
     g = g_ref[...]
     left_gram = lax.dot_general(rows, g, (((1,), (1,)), ((), ())), preferred_element_type=jnp.float32)
-    for c in loads:
-        c.wait()
     left_new[...] = decay_rate * left_prev[...] + (1.0 - decay_rate) * left_gram
     stores[0].start()
     pair = g_ref[:, pl.ds(pl.multiple_of((d // 2) * 2 * share, 2 * share), 2 * share)]
     pair_ref[...] = pair.T
+    stack_ref[:share, :] = left_root_ref[...]
     stack_ref[share:, :] = pair_ref[pl.ds(pl.multiple_of(lax.rem(d, 2) * share, share), share), :]
     both_ref[...] = jnp.dot(stack_ref[...], g, preferred_element_type=jnp.float32)
     right_new[...] = decay_rate * right_prev[...] + (1.0 - decay_rate) * both_ref[share:, :]
@@ -180,20 +171,18 @@
     left_new, right_new, update = call(
         product_kernel,
         (shape((share, order), f32), shape((share, order), f32), shape((share, order), bf16)),
-        in_specs=[vmem] * (2 * NX + 1) + [anywhere] * 3,
+        in_specs=[vmem] * (2 * NX + 4),
         out_specs=(anywhere, anywhere, anywhere),
         scratch_shapes=[
             pltpu.VMEM((order, order), bf16),
             pltpu.VMEM((order, width), bf16),
             pltpu.VMEM((2 * share, order), bf16),
-            pltpu.VMEM((share, order), f32),
-            pltpu.VMEM((share, order), f32),
             pltpu.VMEM((2 * share, order), bf16),
             pltpu.VMEM((2 * share, order), f32),
             pltpu.VMEM((share, order), f32),
             pltpu.VMEM((share, order), f32),
             pltpu.VMEM((share, order), bf16),
-            pltpu.SemaphoreType.DMA((6,)),
+            pltpu.SemaphoreType.DMA((3,)),
         ],
     )(*pieces, root, left_root[0], left_prev[0], right_prev[0])
     return left_new[None], right_new[None], update[None]

time: 123 us -> 123 us (level)
  no operation moved by 1% of the time
where the time goes in v7:
time: 123 us; the launch traced here: 122 us
  blocking collectives  50.4 us (41%)
  starting transfers between devices  46.8 us (38%)
  waiting for transfers between devices  18.9 us (15%)
  Pallas kernels  5.18 us (4%)
    all_gather x1, blocking collectives, on_device(): root_z = lax.all_gather(right_root[0], 'zh', tiled=True)  21.8 us
    all_gather x1, blocking collectives, on_device(): root_a = lax.all_gather(root_a, 'x')  14.3 us
    all_to_all x1, starting transfers between devices, on_device(): lax.all_to_all(routed.reshape((n_mp * NZ,) + piece[1:]), MP + ('zh',), 0,...  14.3 us
    all_gather x1, blocking collectives, on_device(): root_b = lax.all_gather(root_b, 'x')  14.2 us
    all_to_all x1, starting transfers between devices, on_device(): got = lax.all_to_all(sums, ('zl', 'zh'), 0, 0, tiled=True)  10.3 us
    ppermute x1, waiting for transfers between devices, on_device(): low_2 = lax.ppermute(low_1, 'x', swaps[3])  6.11 us
    all_to_all x1, waiting for transfers between devices, on_device(): got = lax.all_to_all(part.reshape(NX, high, cols), 'x', 0, 0, tiled=True)  4.49 us
    all_to_all x1, starting transfers between devices, on_device(): got = lax.all_to_all(part.reshape(NX, high, cols), 'x', 0, 0, tiled=True)  4.44 us
  transfers between devices with their start and end apart: 9, of which 4 were waited for; matrix products, arithmetic and copies ran while one was open for 0% of the time, Pallas kernels for 0%

profile of v7, /device:TPU:8, one launch (start us, length us, event | category | flops | bytes accessed | tf_op | source)
XLA Modules:
  0.0 122.1 jit_solution(2419535962034691064)
XLA Ops:
  0.6 0.0 copy-start.4
  0.6 4.4 %all-to-all-start = ((bf16[4,16,16384]{2,1,0:T(8,128)(2,1)}), bf16[4,16,16384]{2,1,0:T(8,128)(2,1)S(1)}, u32[]{:S(2)}, u32[]{:S(2)}) async-start(bf16[4,16,16384]{2,1,0:T(8,128)(2,1)} %bitcast.20), calls=%async_computation | async-start | bytes 4194304 | tf_op jit(solution)/shard_map/all_to_all | solution.py:135
  5.1 0.0 copy-done.4
  5.1 21.8 %all-gather = bf16[1,256,1024]{2,1,0:T(8,128)(2,1)S(1)} all-gather(bf16[1,64,1024]{2,1,0:T(8,128)(2,1)S(1)} %copy-done.4), channel_id=2, replica_groups=mesh['zh'=4,'x'=4,'zl'=2,'y'=8,'c'=2] {'zh'}, dimensions={1}, use_global_device_ids=true | all-gather | bytes 655360 | tf_op jit(solution)/shard_map/all_gather | solution.py:134
  26.9 4.5 %all-to-all-done.got_ref = bf16[4,16,16384]{2,1,0:T(8,128)(2,1)S(1)} async-done(((bf16[4,16,16384]{2,1,0:T(8,128)(2,1)}), bf16[4,16,16384]{2,1,0:T(8,128)(2,1)S(1)}, u32[]{:S(2)}, u32[]{:S(2)}) %all-to-all-start) | async-done | bytes 2097184 | tf_op jit(solution)/shard_map/all_to_all | solution.py:135
  31.5 0.0 copy-start.3
  31.5 1.1 shard_map.85
  32.5 10.3 %all-to-all-start.1 = ((bf16[8,16,16,128]{3,2,1,0:T(8,128)(2,1)}), bf16[8,16,16,128]{3,2,1,0:T(8,128)(2,1)S(1)}, u32[]{:S(2)}, u32[]{:S(2)}) async-start(bf16[8,16,16,128]{3,2,1,0:T(8,128)(2,1)} %shard_map.85), calls=%async_computation.1 | async-start | bytes 1048576 | tf_op jit(solution)/shard_map/all_to_all | solution.py:149
  42.9 14.3 %all-gather.1 = bf16[512,896]{1,0:T(8,128)(2,1)S(1)} all-gather(bf16[128,896]{1,0:T(8,128)(2,1)S(1)} %get-tuple-element.24), channel_id=3, replica_groups=mesh['zh'=4,'x'=4,'zl'=2,'y'=8,'c'=2] {'x'}, dimensions={0}, use_global_device_ids=true | all-gather | bytes 1146880 | tf_op jit(solution)/shard_map/all_gather | solution.py:148
  57.2 0.0 all-to-all-done.1.got_ref
  57.2 0.0 copy-done.3
  57.2 1.4 %shard_map.86 = bf16[32,4,16,128]{3,2,1,0:T(8,128)(2,1)} custom-call(s32[32]{0:T(128)S(1)} %copy-done.3, bf16[8,16,16,128]{3,2,1,0:T(8,128)(2,1)S(1)} %all-to-all-done.1.got_ref), custom_call_target="tpu_custom_call" | custom-call | tf_op jit(solution)/shard_map/pallas_call | solution.py:151
  58.6 14.3 %all-to-all-start.2 = ((bf16[128,16,128]{2,1,0:T(8,128)(2,1)}), bf16[128,16,128]{2,1,0:T(8,128)(2,1)S(1)}, u32[]{:S(2)}, u32[]{:S(2)}) async-start(bf16[128,16,128]{2,1,0:T(8,128)(2,1)} %bitcast.3), calls=%async_computation.2 | async-start | bytes 1048576 | tf_op jit(solution)/shard_map/all_to_all | solution.py:156
  72.9 14.2 %all-gather.2 = bf16[512,896]{1,0:T(8,128)(2,1)S(1)} all-gather(bf16[128,896]{1,0:T(8,128)(2,1)S(1)} %get-tuple-element.29), channel_id=4, replica_groups=mesh['zh'=4,'x'=4,'zl'=2,'y'=8,'c'=2] {'x'}, dimensions={0}, use_global_device_ids=true | all-gather | bytes 1146880 | tf_op jit(solution)/shard_map/all_gather | solution.py:155
  87.1 4.4 %all-to-all-done.2 = bf16[128,16,128]{2,1,0:T(8,128)(2,1)S(1)} async-done(((bf16[128,16,128]{2,1,0:T(8,128)(2,1)}), bf16[128,16,128]{2,1,0:T(8,128)(2,1)S(1)}, u32[]{:S(2)}, u32[]{:S(2)}) %all-to-all-start.2) | async-done | bytes 524320 | tf_op jit(solution)/shard_map/all_to_all | solution.py:156
  91.6 2.4 %collective-permute-start = (bf16[18,4,16,128]{3,2,1,0:T(8,128)(2,1)S(1)}, bf16[18,4,16,128]{3,2,1,0:T(8,128)(2,1)S(1)}, u32[]{:S(2)}, u32[]{:S(2)}) collective-permute-start(bf16[18,4,16,128]{3,2,1,0:T(8,128)(2,1)S(1)} %get-tuple-element.32.refs_0_), channel_id=1, source_target_pairs={{0,32},{32,0},{64,96},{96,64},{1,33},{33,1},{65,97},{97,65},{2,34}... | collective-permute-start | bytes 884744 | tf_op jit(solution)/shard_map/ppermute | solution.py:163
  94.0 3.6 %collective-permute-start.3 = (bf16[18,4,16,128]{3,2,1,0:T(8,128)(2,1)S(1)}, bf16[18,4,16,128]{3,2,1,0:T(8,128)(2,1)S(1)}, u32[]{:S(2)}, u32[]{:S(2)}) collective-permute-start(bf16[18,4,16,128]{3,2,1,0:T(8,128)(2,1)S(1)} %get-tuple-element.33.refs_1_), channel_id=1, source_target_pairs={{0,96},{32,64},{64,32},{96,0},{1,97},{33,65},{65,33},{97,1},{2,98}... | collective-permute-start | bytes 884744 | tf_op jit(solution)/shard_map/ppermute | solution.py:164
  97.6 2.8 %collective-permute-start.1 = (bf16[18,4,16,128]{3,2,1,0:T(8,128)(2,1)S(1)}, bf16[18,4,16,128]{3,2,1,0:T(8,128)(2,1)S(1)}, u32[]{:S(2)}, u32[]{:S(2)}) collective-permute-start(bf16[18,4,16,128]{3,2,1,0:T(8,128)(2,1)S(1)} %get-tuple-element.33.refs_1_), channel_id=1, source_target_pairs={{0,32},{32,0},{64,96},{96,64},{1,33},{33,1},{65,97},{97,65},{2,34}... | collective-permute-start | bytes 884744 | tf_op jit(solution)/shard_map/ppermute | solution.py:165
  100.4 3.6 %collective-permute-start.5 = (bf16[18,4,16,128]{3,2,1,0:T(8,128)(2,1)S(1)}, bf16[18,4,16,128]{3,2,1,0:T(8,128)(2,1)S(1)}, u32[]{:S(2)}, u32[]{:S(2)}) collective-permute-start(bf16[18,4,16,128]{3,2,1,0:T(8,128)(2,1)S(1)} %get-tuple-element.32.refs_0_), channel_id=1, source_target_pairs={{0,96},{32,64},{64,32},{96,0},{1,97},{33,65},{65,33},{97,1},{2,98}... | collective-permute-start | bytes 884744 | tf_op jit(solution)/shard_map/ppermute | solution.py:166
  104.0 0.0 collective-permute-done.refs_2_
  104.0 3.5 %collective-permute-start.2 = (bf16[18,4,16,128]{3,2,1,0:T(8,128)(2,1)S(1)}, bf16[18,4,16,128]{3,2,1,0:T(8,128)(2,1)S(1)}, u32[]{:S(2)}, u32[]{:S(2)}) collective-permute-start(bf16[18,4,16,128]{3,2,1,0:T(8,128)(2,1)S(1)} %collective-permute-done.refs_2_), channel_id=1, source_target_pairs={{0,96},{32,64},{64,32},{96,0},{1,97},{33,65},{65,33},{97,1},{2,98}... | collective-permute-start | bytes 884744 | tf_op jit(solution)/shard_map/ppermute | solution.py:167
  107.5 0.0 collective-permute-done.3.refs_7_
  107.5 1.9 %collective-permute-start.4 = (bf16[18,4,16,128]{3,2,1,0:T(8,128)(2,1)S(1)}, bf16[18,4,16,128]{3,2,1,0:T(8,128)(2,1)S(1)}, u32[]{:S(2)}, u32[]{:S(2)}) collective-permute-start(bf16[18,4,16,128]{3,2,1,0:T(8,128)(2,1)S(1)} %collective-permute-done.3.refs_7_), channel_id=1, source_target_pairs={{0,32},{32,0},{64,96},{96,64},{1,33},{33,1},{65,97},{97,65},{2,34}... | collective-permute-start | bytes 884744 | tf_op jit(solution)/shard_map/ppermute | solution.py:168
  109.5 0.1 shard_map.88.refs_8_
  109.6 0.0 collective-permute-done.1.refs_3_
  109.6 3.9 %collective-permute-done.5.refs_6_ = bf16[18,4,16,128]{3,2,1,0:T(8,128)(2,1)S(1)} collective-permute-done((bf16[18,4,16,128]{3,2,1,0:T(8,128)(2,1)S(1)}, bf16[18,4,16,128]{3,2,1,0:T(8,128)(2,1)S(1)}, u32[]{:S(2)}, u32[]{:S(2)}) %collective-permute-start.5) | collective-permute-done | bytes 294944 | tf_op jit(solution)/shard_map/ppermute | solution.py:166
  113.5 6.1 %collective-permute-done.2.refs_4_ = bf16[18,4,16,128]{3,2,1,0:T(8,128)(2,1)S(1)} collective-permute-done((bf16[18,4,16,128]{3,2,1,0:T(8,128)(2,1)S(1)}, bf16[18,4,16,128]{3,2,1,0:T(8,128)(2,1)S(1)}, u32[]{:S(2)}, u32[]{:S(2)}) %collective-permute-start.2) | collective-permute-done | bytes 294944 | tf_op jit(solution)/shard_map/ppermute | solution.py:167
  119.6 0.0 collective-permute-done.4.refs_5_
  119.6 0.0 copy-done
  119.6 0.0 copy-done.1
  119.6 0.0 copy-done.2
  119.6 2.5 %shard_map.89 = (f32[64,1024]{1,0:T(8,128)}, f32[64,1024]{1,0:T(8,128)}, bf16[64,1024]{1,0:T(8,128)(2,1)}) custom-call(bf16[18,4,16,128]{3,2,1,0:T(8,128)(2,1)S(1)} %get-tuple-element.32.refs_0_, bf16[18,4,16,128]{3,2,1,0:T(8,128)(2,1)S(1)} %get-tuple-element.33.refs_1_, bf16[18,4,16,128]{3,2,1,0:T(8,128)(2,1)S(1)} %collective-permute-done.refs_2_, ...), custom_call_target="tpu_custom_call" | custom-call | tf_op jit(solution)/shard_map/pallas_call | solution.py:171
  (6 shorter events, 0.1 us)
Async XLA Ops:
  0.6 4.4 %copy-start.4 = (bf16[1,64,1024]{2,1,0:T(8,128)(2,1)S(1)}, bf16[1,64,1024]{2,1,0:T(8,128)(2,1)}, u32[]{:S(2)}) copy-start(bf16[1,64,1024]{2,1,0:T(8,128)(2,1)} %param.11) | copy-start | bytes 393220
  0.6 30.8 %all-to-all-start = ((bf16[4,16,16384]{2,1,0:T(8,128)(2,1)}), bf16[4,16,16384]{2,1,0:T(8,128)(2,1)S(1)}, u32[]{:S(2)}, u32[]{:S(2)}) async-start(bf16[4,16,16384]{2,1,0:T(8,128)(2,1)} %bitcast.20), calls=%async_computation | async-start | bytes 4194304 | tf_op jit(solution)/shard_map/all_to_all | solution.py:135
  31.5 25.7 %copy-start.3 = (s32[32]{0:T(128)S(1)}, s32[32]{0:T(128)}, u32[]{:S(2)}) copy-start(s32[32]{0:T(128)} %owner_ref.1) | copy-start | bytes 388
  32.5 24.6 %all-to-all-start.1 = ((bf16[8,16,16,128]{3,2,1,0:T(8,128)(2,1)}), bf16[8,16,16,128]{3,2,1,0:T(8,128)(2,1)S(1)}, u32[]{:S(2)}, u32[]{:S(2)}) async-start(bf16[8,16,16,128]{3,2,1,0:T(8,128)(2,1)} %shard_map.85), calls=%async_computation.1 | async-start | bytes 1048576 | tf_op jit(solution)/shard_map/all_to_all | solution.py:149
  58.6 32.9 %all-to-all-start.2 = ((bf16[128,16,128]{2,1,0:T(8,128)(2,1)}), bf16[128,16,128]{2,1,0:T(8,128)(2,1)S(1)}, u32[]{:S(2)}, u32[]{:S(2)}) async-start(bf16[128,16,128]{2,1,0:T(8,128)(2,1)} %bitcast.3), calls=%async_computation.2 | async-start | bytes 1048576 | tf_op jit(solution)/shard_map/all_to_all | solution.py:156
  91.5 28.1 %copy-start = (f32[1,64,1024]{2,1,0:T(8,128)S(1)}, f32[1,64,1024]{2,1,0:T(8,128)}, u32[]{:S(2)}) copy-start(f32[1,64,1024]{2,1,0:T(8,128)} %param.8) | copy-start | bytes 786436
  91.5 28.1 %copy-start.1 = (f32[1,64,1024]{2,1,0:T(8,128)S(1)}, f32[1,64,1024]{2,1,0:T(8,128)}, u32[]{:S(2)}) copy-start(f32[1,64,1024]{2,1,0:T(8,128)} %param.9) | copy-start | bytes 786436
  91.5 28.1 %copy-start.2 = (bf16[1,64,1024]{2,1,0:T(8,128)(2,1)S(1)}, bf16[1,64,1024]{2,1,0:T(8,128)(2,1)}, u32[]{:S(2)}) copy-start(bf16[1,64,1024]{2,1,0:T(8,128)(2,1)} %param.10) | copy-start | bytes 393220
  91.6 12.5 %collective-permute-start = (bf16[18,4,16,128]{3,2,1,0:T(8,128)(2,1)S(1)}, bf16[18,4,16,128]{3,2,1,0:T(8,128)(2,1)S(1)}, u32[]{:S(2)}, u32[]{:S(2)}) collective-permute-start(bf16[18,4,16,128]{3,2,1,0:T(8,128)(2,1)S(1)} %get-tuple-element.32.refs_0_), channel_id=1, source_target_pairs={{0,32},{32,0},{64,96},{96,64},{1,33},{33,1},{65,97},{97,65},{2,34}... | collective-permute-start | bytes 884744 | tf_op jit(solution)/shard_map/ppermute | solution.py:163
  94.0 13.6 %collective-permute-start.3 = (bf16[18,4,16,128]{3,2,1,0:T(8,128)(2,1)S(1)}, bf16[18,4,16,128]{3,2,1,0:T(8,128)(2,1)S(1)}, u32[]{:S(2)}, u32[]{:S(2)}) collective-permute-start(bf16[18,4,16,128]{3,2,1,0:T(8,128)(2,1)S(1)} %get-tuple-element.33.refs_1_), channel_id=1, source_target_pairs={{0,96},{32,64},{64,32},{96,0},{1,97},{33,65},{65,33},{97,1},{2,98}... | collective-permute-start | bytes 884744 | tf_op jit(solution)/shard_map/ppermute | solution.py:164
  97.6 12.0 %collective-permute-start.1 = (bf16[18,4,16,128]{3,2,1,0:T(8,128)(2,1)S(1)}, bf16[18,4,16,128]{3,2,1,0:T(8,128)(2,1)S(1)}, u32[]{:S(2)}, u32[]{:S(2)}) collective-permute-start(bf16[18,4,16,128]{3,2,1,0:T(8,128)(2,1)S(1)} %get-tuple-element.33.refs_1_), channel_id=1, source_target_pairs={{0,32},{32,0},{64,96},{96,64},{1,33},{33,1},{65,97},{97,65},{2,34}... | collective-permute-start | bytes 884744 | tf_op jit(solution)/shard_map/ppermute | solution.py:165
  100.4 13.1 %collective-permute-start.5 = (bf16[18,4,16,128]{3,2,1,0:T(8,128)(2,1)S(1)}, bf16[18,4,16,128]{3,2,1,0:T(8,128)(2,1)S(1)}, u32[]{:S(2)}, u32[]{:S(2)}) collective-permute-start(bf16[18,4,16,128]{3,2,1,0:T(8,128)(2,1)S(1)} %get-tuple-element.32.refs_0_), channel_id=1, source_target_pairs={{0,96},{32,64},{64,32},{96,0},{1,97},{33,65},{65,33},{97,1},{2,98}... | collective-permute-start | bytes 884744 | tf_op jit(solution)/shard_map/ppermute | solution.py:166
  104.0 15.5 %collective-permute-start.2 = (bf16[18,4,16,128]{3,2,1,0:T(8,128)(2,1)S(1)}, bf16[18,4,16,128]{3,2,1,0:T(8,128)(2,1)S(1)}, u32[]{:S(2)}, u32[]{:S(2)}) collective-permute-start(bf16[18,4,16,128]{3,2,1,0:T(8,128)(2,1)S(1)} %collective-permute-done.refs_2_), channel_id=1, source_target_pairs={{0,96},{32,64},{64,32},{96,0},{1,97},{33,65},{65,33},{97,1},{2,98}... | collective-permute-start | bytes 884744 | tf_op jit(solution)/shard_map/ppermute | solution.py:167
  107.5 12.1 %collective-permute-start.4 = (bf16[18,4,16,128]{3,2,1,0:T(8,128)(2,1)S(1)}, bf16[18,4,16,128]{3,2,1,0:T(8,128)(2,1)S(1)}, u32[]{:S(2)}, u32[]{:S(2)}) collective-permute-start(bf16[18,4,16,128]{3,2,1,0:T(8,128)(2,1)S(1)} %collective-permute-done.3.refs_7_), channel_id=1, source_target_pairs={{0,32},{32,0},{64,96},{96,64},{1,33},{33,1},{65,97},{97,65},{2,34}... | collective-permute-start | bytes 884744 | tf_op jit(solution)/shard_map/ppermute | solution.py:168

commit v8 on v7

--- a/solution.py
+++ b/solution.py
@@ -93,11 +93,7 @@
             for u in range(NZ // 2 * per):
                 at = pl.multiple_of(((half * NZ // 2 + u // per) * NX + x) * share + u % per * high, high)
                 rest_ref[pl.ds(at, high), :] = piece_refs[2 * j + half][n_src + u // NZ, u % NZ]
-    rows = g_ref[pl.ds(pl.multiple_of(d * share, share), share), :]
     g = g_ref[...]
-    left_gram = lax.dot_general(rows, g, (((1,), (1,)), ((), ())), preferred_element_type=jnp.float32)
-    left_new[...] = decay_rate * left_prev[...] + (1.0 - decay_rate) * left_gram
-    stores[0].start()
     pair = g_ref[:, pl.ds(pl.multiple_of((d // 2) * 2 * share, 2 * share), 2 * share)]
     pair_ref[...] = pair.T
     stack_ref[:share, :] = left_root_ref[...]
@@ -105,6 +101,10 @@
     both_ref[...] = jnp.dot(stack_ref[...], g, preferred_element_type=jnp.float32)
     right_new[...] = decay_rate * right_prev[...] + (1.0 - decay_rate) * both_ref[share:, :]
     stores[1].start()
+    rows = g_ref[pl.ds(pl.multiple_of(d * share, share), share), :]
+    left_gram = lax.dot_general(rows, g, (((1,), (1,)), ((), ())), preferred_element_type=jnp.float32)
+    left_new[...] = decay_rate * left_prev[...] + (1.0 - decay_rate) * left_gram
+    stores[0].start()
     half = both_ref[:share, :].astype(jnp.bfloat16)
     update[:, :main] = jnp.dot(half, root_ref[...], preferred_element_type=jnp.float32).astype(update.dtype)
     update[:, main:] = jnp.dot(half, rest_ref[...], preferred_element_type=jnp.float32).astype(update.dtype)

time: 123 us -> 123 us (level)
  no operation moved by 1% of the time
where the time goes in v8:
time: 123 us; the launch traced here: 122 us
  blocking collectives  50.4 us (41%)
  starting transfers between devices  46.8 us (38%)
  waiting for transfers between devices  18.9 us (15%)
  Pallas kernels  5.25 us (4%)
    all_gather x1, blocking collectives, on_device(): root_z = lax.all_gather(right_root[0], 'zh', tiled=True)  21.8 us
    all_gather x1, blocking collectives, on_device(): root_a = lax.all_gather(root_a, 'x')  14.3 us
    all_to_all x1, starting transfers between devices, on_device(): lax.all_to_all(routed.reshape((n_mp * NZ,) + piece[1:]), MP + ('zh',), 0,...  14.3 us
    all_gather x1, blocking collectives, on_device(): root_b = lax.all_gather(root_b, 'x')  14.2 us
    all_to_all x1, starting transfers between devices, on_device(): got = lax.all_to_all(sums, ('zl', 'zh'), 0, 0, tiled=True)  10.3 us
    ppermute x1, waiting for transfers between devices, on_device(): low_2 = lax.ppermute(low_1, 'x', swaps[3])  6.11 us
    all_to_all x1, waiting for transfers between devices, on_device(): got = lax.all_to_all(part.reshape(NX, high, cols), 'x', 0, 0, tiled=True)  4.49 us
    all_to_all x1, starting transfers between devices, on_device(): got = lax.all_to_all(part.reshape(NX, high, cols), 'x', 0, 0, tiled=True)  4.44 us
  transfers between devices with their start and end apart: 9, of which 4 were waited for; matrix products, arithmetic and copies ran while one was open for 0% of the time, Pallas kernels for 0%

profile of v8, /device:TPU:8, one launch (start us, length us, event | category | flops | bytes accessed | tf_op | source)
XLA Modules:
  0.0 122.2 jit_solution(7296022388273165532)
XLA Ops:
  0.6 0.0 copy-start.4
  0.6 4.4 %all-to-all-start = ((bf16[4,16,16384]{2,1,0:T(8,128)(2,1)}), bf16[4,16,16384]{2,1,0:T(8,128)(2,1)S(1)}, u32[]{:S(2)}, u32[]{:S(2)}) async-start(bf16[4,16,16384]{2,1,0:T(8,128)(2,1)} %bitcast.20), calls=%async_computation | async-start | bytes 4194304 | tf_op jit(solution)/shard_map/all_to_all | solution.py:135
  5.1 0.0 copy-done.4
  5.1 21.8 %all-gather = bf16[1,256,1024]{2,1,0:T(8,128)(2,1)S(1)} all-gather(bf16[1,64,1024]{2,1,0:T(8,128)(2,1)S(1)} %copy-done.4), channel_id=2, replica_groups=mesh['zh'=4,'x'=4,'zl'=2,'y'=8,'c'=2] {'zh'}, dimensions={1}, use_global_device_ids=true | all-gather | bytes 655360 | tf_op jit(solution)/shard_map/all_gather | solution.py:134
  26.9 4.5 %all-to-all-done.got_ref = bf16[4,16,16384]{2,1,0:T(8,128)(2,1)S(1)} async-done(((bf16[4,16,16384]{2,1,0:T(8,128)(2,1)}), bf16[4,16,16384]{2,1,0:T(8,128)(2,1)S(1)}, u32[]{:S(2)}, u32[]{:S(2)}) %all-to-all-start) | async-done | bytes 2097184 | tf_op jit(solution)/shard_map/all_to_all | solution.py:135
  31.5 0.0 copy-start.3
  31.5 1.1 shard_map.85
  32.5 10.3 %all-to-all-start.1 = ((bf16[8,16,16,128]{3,2,1,0:T(8,128)(2,1)}), bf16[8,16,16,128]{3,2,1,0:T(8,128)(2,1)S(1)}, u32[]{:S(2)}, u32[]{:S(2)}) async-start(bf16[8,16,16,128]{3,2,1,0:T(8,128)(2,1)} %shard_map.85), calls=%async_computation.1 | async-start | bytes 1048576 | tf_op jit(solution)/shard_map/all_to_all | solution.py:149
  42.9 14.3 %all-gather.1 = bf16[512,896]{1,0:T(8,128)(2,1)S(1)} all-gather(bf16[128,896]{1,0:T(8,128)(2,1)S(1)} %get-tuple-element.24), channel_id=3, replica_groups=mesh['zh'=4,'x'=4,'zl'=2,'y'=8,'c'=2] {'x'}, dimensions={0}, use_global_device_ids=true | all-gather | bytes 1146880 | tf_op jit(solution)/shard_map/all_gather | solution.py:148
  57.2 0.0 all-to-all-done.1.got_ref
  57.2 0.0 copy-done.3
  57.2 1.4 %shard_map.86 = bf16[32,4,16,128]{3,2,1,0:T(8,128)(2,1)} custom-call(s32[32]{0:T(128)S(1)} %copy-done.3, bf16[8,16,16,128]{3,2,1,0:T(8,128)(2,1)S(1)} %all-to-all-done.1.got_ref), custom_call_target="tpu_custom_call" | custom-call | tf_op jit(solution)/shard_map/pallas_call | solution.py:151
  58.6 14.3 %all-to-all-start.2 = ((bf16[128,16,128]{2,1,0:T(8,128)(2,1)}), bf16[128,16,128]{2,1,0:T(8,128)(2,1)S(1)}, u32[]{:S(2)}, u32[]{:S(2)}) async-start(bf16[128,16,128]{2,1,0:T(8,128)(2,1)} %bitcast.3), calls=%async_computation.2 | async-start | bytes 1048576 | tf_op jit(solution)/shard_map/all_to_all | solution.py:156
  72.9 14.2 %all-gather.2 = bf16[512,896]{1,0:T(8,128)(2,1)S(1)} all-gather(bf16[128,896]{1,0:T(8,128)(2,1)S(1)} %get-tuple-element.29), channel_id=4, replica_groups=mesh['zh'=4,'x'=4,'zl'=2,'y'=8,'c'=2] {'x'}, dimensions={0}, use_global_device_ids=true | all-gather | bytes 1146880 | tf_op jit(solution)/shard_map/all_gather | solution.py:155
  87.1 4.4 %all-to-all-done.2 = bf16[128,16,128]{2,1,0:T(8,128)(2,1)S(1)} async-done(((bf16[128,16,128]{2,1,0:T(8,128)(2,1)}), bf16[128,16,128]{2,1,0:T(8,128)(2,1)S(1)}, u32[]{:S(2)}, u32[]{:S(2)}) %all-to-all-start.2) | async-done | bytes 524320 | tf_op jit(solution)/shard_map/all_to_all | solution.py:156
  91.6 2.4 %collective-permute-start = (bf16[18,4,16,128]{3,2,1,0:T(8,128)(2,1)S(1)}, bf16[18,4,16,128]{3,2,1,0:T(8,128)(2,1)S(1)}, u32[]{:S(2)}, u32[]{:S(2)}) collective-permute-start(bf16[18,4,16,128]{3,2,1,0:T(8,128)(2,1)S(1)} %get-tuple-element.32.refs_0_), channel_id=1, source_target_pairs={{0,32},{32,0},{64,96},{96,64},{1,33},{33,1},{65,97},{97,65},{2,34}... | collective-permute-start | bytes 884744 | tf_op jit(solution)/shard_map/ppermute | solution.py:163
  94.0 3.6 %collective-permute-start.3 = (bf16[18,4,16,128]{3,2,1,0:T(8,128)(2,1)S(1)}, bf16[18,4,16,128]{3,2,1,0:T(8,128)(2,1)S(1)}, u32[]{:S(2)}, u32[]{:S(2)}) collective-permute-start(bf16[18,4,16,128]{3,2,1,0:T(8,128)(2,1)S(1)} %get-tuple-element.33.refs_1_), channel_id=1, source_target_pairs={{0,96},{32,64},{64,32},{96,0},{1,97},{33,65},{65,33},{97,1},{2,98}... | collective-permute-start | bytes 884744 | tf_op jit(solution)/shard_map/ppermute | solution.py:164
  97.6 2.8 %collective-permute-start.1 = (bf16[18,4,16,128]{3,2,1,0:T(8,128)(2,1)S(1)}, bf16[18,4,16,128]{3,2,1,0:T(8,128)(2,1)S(1)}, u32[]{:S(2)}, u32[]{:S(2)}) collective-permute-start(bf16[18,4,16,128]{3,2,1,0:T(8,128)(2,1)S(1)} %get-tuple-element.33.refs_1_), channel_id=1, source_target_pairs={{0,32},{32,0},{64,96},{96,64},{1,33},{33,1},{65,97},{97,65},{2,34}... | collective-permute-start | bytes 884744 | tf_op jit(solution)/shard_map/ppermute | solution.py:165
  100.4 3.6 %collective-permute-start.5 = (bf16[18,4,16,128]{3,2,1,0:T(8,128)(2,1)S(1)}, bf16[18,4,16,128]{3,2,1,0:T(8,128)(2,1)S(1)}, u32[]{:S(2)}, u32[]{:S(2)}) collective-permute-start(bf16[18,4,16,128]{3,2,1,0:T(8,128)(2,1)S(1)} %get-tuple-element.32.refs_0_), channel_id=1, source_target_pairs={{0,96},{32,64},{64,32},{96,0},{1,97},{33,65},{65,33},{97,1},{2,98}... | collective-permute-start | bytes 884744 | tf_op jit(solution)/shard_map/ppermute | solution.py:166
  104.0 0.0 collective-permute-done.refs_2_
  104.0 3.5 %collective-permute-start.2 = (bf16[18,4,16,128]{3,2,1,0:T(8,128)(2,1)S(1)}, bf16[18,4,16,128]{3,2,1,0:T(8,128)(2,1)S(1)}, u32[]{:S(2)}, u32[]{:S(2)}) collective-permute-start(bf16[18,4,16,128]{3,2,1,0:T(8,128)(2,1)S(1)} %collective-permute-done.refs_2_), channel_id=1, source_target_pairs={{0,96},{32,64},{64,32},{96,0},{1,97},{33,65},{65,33},{97,1},{2,98}... | collective-permute-start | bytes 884744 | tf_op jit(solution)/shard_map/ppermute | solution.py:167
  107.5 0.0 collective-permute-done.3.refs_7_
  107.5 1.9 %collective-permute-start.4 = (bf16[18,4,16,128]{3,2,1,0:T(8,128)(2,1)S(1)}, bf16[18,4,16,128]{3,2,1,0:T(8,128)(2,1)S(1)}, u32[]{:S(2)}, u32[]{:S(2)}) collective-permute-start(bf16[18,4,16,128]{3,2,1,0:T(8,128)(2,1)S(1)} %collective-permute-done.3.refs_7_), channel_id=1, source_target_pairs={{0,32},{32,0},{64,96},{96,64},{1,33},{33,1},{65,97},{97,65},{2,34}... | collective-permute-start | bytes 884744 | tf_op jit(solution)/shard_map/ppermute | solution.py:168
  109.5 0.1 shard_map.88.refs_8_
  109.6 0.0 collective-permute-done.1.refs_3_
  109.6 3.9 %collective-permute-done.5.refs_6_ = bf16[18,4,16,128]{3,2,1,0:T(8,128)(2,1)S(1)} collective-permute-done((bf16[18,4,16,128]{3,2,1,0:T(8,128)(2,1)S(1)}, bf16[18,4,16,128]{3,2,1,0:T(8,128)(2,1)S(1)}, u32[]{:S(2)}, u32[]{:S(2)}) %collective-permute-start.5) | collective-permute-done | bytes 294944 | tf_op jit(solution)/shard_map/ppermute | solution.py:166
  113.5 6.1 %collective-permute-done.2.refs_4_ = bf16[18,4,16,128]{3,2,1,0:T(8,128)(2,1)S(1)} collective-permute-done((bf16[18,4,16,128]{3,2,1,0:T(8,128)(2,1)S(1)}, bf16[18,4,16,128]{3,2,1,0:T(8,128)(2,1)S(1)}, u32[]{:S(2)}, u32[]{:S(2)}) %collective-permute-start.2) | collective-permute-done | bytes 294944 | tf_op jit(solution)/shard_map/ppermute | solution.py:167
  119.6 0.0 collective-permute-done.4.refs_5_
  119.6 0.0 copy-done
  119.6 0.0 copy-done.1
  119.6 0.0 copy-done.2
  119.6 2.6 %shard_map.89 = (f32[64,1024]{1,0:T(8,128)}, f32[64,1024]{1,0:T(8,128)}, bf16[64,1024]{1,0:T(8,128)(2,1)}) custom-call(bf16[18,4,16,128]{3,2,1,0:T(8,128)(2,1)S(1)} %get-tuple-element.32.refs_0_, bf16[18,4,16,128]{3,2,1,0:T(8,128)(2,1)S(1)} %get-tuple-element.33.refs_1_, bf16[18,4,16,128]{3,2,1,0:T(8,128)(2,1)S(1)} %collective-permute-done.refs_2_, ...), custom_call_target="tpu_custom_call" | custom-call | tf_op jit(solution)/shard_map/pallas_call | solution.py:171
  (6 shorter events, 0.1 us)
Async XLA Ops:
  0.6 4.4 %copy-start.4 = (bf16[1,64,1024]{2,1,0:T(8,128)(2,1)S(1)}, bf16[1,64,1024]{2,1,0:T(8,128)(2,1)}, u32[]{:S(2)}) copy-start(bf16[1,64,1024]{2,1,0:T(8,128)(2,1)} %param.11) | copy-start | bytes 393220
  0.6 30.8 %all-to-all-start = ((bf16[4,16,16384]{2,1,0:T(8,128)(2,1)}), bf16[4,16,16384]{2,1,0:T(8,128)(2,1)S(1)}, u32[]{:S(2)}, u32[]{:S(2)}) async-start(bf16[4,16,16384]{2,1,0:T(8,128)(2,1)} %bitcast.20), calls=%async_computation | async-start | bytes 4194304 | tf_op jit(solution)/shard_map/all_to_all | solution.py:135
  31.5 25.7 %copy-start.3 = (s32[32]{0:T(128)S(1)}, s32[32]{0:T(128)}, u32[]{:S(2)}) copy-start(s32[32]{0:T(128)} %owner_ref.1) | copy-start | bytes 388
  32.5 24.6 %all-to-all-start.1 = ((bf16[8,16,16,128]{3,2,1,0:T(8,128)(2,1)}), bf16[8,16,16,128]{3,2,1,0:T(8,128)(2,1)S(1)}, u32[]{:S(2)}, u32[]{:S(2)}) async-start(bf16[8,16,16,128]{3,2,1,0:T(8,128)(2,1)} %shard_map.85), calls=%async_computation.1 | async-start | bytes 1048576 | tf_op jit(solution)/shard_map/all_to_all | solution.py:149
  58.6 32.9 %all-to-all-start.2 = ((bf16[128,16,128]{2,1,0:T(8,128)(2,1)}), bf16[128,16,128]{2,1,0:T(8,128)(2,1)S(1)}, u32[]{:S(2)}, u32[]{:S(2)}) async-start(bf16[128,16,128]{2,1,0:T(8,128)(2,1)} %bitcast.3), calls=%async_computation.2 | async-start | bytes 1048576 | tf_op jit(solution)/shard_map/all_to_all | solution.py:156
  91.5 28.1 %copy-start = (f32[1,64,1024]{2,1,0:T(8,128)S(1)}, f32[1,64,1024]{2,1,0:T(8,128)}, u32[]{:S(2)}) copy-start(f32[1,64,1024]{2,1,0:T(8,128)} %param.8) | copy-start | bytes 786436
  91.5 28.1 %copy-start.1 = (f32[1,64,1024]{2,1,0:T(8,128)S(1)}, f32[1,64,1024]{2,1,0:T(8,128)}, u32[]{:S(2)}) copy-start(f32[1,64,1024]{2,1,0:T(8,128)} %param.9) | copy-start | bytes 786436
  91.5 28.1 %copy-start.2 = (bf16[1,64,1024]{2,1,0:T(8,128)(2,1)S(1)}, bf16[1,64,1024]{2,1,0:T(8,128)(2,1)}, u32[]{:S(2)}) copy-start(bf16[1,64,1024]{2,1,0:T(8,128)(2,1)} %param.10) | copy-start | bytes 393220
  91.6 12.5 %collective-permute-start = (bf16[18,4,16,128]{3,2,1,0:T(8,128)(2,1)S(1)}, bf16[18,4,16,128]{3,2,1,0:T(8,128)(2,1)S(1)}, u32[]{:S(2)}, u32[]{:S(2)}) collective-permute-start(bf16[18,4,16,128]{3,2,1,0:T(8,128)(2,1)S(1)} %get-tuple-element.32.refs_0_), channel_id=1, source_target_pairs={{0,32},{32,0},{64,96},{96,64},{1,33},{33,1},{65,97},{97,65},{2,34}... | collective-permute-start | bytes 884744 | tf_op jit(solution)/shard_map/ppermute | solution.py:163
  94.0 13.6 %collective-permute-start.3 = (bf16[18,4,16,128]{3,2,1,0:T(8,128)(2,1)S(1)}, bf16[18,4,16,128]{3,2,1,0:T(8,128)(2,1)S(1)}, u32[]{:S(2)}, u32[]{:S(2)}) collective-permute-start(bf16[18,4,16,128]{3,2,1,0:T(8,128)(2,1)S(1)} %get-tuple-element.33.refs_1_), channel_id=1, source_target_pairs={{0,96},{32,64},{64,32},{96,0},{1,97},{33,65},{65,33},{97,1},{2,98}... | collective-permute-start | bytes 884744 | tf_op jit(solution)/shard_map/ppermute | solution.py:164
  97.6 12.0 %collective-permute-start.1 = (bf16[18,4,16,128]{3,2,1,0:T(8,128)(2,1)S(1)}, bf16[18,4,16,128]{3,2,1,0:T(8,128)(2,1)S(1)}, u32[]{:S(2)}, u32[]{:S(2)}) collective-permute-start(bf16[18,4,16,128]{3,2,1,0:T(8,128)(2,1)S(1)} %get-tuple-element.33.refs_1_), channel_id=1, source_target_pairs={{0,32},{32,0},{64,96},{96,64},{1,33},{33,1},{65,97},{97,65},{2,34}... | collective-permute-start | bytes 884744 | tf_op jit(solution)/shard_map/ppermute | solution.py:165
  100.4 13.1 %collective-permute-start.5 = (bf16[18,4,16,128]{3,2,1,0:T(8,128)(2,1)S(1)}, bf16[18,4,16,128]{3,2,1,0:T(8,128)(2,1)S(1)}, u32[]{:S(2)}, u32[]{:S(2)}) collective-permute-start(bf16[18,4,16,128]{3,2,1,0:T(8,128)(2,1)S(1)} %get-tuple-element.32.refs_0_), channel_id=1, source_target_pairs={{0,96},{32,64},{64,32},{96,0},{1,97},{33,65},{65,33},{97,1},{2,98}... | collective-permute-start | bytes 884744 | tf_op jit(solution)/shard_map/ppermute | solution.py:166
  104.0 15.5 %collective-permute-start.2 = (bf16[18,4,16,128]{3,2,1,0:T(8,128)(2,1)S(1)}, bf16[18,4,16,128]{3,2,1,0:T(8,128)(2,1)S(1)}, u32[]{:S(2)}, u32[]{:S(2)}) collective-permute-start(bf16[18,4,16,128]{3,2,1,0:T(8,128)(2,1)S(1)} %collective-permute-done.refs_2_), channel_id=1, source_target_pairs={{0,96},{32,64},{64,32},{96,0},{1,97},{33,65},{65,33},{97,1},{2,98}... | collective-permute-start | bytes 884744 | tf_op jit(solution)/shard_map/ppermute | solution.py:167
  107.5 12.1 %collective-permute-start.4 = (bf16[18,4,16,128]{3,2,1,0:T(8,128)(2,1)S(1)}, bf16[18,4,16,128]{3,2,1,0:T(8,128)(2,1)S(1)}, u32[]{:S(2)}, u32[]{:S(2)}) collective-permute-start(bf16[18,4,16,128]{3,2,1,0:T(8,128)(2,1)S(1)} %collective-permute-done.3.refs_7_), channel_id=1, source_target_pairs={{0,32},{32,0},{64,96},{96,64},{1,33},{33,1},{65,97},{97,65},{2,34}... | collective-permute-start | bytes 884744 | tf_op jit(solution)/shard_map/ppermute | solution.py:168
